TPU v7x, 32 devices: a whole 2x2x4 slice. The times are simulated.
32 devices in a mesh: wide: 8 (over y, x, core), narrow: 4 (over z).
Axes of the slice: x: 2, y: 2, z: 4, core: 2. Of those that a mesh axis runs over, the one named last changes fastest.
Arguments:
- inputs: bfloat16 [32768, 2048], P('wide', 'narrow'), may hold values from -6 to 6
- flags: int32 [32768], replicated, may hold values from 0 to 1, as said below
- w_one: bfloat16 [2048, 2048], P(None, 'narrow'), may hold values from -0.125 to 0.125
- gamma_one: float32 [2048], P(('narrow', 'wide')), may hold values from 0.1 to 0.4
- beta_one: float32 [2048], P(('narrow', 'wide')), may hold values from -0.2 to 0.2
- decay_one: float32 [2048], P(('narrow', 'wide')), may hold values from 0.9 to 1
- w_two: bfloat16 [2048, 2048], P(None, 'narrow'), may hold values from -0.125 to 0.125
- gamma_two: float32 [2048], P(('narrow', 'wide')), may hold values from 0.1 to 0.4
- beta_two: float32 [2048], P(('narrow', 'wide')), may hold values from -0.2 to 0.2
- decay_two: float32 [2048], P(('narrow', 'wide')), may hold values from 0.9 to 1
- cotangent: bfloat16 [32768, 2048], P('wide', 'narrow'), may hold values from -6 to 6
Outputs:
- output: bfloat16 [32768, 2048], P('wide', 'narrow')
- grad_inputs: float32 [32768, 2048], P('wide', 'narrow')
- grad_w_one: float32 [2048, 2048], P('wide', 'narrow')
- grad_gamma_one: float32 [2048], P(('narrow', 'wide'))
- grad_beta_one: float32 [2048], P(('narrow', 'wide'))
- grad_decay_one: float32 [2048], P(('narrow', 'wide'))
- grad_w_two: float32 [2048, 2048], P('wide', 'narrow')
- grad_gamma_two: float32 [2048], P(('narrow', 'wide'))
- grad_beta_two: float32 [2048], P(('narrow', 'wide'))
- grad_decay_two: float32 [2048], P(('narrow', 'wide'))
Inputs may be any that keep to these rules, and one draw needn't show every extreme that they name: flags is 1 at the first frame of each clip and 0 elsewhere; each row of 512 frames begins a clip, and no clip crosses a row's end; every clip holds 64 to 512 frames, except a row's last, which may be shorter.
All inputs are finite; a program needn't handle non-finite values.
Results may differ from a plain program's by a relative error of at most 0.0068.
Values may be sent and summed in bfloat16 or wider, within the bound.
No kernel may reach another device: no remote copies, remote signals or barrier semaphores. Data moves between devices by JAX's collectives and lax.ppermute only.
A program may use at most 448 MiB of HBM per device.

v0:
```python
import functools

import jax
import jax.numpy as jnp
from jax import lax
from jax.experimental import pallas as pl
from jax.experimental.pallas import tpu as pltpu
from jax.sharding import PartitionSpec as P

ROW_LEN = 512
EPSILON = 1e-05
LOG2E = 1.4426950408889634
LN2 = 0.6931471805599453
LANES = 128
SUB = 16
CHUNK = 64
VMEM_LIMIT = 56 * 2**20
BOTH = ("narrow", "wide")

params_of = functools.partial(pltpu.CompilerParams, vmem_limit_bytes=VMEM_LIMIT)
SMEM = pl.BlockSpec(memory_space=pltpu.SMEM)
BRIEF = pl.CostEstimate(flops=1, bytes_accessed=1, transcendentals=0)


def whole(shape):
    return pl.BlockSpec(shape, lambda *_: (0,) * len(shape))


def swap(blocks):
    return lax.all_to_all(blocks, "narrow", split_axis=0, concat_axis=0)


def merge_all(value, merge, axis, size):
    k = 1
    while k < size:
        other = lax.ppermute(value, axis, [(i, i ^ k) for i in range(size)])
        value = merge(value, other)
        k *= 2
    return value


def add(a, b):
    return a + b


def merge_moments(frames):
    count = [frames]

    def merge(a, b):
        gap = a[0:1] - b[0:1]
        squares = a[1:2] + b[1:2] + gap * gap * (count[0] / 2)
        count[0] *= 2
        means = (a + b) * 0.5
        return jnp.concatenate([means[0:1], squares, means[2:3], a[3:] + b[3:]])

    return merge


def gather_rows(weights, wide):
    rows = weights[0].shape[0] // wide
    first = lax.axis_index("wide") * rows
    shares = [lax.dynamic_slice_in_dim(weight, first, rows, 0) for weight in weights]
    both = lax.all_gather(jnp.concatenate(shares, 0), "narrow", axis=1, tiled=True)
    return [both[i * rows : (i + 1) * rows] for i in range(len(weights))]


def project_kernel(groups, x_refs, w_ref, z_ref, moments_ref, joined_ref=None):
    frames, cols = z_ref.shape
    here = pl.program_id(0)
    step = min(256, frames)
    sums = jnp.zeros((1, cols), jnp.float32)
    for m in range(0, frames, step):
        acc = None
        for ref, lo, count, feature in groups:
            if not lo <= m < lo + count:
                continue
            x_ref = x_refs[ref]
            block, first, depth = feature
            x = x_ref[block, m - lo : m - lo + step, :]
            term = jnp.dot(x, w_ref[first : first + depth, :], preferred_element_type=jnp.float32)
            acc = term if acc is None else acc + term
        rounded = acc.astype(jnp.bfloat16)
        z_ref[m : m + step, :] = rounded
        sums += jnp.sum(rounded.astype(jnp.float32), 0, keepdims=True)
    mean = sums / frames
    squares = jnp.zeros((1, cols), jnp.float32)
    for m in range(0, frames, step):
        gap = z_ref[m : m + step, :].astype(jnp.float32) - mean
        squares += jnp.sum(gap * gap, 0, keepdims=True)
    at = pl.ds(pl.multiple_of(here * cols, cols), cols)
    moments_ref[0:1, at] = mean
    moments_ref[1:2, at] = squares
    if joined_ref is None:
        own = x_refs[0][0, :, at].astype(jnp.float32)
        moments_ref[2:3, at] = jnp.sum(own, 0, keepdims=True) / frames
        return
    total = jnp.zeros((1, joined_ref.shape[1]), jnp.float32)
    lo = 0
    for x_ref in x_refs:
        count = x_ref.shape[1]
        own = x_ref[here]
        joined_ref[lo : lo + count, :] = own
        total += jnp.sum(own.astype(jnp.float32), 0, keepdims=True)
        lo += count
    place = pl.ds(pl.multiple_of(here * joined_ref.shape[1], joined_ref.shape[1]), joined_ref.shape[1])
    moments_ref[2:3, place] = total / frames


def project(pieces, weight):
    blocks, _, depth = pieces[0].shape
    frames = sum(p.shape[1] for p in pieces)
    rows, cols = weight.shape
    joined = blocks > 1
    steps = blocks if joined else 4
    width = cols // steps
    groups = []
    lo = 0
    for i, p in enumerate(pieces):
        groups += [(i, lo, p.shape[1], (k, k * depth, depth)) for k in range(blocks)]
        lo += p.shape[1]
    out_shape = [
        jax.ShapeDtypeStruct((frames, cols), jnp.bfloat16),
        jax.ShapeDtypeStruct((3, cols), jnp.float32),
    ]
    out_specs = [pl.BlockSpec((frames, width), lambda i: (0, i)), whole((3, cols))]
    if joined:
        out_shape.append(jax.ShapeDtypeStruct((frames, rows), jnp.bfloat16))
        out_specs.append(pl.BlockSpec((frames, depth), lambda i: (0, i)))

    def kernel(*refs):
        project_kernel(groups, refs[: len(pieces)], *refs[len(pieces) :])

    return pl.pallas_call(
        kernel,
        grid=(steps,),
        in_specs=[whole(p.shape) for p in pieces]
        + [pl.BlockSpec((rows, width), lambda i: (0, i))],
        out_specs=out_specs,
        out_shape=out_shape,
        compiler_params=params_of(),
        cost_estimate=BRIEF,
        name="project",
    )(*pieces, weight)


def to_steps(row_ref, lanes_ref, tiles):
    for j in range(tiles):
        lanes_ref[j : j + 1, :] = row_ref[:, j * LANES : (j + 1) * LANES]


def forward_kernel(total_frames, ranges, keep, moments, gains, z_ref, s_ref, *refs):
    parts = len(ranges)
    h_refs, (vec, state, seq) = refs[:parts], refs[parts:]
    rows, chunk, width = z_ref.shape
    tiles = width // LANES

    @pl.when(pl.program_id(0) == 0)
    def _():
        scale = gains[0:1, :] * lax.rsqrt(moments[1:2, :] / total_frames + EPSILON)
        lanes = [moments[0:1, :], scale * LOG2E, gains[1:2, :] * LOG2E, gains[2:3, :] * LOG2E]
        for i, row in enumerate(lanes):
            for j in range(tiles):
                vec[i, j : j + 1, :] = row[:, j * LANES : (j + 1) * LANES]
        state[...] = jnp.zeros_like(state)

    mean, scale, shift, decay = (vec[i] for i in range(4))
    first = pl.program_id(0) * chunk

    def block(c, running):
        running = list(running)
        for r in range(rows):
            values = z_ref[r, pl.ds(pl.multiple_of(c * SUB, SUB), SUB), :].astype(jnp.float32)
            for j in range(tiles):
                for half in range(SUB // 8):
                    seq[r, pl.ds(half * 8 * tiles + j, 8, stride=tiles), :] = values[
                        half * 8 : half * 8 + 8, j * LANES : (j + 1) * LANES
                    ]
        for k in range(SUB):
            for r in range(rows):
                value = (seq[r, k * tiles : (k + 1) * tiles, :] - mean) * scale + shift
                before = value + (decay * keep[r, first + c * SUB + k]) * running[r]
                fresh = jnp.where(
                    before > 30.0, before * LN2, jnp.log(1.0 + jnp.exp2(before))
                )
                running[r] = fresh
                s_ref[r, pl.ds(pl.multiple_of((c * SUB + k) * tiles, tiles), tiles), :] = fresh
        for r in range(rows):
            for (lo, hi), h_ref in zip(ranges, h_refs, strict=True):
                per_block = tiles // h_ref.shape[0]
                for q in range(h_ref.shape[0]):
                    for j in range(lo, hi):
                        tile = q * per_block + j
                        halves = [
                            s_ref[
                                r,
                                pl.ds((c * SUB + half * 8) * tiles + tile, 8, stride=tiles),
                                :,
                            ]
                            for half in range(SUB // 8)
                        ]
                        h_ref[
                            q,
                            r,
                            pl.ds(pl.multiple_of(c * SUB, SUB), SUB),
                            (j - lo) * LANES : (j - lo + 1) * LANES,
                        ] = jnp.concatenate(halves, 0).astype(jnp.bfloat16)
        return tuple(running)

    running = lax.fori_loop(0, chunk // SUB, block, tuple(state[r] for r in range(rows)))
    for r in range(rows):
        state[r] = running[r]


def forward(z, moments, gains, keep, blocks, ranges, total_frames):
    rows, length = keep.shape
    width = z.shape[1]
    tiles = width // LANES
    results = pl.pallas_call(
        functools.partial(forward_kernel, total_frames, ranges),
        grid=(length // CHUNK,),
        in_specs=[
            SMEM,
            whole((3, width)),
            whole((3, width)),
            pl.BlockSpec((rows, CHUNK, width), lambda i: (0, i, 0)),
        ],
        out_specs=[pl.BlockSpec((rows, CHUNK * tiles, LANES), lambda i: (0, i, 0))]
        + [
            pl.BlockSpec((blocks, rows, CHUNK, (hi - lo) * LANES), lambda i: (0, 0, i, 0))
            for lo, hi in ranges
        ],
        out_shape=[jax.ShapeDtypeStruct((rows, length * tiles, LANES), jnp.float32)]
        + [
            jax.ShapeDtypeStruct((blocks, rows, length, (hi - lo) * LANES), jnp.bfloat16)
            for lo, hi in ranges
        ],
        scratch_shapes=[
            pltpu.VMEM((4, tiles, LANES), jnp.float32),
            pltpu.VMEM((rows, tiles, LANES), jnp.float32),
            pltpu.VMEM((rows, SUB * tiles, LANES), jnp.float32),
        ],
        compiler_params=params_of(),
        cost_estimate=BRIEF,
        name="forward",
    )(keep, moments, gains, z.reshape(rows, length, width))
    return results[0], [h.reshape(blocks, rows * length, -1) for h in results[1:]]


def backward_kernel(ranges, keep, moments, gains, s_ref, before_ref, z_ref, *refs):
    parts = len(ranges)
    g_refs, (dpre_ref, sums_ref, vec, state, seq, grads) = refs[:parts], refs[parts:]
    rows, chunk, width = z_ref.shape
    tiles = width // LANES
    step = pl.program_id(0)
    first = (pl.num_programs(0) - 1 - step) * chunk

    @pl.when(step == 0)
    def _():
        for j in range(tiles):
            vec[j : j + 1, :] = gains[2:3, j * LANES : (j + 1) * LANES]
        state[...] = jnp.zeros_like(state)
        sums_ref[...] = jnp.zeros_like(sums_ref)

    decay = vec[...]
    mean = moments[0:1, :]
    blocks = chunk // SUB

    def block(i, running):
        *running, dsum = running
        c = blocks - 1 - i
        base = pl.multiple_of(c * SUB, SUB)
        for r in range(rows):
            for (lo, hi), g_ref in zip(ranges, g_refs, strict=True):
                per_block = tiles // g_ref.shape[0]
                for q in range(g_ref.shape[0]):
                    values = g_ref[q, r, pl.ds(base, SUB), :].astype(jnp.float32)
                    for j in range(lo, hi):
                        tile = q * per_block + j
                        for half in range(SUB // 8):
                            seq[r, pl.ds(half * 8 * tiles + tile, 8, stride=tiles), :] = values[
                                half * 8 : half * 8 + 8, (j - lo) * LANES : (j - lo + 1) * LANES
                            ]
        for k in range(SUB - 1, -1, -1):
            for r in range(rows):
                at = c * SUB + k
                s = s_ref[r, pl.ds(pl.multiple_of(at * tiles, tiles), tiles), :]
                if k > 0:
                    prior = s_ref[r, pl.ds(pl.multiple_of((at - 1) * tiles, tiles), tiles), :]
                else:
                    inner = s_ref[
                        r, pl.ds(pl.multiple_of(jnp.maximum(at - 1, 0) * tiles, tiles), tiles), :
                    ]
                    prior = jnp.where(c > 0, inner, before_ref[r])
                mark = keep[r, first + at]
                slope = 1.0 - jnp.exp2(s * -LOG2E)
                dpre = (seq[r, k * tiles : (k + 1) * tiles, :] + running[r]) * slope
                held = dpre * mark
                running[r] = held * decay
                dsum = dsum + held * prior
                grads[r, k * tiles : (k + 1) * tiles, :] = dpre
        gb = jnp.zeros((8, width), jnp.float32)
        gg = jnp.zeros((8, width), jnp.float32)
        for r in range(rows):
            gaps = z_ref[r, pl.ds(base, SUB), :].astype(jnp.float32) - mean
            for half in range(SUB // 8):
                dpre = jnp.concatenate(
                    [
                        grads[r, pl.ds(half * 8 * tiles + j, 8, stride=tiles), :]
                        for j in range(tiles)
                    ],
                    1,
                )
                dpre_ref[r, pl.ds(pl.multiple_of(base + half * 8, 8), 8), :] = dpre
                gb += dpre
                gg += dpre * gaps[half * 8 : half * 8 + 8, :]
        sums_ref[0:8, :] += gb
        sums_ref[8:16, :] += gg
        return (*running, dsum)

    start = tuple(state[r] for r in range(rows)) + (state[rows],)
    *running, dsum = lax.fori_loop(0, blocks, block, start)
    for r in range(rows):
        state[r] = running[r]
    state[rows] = dsum

    @pl.when(step == pl.num_programs(0) - 1)
    def _():
        gb = jnp.sum(sums_ref[0:8, :], 0, keepdims=True)
        gg = jnp.sum(sums_ref[8:16, :], 0, keepdims=True)
        sums_ref[0:1, :] = gb
        sums_ref[1:2, :] = gg
        for j in range(tiles):
            sums_ref[2:3, j * LANES : (j + 1) * LANES] = state[rows, j : j + 1, :]


def backward(grads, ranges, states, z, moments, gains, keep):
    rows, length = keep.shape
    width = z.shape[1]
    tiles = width // LANES
    blocks = grads[0].shape[0]
    last = length // CHUNK - 1
    dpre, sums = pl.pallas_call(
        functools.partial(backward_kernel, ranges),
        grid=(length // CHUNK,),
        in_specs=[
            SMEM,
            whole((3, width)),
            whole((3, width)),
            pl.BlockSpec((rows, CHUNK * tiles, LANES), lambda i: (0, last - i, 0)),
            pl.BlockSpec(
                (rows, tiles, LANES), lambda i: (0, jnp.maximum((last - i) * CHUNK - 1, 0), 0)
            ),
            pl.BlockSpec((rows, CHUNK, width), lambda i: (0, last - i, 0)),
        ]
        + [
            pl.BlockSpec((blocks, rows, CHUNK, (hi - lo) * LANES), lambda i: (0, 0, last - i, 0))
            for lo, hi in ranges
        ],
        out_specs=[
            pl.BlockSpec((rows, CHUNK, width), lambda i: (0, last - i, 0)),
            whole((16, width)),
        ],
        out_shape=[
            jax.ShapeDtypeStruct((rows, length, width), jnp.float32),
            jax.ShapeDtypeStruct((16, width), jnp.float32),
        ],
        scratch_shapes=[
            pltpu.VMEM((tiles, LANES), jnp.float32),
            pltpu.VMEM((rows + 1, tiles, LANES), jnp.float32),
            pltpu.VMEM((rows, SUB * tiles, LANES), jnp.float32),
            pltpu.VMEM((rows, SUB * tiles, LANES), jnp.float32),
        ],
        compiler_params=params_of(),
        cost_estimate=BRIEF,
        name="backward",
    )(
        keep,
        moments,
        gains,
        states,
        states,
        z.reshape(rows, length, width),
        *[g.reshape(blocks, rows, length, -1) for g in grads],
    )
    return dpre.reshape(rows * length, width), sums[0:3]


def dproject_kernel(total_frames, moments, gains, sums, dpre_ref, z_ref, w_ref, dz_ref, level_ref, da_ref):
    rstd = lax.rsqrt(moments[1:2, :] / total_frames + EPSILON)
    scale = gains[0:1, :] * rstd
    level = sums[0:1, :] / total_frames
    slope = sums[1:2, :] * (rstd * rstd) / total_frames
    gap = z_ref[...].astype(jnp.float32) - moments[0:1, :]
    dz = (scale * (dpre_ref[...] - level - gap * slope)).astype(jnp.bfloat16)
    dz_ref[...] = dz
    here = jnp.sum(dz.astype(jnp.float32), 0, keepdims=True)

    @pl.when(pl.program_id(0) == 0)
    def _():
        level_ref[...] = here

    @pl.when(pl.program_id(0) > 0)
    def _():
        level_ref[...] += here

    parts = da_ref.shape[0]
    depth = w_ref.shape[0] // parts
    for p in range(parts):
        da_ref[p] = lax.dot_general(
            dz_ref[...],
            w_ref[p * depth : (p + 1) * depth, :],
            (((1,), (1,)), ((), ())),
            preferred_element_type=jnp.float32,
        ).astype(jnp.bfloat16)


def dproject(dpre, z, moments, gains, sums, weight, parts, total_frames):
    frames, width = z.shape
    rows = weight.shape[0]
    step = min(256, frames)
    return pl.pallas_call(
        functools.partial(dproject_kernel, total_frames),
        grid=(frames // step,),
        in_specs=[
            whole((3, width)),
            whole((3, width)),
            whole((3, width)),
            pl.BlockSpec((step, width), lambda i: (i, 0)),
            pl.BlockSpec((step, width), lambda i: (i, 0)),
            whole((rows, width)),
        ],
        out_specs=[
            pl.BlockSpec((step, width), lambda i: (i, 0)),
            whole((1, width)),
            pl.BlockSpec((parts, step, rows // parts), lambda i: (0, i, 0)),
        ],
        out_shape=[
            jax.ShapeDtypeStruct((frames, width), jnp.bfloat16),
            jax.ShapeDtypeStruct((1, width), jnp.float32),
            jax.ShapeDtypeStruct((parts, frames, rows // parts), jnp.bfloat16),
        ],
        compiler_params=params_of(),
        cost_estimate=BRIEF,
        name="dproject",
    )(moments, gains, sums, dpre, z, weight)


def weight_kernel(level, source_ref, dz_ref, center_ref, out_ref):
    terms = lax.dot_general(
        source_ref[...], dz_ref[...], (((0,), (0,)), ((), ())), preferred_element_type=jnp.float32
    )
    out_ref[...] = (terms - center_ref[...] * level[...]).astype(jnp.bfloat16)


def weight_terms(source, center, dz, level):
    frames, rows = source.shape
    cols = dz.shape[1]
    tile = 256
    return pl.pallas_call(
        weight_kernel,
        grid=(rows // tile,),
        in_specs=[
            whole((1, cols)),
            pl.BlockSpec((frames, tile), lambda i: (0, i)),
            whole((frames, cols)),
            pl.BlockSpec((tile, 1), lambda i: (i, 0)),
        ],
        out_specs=pl.BlockSpec((tile, cols), lambda i: (i, 0)),
        out_shape=jax.ShapeDtypeStruct((rows, cols), jnp.bfloat16),
        compiler_params=params_of(),
        cost_estimate=BRIEF,
        name="weight",
    )(level, source, dz, center.reshape(rows, 1))


def per_device(sizes, inputs, flags, w_one, *rest):
    gamma_one, beta_one, decay_one, w_two, gamma_two, beta_two, decay_two, cotangent = rest
    wide, narrow = sizes["wide"], sizes["narrow"]
    n = lax.axis_index("narrow")
    w = lax.axis_index("wide")
    frames = inputs.shape[0] // narrow
    part = inputs.shape[1]
    tiles = part // LANES
    total_frames = inputs.shape[0] * wide
    rows = frames // ROW_LEN
    first = w * inputs.shape[0] + n * frames
    keep = lax.dynamic_slice_in_dim(flags, first, frames, 0).reshape(rows, ROW_LEN)
    keep = (1 - keep).astype(jnp.float32)
    tie = lax.optimization_barrier

    def along(value, merge):
        return merge_all(value, merge, "narrow", narrow)

    def across(value, merge):
        return merge_all(value, merge, "wide", wide)

    own = jnp.stack([gamma_one, beta_one, decay_one, gamma_two, beta_two, decay_two])
    each = own.shape[1]
    spread = jnp.zeros((6, each * wide * narrow), jnp.float32)
    spread = lax.dynamic_update_slice_in_dim(spread, own, (n * wide + w) * each, 1)

    groups = [(0, tiles // 4), (tiles // 4, 3 * tiles // 4), (3 * tiles // 4, tiles)]

    def columns(held, g):
        lo, hi = groups[g]
        return swap(held[:, lo * LANES : hi * LANES].reshape(narrow, frames, -1))

    split = frames // 4
    held = inputs.reshape(narrow, frames, part)
    piece = swap(held[:, :split])
    share_one, share_two = gather_rows([w_one, w_two], wide)
    share_one, share_two, held = tie((share_one, share_two, held))
    pieces = [piece, swap(held[:, split:])]
    full_one = lax.all_gather(share_one, "wide", axis=0, tiled=True)
    full_one, share_two = tie((full_one, share_two))
    full_two = lax.all_gather(share_two, "wide", axis=0, tiled=True)

    pieces, held = tie((pieces, cotangent))
    group = columns(held, 0)
    z_one, moments, source = project(pieces, full_one)
    moments, group = tie((moments, group))
    grads = [group]
    moments = jnp.concatenate([moments, spread])
    merge = merge_moments(frames)
    moments = along(moments, merge)
    moments, held = tie((moments, cotangent))
    group = columns(held, 1)
    moments_one = across(moments, merge)
    gains_one, gains_two = moments_one[3:6], moments_one[6:9]
    moments_one = moments_one[:3]
    every = [(0, z_one.shape[1] // LANES)]
    states_one, (h_one,) = forward(
        z_one, moments_one, gains_one, keep, 1, every, total_frames
    )
    z_two, moments = project([h_one], full_two)
    moments, group = tie((moments, group))
    grads.append(group)
    merge = merge_moments(frames)
    moments = along(moments, merge)
    moments, held = tie((moments, cotangent))
    group = columns(held, 2)
    moments_two = across(moments, merge)
    states_two, h_two = forward(
        z_two, moments_two, gains_two, keep, narrow, groups, total_frames
    )
    h_two, group = tie((h_two, group))
    grads.append(group)

    second = [swap(h_two[0])]
    dpre, sums = backward(grads, groups, states_two, z_two, moments_two, gains_two, keep)
    sums, second[0] = tie((sums, second[0]))
    sums = along(sums, add)
    sums, h_two = tie((sums, h_two))
    group = swap(h_two[1])
    sums_two = across(sums, add)
    dz_two, level_two, dh_one = dproject(
        dpre, z_two, moments_two, gains_two, sums_two, full_two, 1, total_frames
    )
    dpre, sums = backward([dh_one], every, states_one, z_one, moments_one, gains_one, keep)
    own_level_two = level_two
    sums = jnp.concatenate([sums, level_two], 0)
    sums, group = tie((sums, group))
    second.append(group)
    sums = along(sums, add)
    sums, h_two = tie((sums, h_two))
    group = swap(h_two[2])
    sums_one = across(sums, add)
    level_two = sums_one[3:]
    sums_one = sums_one[:3]
    dz_one, level_one, dsource = dproject(
        dpre, z_one, moments_one, gains_one, sums_one, full_one, narrow, total_frames
    )
    dsource, group, dz_one, dz_two = tie((dsource, group, dz_one, dz_two))
    second.append(group)
    arrived = swap(dsource).reshape(inputs.shape)

    whole_two = jnp.concatenate(second, axis=2).reshape(inputs.shape).astype(jnp.float32)
    output = (inputs.astype(jnp.float32) + whole_two).astype(jnp.bfloat16)

    center_one, center_two = moments_one[2], moments_two[2]
    terms_two = weight_terms(h_one[0], center_two, dz_two, own_level_two)
    terms_one = weight_terms(source, center_one, dz_one, level_one)
    level_one = along(across(level_one, add), add)
    grad_inputs = cotangent.astype(jnp.float32) + arrived.astype(jnp.float32)

    def summed(terms, center, level):
        plane = lax.psum_scatter(terms, "wide", scatter_dimension=0, tiled=True)
        span = plane.shape[0]
        blocks = plane.reshape(span, narrow, part).transpose(1, 0, 2)
        weight = jnp.sum(swap(blocks).astype(jnp.float32), 0)
        rows_of = lax.dynamic_slice_in_dim(center, w * span, span, 0)
        cols_of = lax.dynamic_slice_in_dim(level[0], n * part, part, 0)
        return weight + rows_of[:, None] * cols_of[None, :]

    dw_two = summed(terms_two, center_two, level_two)
    dw_one = summed(terms_one, center_one, level_one)

    def small(sums, moments):
        rstd = lax.rsqrt(moments[1] / total_frames + EPSILON)
        whole_ones = (sums[1] * rstd, sums[0], sums[2])
        return [lax.dynamic_slice_in_dim(v, (n * wide + w) * each, each, 0) for v in whole_ones]

    return (
        output,
        grad_inputs,
        dw_one,
        *small(sums_one, moments_one),
        dw_two,
        *small(sums_two, moments_two),
    )


def solution(mesh):
    neurons = P(("narrow", "wide"))
    frames = P("wide", "narrow")
    weight = P(None, "narrow")
    small = (neurons, neurons, neurons)
    return jax.shard_map(
        functools.partial(per_device, dict(mesh.shape)),
        mesh=mesh,
        in_specs=(frames, P(), weight, *small, weight, *small, frames),
        out_specs=(frames, frames, frames, *small, frames, *small),
        check_vma=False,
    )
```

profile of v0, /device:TPU:0, one launch (start us, length us, event | category | flops | bytes accessed | tf_op | source)
XLA Modules:
  0.0 651.8 jit_solution(14448760703719064075)
XLA Ops:
  10.7 48.7 %all-gather.4.cloned.1.call-done = bf16[512,2048]{1,0:T(8,128)(2,1)} async-done(((bf16[512,512]{1,0:T(8,128)(2,1)}), bf16[512,2048]{1,0:T(8,128)(2,1)}) %all-gather.4.cloned.1.call-update) | async-done | bytes 2097168 | tf_op jit(solution)/shard_map/all_gather | solution.py:63
  72.5 21.8 %all-to-all-done.refs_0_ = bf16[4,256,512]{2,1,0:T(8,128)(2,1)S(1)} async-done(((bf16[4,256,512]{2,1,0:T(8,128)(2,1)}), bf16[4,256,512]{2,1,0:T(8,128)(2,1)S(1)}, u32[]{:S(2)}, u32[]{:S(2)}) %all-to-all-start) | async-done | bytes 1048608 | tf_op jit(solution)/shard_map/all_to_all | solution.py:30
  99.1 16.8 %all-gather.6.cloned.1.call-done.refs_2_.w_ref = bf16[2048,2048]{1,0:T(8,128)(2,1)} async-done(((bf16[256,2048]{1,0:T(8,128)(2,1)}), bf16[2048,2048]{1,0:T(8,128)(2,1)}) %all-gather.6.cloned.1.call-update) | async-done | bytes 8388624 | tf_op jit(solution)/shard_map/all_gather | solution.py:514
  115.9 53.4 %all-to-all-done.1.refs_1_ = bf16[4,768,512]{2,1,0:T(8,128)(2,1)} async-done(((bf16[4,768,512]{2,1,0:T(8,128)(2,1)}), bf16[4,768,512]{2,1,0:T(8,128)(2,1)}, u32[]{:S(2)}, u32[]{:S(2)}) %all-to-all-start.1) | async-done | bytes 3145760 | tf_op jit(solution)/shard_map/all_to_all | solution.py:30
  175.4 15.5 %project.2 = (bf16[1024,2048]{1,0:T(8,128)(2,1)}, f32[3,2048]{1,0:T(4,128)}, bf16[1024,2048]{1,0:T(8,128)(2,1)}) custom-call(bf16[4,256,512]{2,1,0:T(8,128)(2,1)} %copy-done.4, bf16[4,768,512]{2,1,0:T(8,128)(2,1)} %all-to-all-done.1.refs_1_, bf16[2048,2048]{1,0:T(8,128)(2,1)} %all-gather.6.cloned.1.call-done.refs_2_.w_ref), custom_call_target="tpu_custom_call" | custom-call | flops 1 | bytes 1 | tf_op jit(solution)/shard_map/project/pallas_call | solution.py:133
  190.9 9.3 %all-to-all-done.2 = bf16[4,1024,128]{2,1,0:T(8,128)(2,1)S(1)} async-done(((bf16[4,1024,128]{2,1,0:T(8,128)(2,1)}), bf16[4,1024,128]{2,1,0:T(8,128)(2,1)S(1)}, u32[]{:S(2)}, u32[]{:S(2)}) %all-to-all-start.2) | async-done | bytes 1048608 | tf_op jit(solution)/shard_map/all_to_all | solution.py:30
  208.1 6.8 %collective-permute-done.1 = f32[9,2048]{1,0:T(8,128)S(1)} collective-permute-done((f32[9,2048]{1,0:T(8,128)S(1)}, f32[9,2048]{1,0:T(8,128)S(1)}, u32[]{:S(2)}, u32[]{:S(2)}) %collective-permute-start.1) | collective-permute-done | bytes 73760 | tf_op jit(solution)/shard_map/ppermute | solution.py:36
  232.4 14.5 %forward.2 = (f32[2,8192,128]{2,1,0:T(8,128)}, bf16[1,2,512,2048]{3,2,1,0:T(8,128)(2,1)}) custom-call(f32[2,512]{1,0:T(2,128)} %convert_element_type.34.keep, f32[3,2048]{1,0:T(4,128)} %pad_maximum_fusion.7.moments, f32[3,2048]{1,0:T(4,128)} %get-tuple-element.132.gains, bf16[2,512,2048]{2,1,0:T(8,128)(2,1)} %bitcast.64), custom_call_target="tpu_custom_call" | custom-call | flops 1 | bytes 1 | tf_op jit(solution)/shard_map/forward/pallas_call | solution.py:218
  246.9 15.1 %project.3 = (bf16[1024,2048]{1,0:T(8,128)(2,1)}, f32[3,2048]{1,0:T(4,128)}) custom-call(bf16[1,1024,2048]{2,1,0:T(8,128)(2,1)} %bitcast.70, bf16[2048,2048]{1,0:T(8,128)(2,1)} %all-gather.8.cloned.1.call-done.refs_1_.w_ref), custom_call_target="tpu_custom_call" | custom-call | flops 1 | bytes 1 | tf_op jit(solution)/shard_map/project/pallas_call | solution.py:133
  261.9 12.0 %all-to-all-done.3 = bf16[4,1024,256]{2,1,0:T(8,128)(2,1)S(1)} async-done(((bf16[4,1024,256]{2,1,0:T(8,128)(2,1)}), bf16[4,1024,256]{2,1,0:T(8,128)(2,1)S(1)}, u32[]{:S(2)}, u32[]{:S(2)}) %all-to-all-start.3) | async-done | bytes 2097184 | tf_op jit(solution)/shard_map/all_to_all | solution.py:30
  298.3 14.9 %forward.3 = (f32[2,8192,128]{2,1,0:T(8,128)}, bf16[4,2,512,128]{3,2,1,0:T(8,128)(2,1)}, bf16[4,2,512,256]{3,2,1,0:T(8,128)(2,1)}, bf16[4,2,512,128]{3,2,1,0:T(8,128)(2,1)}) custom-call(f32[2,512]{1,0:T(2,128)} %convert_element_type.34.keep, f32[3,2048]{1,0:T(4,128)} %pad_maximum_fusion.12.moments, f32[3,2048]{1,0:T(4,128)} %get-tuple-element.131.gains, ...), custom_call_target="tpu_custom_call" | custom-call | flops 1 | bytes 1 | tf_op jit(solution)/shard_map/forward/pallas_call | solution.py:218
  313.1 9.3 %all-to-all-done.4 = bf16[4,1024,128]{2,1,0:T(8,128)(2,1)S(1)} async-done(((bf16[4,1024,128]{2,1,0:T(8,128)(2,1)}), bf16[4,1024,128]{2,1,0:T(8,128)(2,1)S(1)}, u32[]{:S(2)}, u32[]{:S(2)}) %all-to-all-start.4) | async-done | bytes 1048608 | tf_op jit(solution)/shard_map/all_to_all | solution.py:30
  325.9 14.9 %backward.2 = (f32[2,512,2048]{2,1,0:T(8,128)}, f32[16,2048]{1,0:T(8,128)}) custom-call(f32[2,512]{1,0:T(2,128)} %convert_element_type.34.keep, f32[3,2048]{1,0:T(4,128)} %pad_maximum_fusion.12.moments, f32[3,2048]{1,0:T(4,128)} %get-tuple-element.131.gains, f32[2,8192,128]{2,1,0:T(8,128)} %get-tuple-element.82.s_ref.before_ref, ...), custom_call_target="tpu_custom_call" | custom-call | flops 1 | bytes 1 | tf_op jit(solution)/shard_map/backward/pallas_call | solution.py:342
  341.6 9.4 %all-to-all-done.5 = bf16[4,1024,128]{2,1,0:T(8,128)(2,1)S(1)} async-done(((bf16[4,1024,128]{2,1,0:T(8,128)(2,1)}), bf16[4,1024,128]{2,1,0:T(8,128)(2,1)S(1)}, u32[]{:S(2)}, u32[]{:S(2)}) %all-to-all-start.5) | async-done | bytes 1048608 | tf_op jit(solution)/shard_map/all_to_all | solution.py:30
  373.6 17.5 %dproject.2 = (bf16[1024,2048]{1,0:T(8,128)(2,1)}, f32[1,2048]{1,0:T(1,128)}, bf16[1,1024,2048]{2,1,0:T(8,128)(2,1)}) custom-call(f32[3,2048]{1,0:T(4,128)} %pad_maximum_fusion.12.moments, f32[3,2048]{1,0:T(4,128)} %get-tuple-element.131.gains, f32[3,2048]{1,0:T(4,128)} %add.253.sums, f32[1024,2048]{1,0:T(8,128)} %bitcast.73, ...), custom_call_target="tpu_custom_call" | custom-call | flops 1 | bytes 1 | tf_op jit(solution)/shard_map/dproject/pallas_call | solution.py:421
  391.1 14.7 %backward.3 = (f32[2,512,2048]{2,1,0:T(8,128)}, f32[16,2048]{1,0:T(8,128)}) custom-call(f32[2,512]{1,0:T(2,128)} %convert_element_type.34.keep, f32[3,2048]{1,0:T(4,128)} %pad_maximum_fusion.7.moments, f32[3,2048]{1,0:T(4,128)} %get-tuple-element.132.gains, f32[2,8192,128]{2,1,0:T(8,128)} %get-tuple-element.93.s_ref.before_ref, ...), custom_call_target="tpu_custom_call" | custom-call | flops 1 | bytes 1 | tf_op jit(solution)/shard_map/backward/pallas_call | solution.py:342
  431.3 17.6 %dproject.3 = (bf16[1024,2048]{1,0:T(8,128)(2,1)}, f32[1,2048]{1,0:T(1,128)}, bf16[4,1024,512]{2,1,0:T(8,128)(2,1)}) custom-call(f32[3,2048]{1,0:T(4,128)} %pad_maximum_fusion.7.moments, f32[3,2048]{1,0:T(4,128)} %get-tuple-element.132.gains, f32[3,2048]{1,0:T(4,128)} %bitcast.84, f32[1024,2048]{1,0:T(8,128)} %bitcast.72, ...), custom_call_target="tpu_custom_call" | custom-call | flops 1 | bytes 1 | tf_op jit(solution)/shard_map/dproject/pallas_call | solution.py:421
  448.8 14.8 %weight.3 = bf16[2048,2048]{1,0:T(8,128)(2,1)} custom-call(f32[1,2048]{1,0:T(1,128)} %get-tuple-element.101.level, bf16[1024,2048]{1,0:T(8,128)(2,1)} %bitcast.71, bf16[1024,2048]{1,0:T(8,128)(2,1)} %get-tuple-element.117.dz_ref, f32[2048,1]{1,0:T(8,128)} %copy.25.center_ref), custom_call_target="tpu_custom_call" | custom-call | flops 1 | bytes 1 | tf_op jit(solution)/shard_map/weight/pallas_call | solution.py:459
  465.1 14.7 %weight.2 = bf16[2048,2048]{1,0:T(8,128)(2,1)} custom-call(f32[1,2048]{1,0:T(1,128)} %get-tuple-element.114.level, bf16[1024,2048]{1,0:T(8,128)(2,1)} %get-tuple-element.115.source_ref, bf16[1024,2048]{1,0:T(8,128)(2,1)} %get-tuple-element.116.dz_ref, f32[2048,1]{1,0:T(8,128)} %copy.23.center_ref), custom_call_target="tpu_custom_call" | custom-call | flops 1 | bytes 1 | tf_op jit(solution)/shard_map/weight/pallas_call | solution.py:459
  496.6 54.9 %collective-permute-done.23 = f32[1,2048]{1,0:T(1,128)S(1)} collective-permute-done((f32[1,2048]{1,0:T(1,128)S(1)}, f32[1,2048]{1,0:T(1,128)S(1)}, u32[]{:S(2)}, u32[]{:S(2)}) %collective-permute-start.23) | collective-permute-done | bytes 8224 | tf_op jit(solution)/shard_map/ppermute | solution.py:36
  559.3 18.1 %all-to-all-done.8 = bf16[4,1024,512]{2,1,0:T(8,128)(2,1)} async-done(((bf16[4,1024,512]{2,1,0:T(8,128)(2,1)}), bf16[4,1024,512]{2,1,0:T(8,128)(2,1)}, u32[]{:S(2)}, u32[]{:S(2)}) %all-to-all-start.8) | async-done | bytes 4194336 | tf_op jit(solution)/shard_map/all_to_all | solution.py:30
  587.4 22.8 %reduce-scatter.3.cloned.1.call-done = bf16[256,2048]{1,0:T(8,128)(2,1)} async-done(((bf16[2048,2048]{1,0:T(8,128)(2,1)}), bf16[256,2048]{1,0:T(8,128)(2,1)}) %reduce-scatter.3.cloned.1.call-update) | async-done | bytes 1048592 | tf_op jit(solution)/shard_map/reduce_scatter | solution.py:587
  617.1 8.3 %convert_add_fusion = f32[4096,512]{1,0:T(8,128)} fusion(bf16[4096,512]{1,0:T(8,128)(2,1)} %param.21, bf16[4,1024,512]{2,1,0:T(8,128)(2,1)} %all-to-all-done.8), kind=kLoop, calls=%fused_computation | loop fusion | flops 6291456 | bytes 16777216 | tf_op jit(solution)/shard_map/add | solution.py:584
  626.5 16.5 %all-to-all-done.9 = bf16[4,256,512]{2,1,0:T(8,128)(2,1)} async-done(((bf16[4,256,512]{2,1,0:T(8,128)(2,1)}), bf16[4,256,512]{2,1,0:T(8,128)(2,1)}, u32[]{:S(2)}, u32[]{:S(2)}) %all-to-all-start.9) | async-done | bytes 1048608 | tf_op jit(solution)/shard_map/all_to_all | solution.py:30
  (211 shorter events, 175.2 us)
Async XLA Ops:
  7.2 52.2 %all-gather.4.cloned.1.call-start = ((), (), s32[]{:S(2)}) async-start(), calls=%async_computation.13 | async-start | bytes 2621440 | tf_op jit(solution)/shard_map/all_gather | solution.py:63
  10.6 105.2 %all-gather.6.cloned.1.call-start = ((), (), s32[]{:S(2)}) async-start(), calls=%async_computation.14 | async-start | bytes 9437184 | tf_op jit(solution)/shard_map/all_gather | solution.py:514
  64.9 29.5 %all-to-all-start = ((bf16[4,256,512]{2,1,0:T(8,128)(2,1)}), bf16[4,256,512]{2,1,0:T(8,128)(2,1)S(1)}, u32[]{:S(2)}, u32[]{:S(2)}) async-start(bf16[4,256,512]{2,1,0:T(8,128)(2,1)} %slice.298), calls=%async_computation | async-start | bytes 2097152 | tf_op jit(solution)/shard_map/all_to_all | solution.py:30
  94.3 74.9 %all-to-all-start.1 = ((bf16[4,768,512]{2,1,0:T(8,128)(2,1)}), bf16[4,768,512]{2,1,0:T(8,128)(2,1)}, u32[]{:S(2)}, u32[]{:S(2)}) async-start(bf16[4,768,512]{2,1,0:T(8,128)(2,1)} %slice.227), calls=%async_computation.1 | async-start | bytes 6291456 | tf_op jit(solution)/shard_map/all_to_all | solution.py:30
  99.0 147.8 %all-gather.8.cloned.1.call-start = ((), (), s32[]{:S(2)}) async-start(), calls=%async_computation.15 | async-start | bytes 9437184 | tf_op jit(solution)/shard_map/all_gather | solution.py:516
  171.5 28.7 %all-to-all-start.2 = ((bf16[4,1024,128]{2,1,0:T(8,128)(2,1)}), bf16[4,1024,128]{2,1,0:T(8,128)(2,1)S(1)}, u32[]{:S(2)}, u32[]{:S(2)}) async-start(bf16[4,1024,128]{2,1,0:T(8,128)(2,1)} %bitcast.1), calls=%async_computation.2 | async-start | bytes 2097152 | tf_op jit(solution)/shard_map/all_to_all | solution.py:30
  201.0 5.0 collective-permute-start
  208.1 6.8 %collective-permute-start.1 = (f32[9,2048]{1,0:T(8,128)S(1)}, f32[9,2048]{1,0:T(8,128)S(1)}, u32[]{:S(2)}, u32[]{:S(2)}) collective-permute-start(f32[9,2048]{1,0:T(8,128)S(1)} %pad_maximum_fusion.3), channel_id=1, source_target_pairs={{0,2},{1,3},{2,0},{3,1},{4,6},{5,7},{6,4},{7,5},{8,10},{9,11},{10,... | collective-permute-start | bytes 221192 | tf_op jit(solution)/shard_map/ppermute | solution.py:36
  217.3 8.1 %collective-permute-start.3 = (f32[9,2048]{1,0:T(8,128)}, f32[9,2048]{1,0:T(8,128)S(1)}, u32[]{:S(2)}, u32[]{:S(2)}) collective-permute-start(f32[9,2048]{1,0:T(8,128)} %pad_maximum_fusion.5), channel_id=1, source_target_pairs={{0,8},{4,12},{8,0},{12,4},{16,24},{20,28},{24,16},{28,20},{1,9},{5... | collective-permute-start | bytes 221192 | tf_op jit(solution)/shard_map/ppermute | solution.py:36
  221.8 52.1 %all-to-all-start.3 = ((bf16[4,1024,256]{2,1,0:T(8,128)(2,1)}), bf16[4,1024,256]{2,1,0:T(8,128)(2,1)S(1)}, u32[]{:S(2)}, u32[]{:S(2)}) async-start(bf16[4,1024,256]{2,1,0:T(8,128)(2,1)} %bitcast.10), calls=%async_computation.3 | async-start | bytes 4194304 | tf_op jit(solution)/shard_map/all_to_all | solution.py:30
  225.6 5.3 collective-permute-start.4
  290.2 7.3 %collective-permute-start.9 = (f32[3,2048]{1,0:T(4,128)S(1)}, f32[3,2048]{1,0:T(4,128)S(1)}, u32[]{:S(2)}, u32[]{:S(2)}) collective-permute-start(f32[3,2048]{1,0:T(4,128)S(1)} %pad_maximum_fusion.11), channel_id=1, source_target_pairs={{0,16},{4,20},{8,24},{12,28},{16,0},{20,4},{24,8},{28,12},{1,17},{... | collective-permute-start | bytes 73736 | tf_op jit(solution)/shard_map/ppermute | solution.py:36
  294.0 28.4 %all-to-all-start.4 = ((bf16[4,1024,128]{2,1,0:T(8,128)(2,1)}), bf16[4,1024,128]{2,1,0:T(8,128)(2,1)S(1)}, u32[]{:S(2)}, u32[]{:S(2)}) async-start(bf16[4,1024,128]{2,1,0:T(8,128)(2,1)} %bitcast.17), calls=%async_computation.4 | async-start | bytes 2097152 | tf_op jit(solution)/shard_map/all_to_all | solution.py:30
  322.4 28.7 %all-to-all-start.5 = ((bf16[4,1024,128]{2,1,0:T(8,128)(2,1)}), bf16[4,1024,128]{2,1,0:T(8,128)(2,1)S(1)}, u32[]{:S(2)}, u32[]{:S(2)}) async-start(bf16[4,1024,128]{2,1,0:T(8,128)(2,1)} %bitcast.83), calls=%async_computation.5 | async-start | bytes 2097152 | tf_op jit(solution)/shard_map/all_to_all | solution.py:30
  355.0 4.9 collective-permute-start.11
  359.9 49.0 %all-to-all-start.6 = ((bf16[4,1024,256]{2,1,0:T(8,128)(2,1)}), bf16[4,1024,256]{2,1,0:T(8,128)(2,1)S(1)}, u32[]{:S(2)}, u32[]{:S(2)}) async-start(bf16[4,1024,256]{2,1,0:T(8,128)(2,1)} %bitcast.79), calls=%async_computation.6 | async-start | bytes 4194304 | tf_op jit(solution)/shard_map/all_to_all | solution.py:30
  417.8 31.0 %all-to-all-start.7 = ((bf16[4,1024,128]{2,1,0:T(8,128)(2,1)}), bf16[4,1024,128]{2,1,0:T(8,128)(2,1)S(1)}, u32[]{:S(2)}, u32[]{:S(2)}) async-start(bf16[4,1024,128]{2,1,0:T(8,128)(2,1)} %bitcast.80), calls=%async_computation.7 | async-start | bytes 2097152 | tf_op jit(solution)/shard_map/all_to_all | solution.py:30
  421.3 135.7 %reduce-scatter.5.cloned.1.call-start = ((), (), s32[]{:S(2)}) async-start(), calls=%async_computation.17 | async-start | bytes 9437184 | tf_op jit(solution)/shard_map/reduce_scatter | solution.py:587
  463.7 146.6 %reduce-scatter.3.cloned.1.call-start = ((), (), s32[]{:S(2)}) async-start(), calls=%async_computation.16 | async-start | bytes 9437184 | tf_op jit(solution)/shard_map/reduce_scatter | solution.py:587
  479.9 97.5 %all-to-all-start.8 = ((bf16[4,1024,512]{2,1,0:T(8,128)(2,1)}), bf16[4,1024,512]{2,1,0:T(8,128)(2,1)}, u32[]{:S(2)}, u32[]{:S(2)}) async-start(bf16[4,1024,512]{2,1,0:T(8,128)(2,1)} %get-tuple-element.113), calls=%async_computation.8 | async-start | bytes 8388608 | tf_op jit(solution)/shard_map/all_to_all | solution.py:30
  493.9 57.6 %collective-permute-start.23 = (f32[1,2048]{1,0:T(1,128)S(1)}, f32[1,2048]{1,0:T(1,128)S(1)}, u32[]{:S(2)}, u32[]{:S(2)}) collective-permute-start(f32[1,2048]{1,0:T(1,128)S(1)} %add.263), channel_id=1, source_target_pairs={{0,1},{1,0},{2,3},{3,2},{4,5},{5,4},{6,7},{7,6},{8,9},{9,8},{10,11... | collective-permute-start | bytes 24584 | tf_op jit(solution)/shard_map/ppermute | solution.py:36
  551.5 29.4 %collective-permute-start.24 = (f32[1,2048]{1,0:T(1,128)S(1)}, f32[1,2048]{1,0:T(1,128)S(1)}, u32[]{:S(2)}, u32[]{:S(2)}) collective-permute-start(f32[1,2048]{1,0:T(1,128)S(1)} %add.264), channel_id=1, source_target_pairs={{0,2},{1,3},{2,0},{3,1},{4,6},{5,7},{6,4},{7,5},{8,10},{9,11},{10,... | collective-permute-start | bytes 24584 | tf_op jit(solution)/shard_map/ppermute | solution.py:36
  577.4 35.2 %all-to-all-start.10 = ((bf16[4,256,512]{2,1,0:T(8,128)(2,1)}), bf16[4,256,512]{2,1,0:T(8,128)(2,1)S(1)}, u32[]{:S(2)}, u32[]{:S(2)}) async-start(bf16[4,256,512]{2,1,0:T(8,128)(2,1)} %bitcast.75), calls=%async_computation.12 | async-start | bytes 2097152 | tf_op jit(solution)/shard_map/all_to_all | solution.py:30
  612.5 30.4 %all-to-all-start.9 = ((bf16[4,256,512]{2,1,0:T(8,128)(2,1)}), bf16[4,256,512]{2,1,0:T(8,128)(2,1)}, u32[]{:S(2)}, u32[]{:S(2)}) async-start(bf16[4,256,512]{2,1,0:T(8,128)(2,1)} %bitcast.62), calls=%async_computation.10 | async-start | bytes 2097152 | tf_op jit(solution)/shard_map/all_to_all | solution.py:30
  (36 other events, 742.8 us)
Sparse Core Ops, SparseCore 0:
  10.7 48.6 all-gather.3
  62.7 53.0 all-gather.5
  117.7 54.3 all-gather.7
  463.8 70.8 reduce-scatter.4
  538.9 71.2 reduce-scatter.2
where the time goes:
time: 655 us; the launch traced here: 652 us
  waiting for transfers between devices  363 us (55%)
  Pallas kernels  154 us (24%)
  starting transfers between devices  60.1 us (9%)
  local copies, waits for them, and re-layouts  32.1 us (5%)
  other arithmetic  28.3 us (4%)
  between operations  14.6 us (2%)
    all_to_all x11, waiting for transfers between devices, swap(): return lax.all_to_all(blocks, 'narrow', split_axis=0, concat_axis=0)  152 us
    ppermute x25, waiting for transfers between devices, merge_all(): other = lax.ppermute(value, axis, [(i, i ^ k) for i in range(size)])  122 us
    all_gather x1, waiting for transfers between devices, gather_rows(): lax.all_gather(jnp.concatenate(shares, 0), 'narrow', axis=1, tiled=True)  48.7 us
    all_to_all x11, starting transfers between devices, swap(): return lax.all_to_all(blocks, 'narrow', split_axis=0, concat_axis=0)  42.8 us
    pallas_call x2, Pallas kernels, dproject(): pl.pallas_call(functools.partial(dproject_kernel, total_frames), grid=(fr...  35.1 us
    pallas_call x2, Pallas kernels, project(): pl.pallas_call(kernel, grid=(steps,), in_specs=[whole(p.shape) for p in p...  30.6 us
    pallas_call x2, Pallas kernels, backward(): pl.pallas_call(functools.partial(backward_kernel, ranges), grid=(length /...  29.6 us
    pallas_call x2, Pallas kernels, weight_terms(): pl.pallas_call(weight_kernel, grid=(rows // tile,), in_specs=[whole((1, c...  29.5 us
  transfers between devices with their start and end apart: 41, of which 34 were waited for; matrix products, arithmetic and copies ran while one was open for 7% of the time, Pallas kernels for 21%

commit v1 on v0

--- a/solution.py
+++ b/solution.py
@@ -47,11 +47,12 @@
     count = [frames]
 
     def merge(a, b):
+        row = lax.broadcasted_iota(jnp.int32, a.shape, 0)
+        scale = jnp.where((row == 0) | (row == 2), 0.5, 1.0)
         gap = a[0:1] - b[0:1]
-        squares = a[1:2] + b[1:2] + gap * gap * (count[0] / 2)
+        squares = gap * gap * (count[0] / 2)
         count[0] *= 2
-        means = (a + b) * 0.5
-        return jnp.concatenate([means[0:1], squares, means[2:3], a[3:] + b[3:]])
+        return (a + b) * scale + jnp.where(row == 1, squares, 0.0)
 
     return merge
 
@@ -414,10 +415,11 @@
         ).astype(jnp.bfloat16)
 
 
-def dproject(dpre, z, moments, gains, sums, weight, parts, total_frames):
-    frames, width = z.shape
+def dproject(dpre, z, moments, gains, sums, weight, parts, total_frames, lo, hi):
+    width = z.shape[1]
     rows = weight.shape[0]
-    step = min(256, frames)
+    step = min(256, hi - lo)
+    frames = hi - lo
     return pl.pallas_call(
         functools.partial(dproject_kernel, total_frames),
         grid=(frames // step,),
@@ -425,8 +427,8 @@
             whole((3, width)),
             whole((3, width)),
             whole((3, width)),
-            pl.BlockSpec((step, width), lambda i: (i, 0)),
-            pl.BlockSpec((step, width), lambda i: (i, 0)),
+            pl.BlockSpec((step, width), lambda i: (i + lo // step, 0)),
+            pl.BlockSpec((step, width), lambda i: (i + lo // step, 0)),
             whole((rows, width)),
         ],
         out_specs=[
@@ -445,32 +447,44 @@
     )(moments, gains, sums, dpre, z, weight)
 
 
-def weight_kernel(level, source_ref, dz_ref, center_ref, out_ref):
-    terms = lax.dot_general(
-        source_ref[...], dz_ref[...], (((0,), (0,)), ((), ())), preferred_element_type=jnp.float32
-    )
-    out_ref[...] = (terms - center_ref[...] * level[...]).astype(jnp.bfloat16)
-
-
-def weight_terms(source, center, dz, level):
+def weight_kernel(pieces, *refs):
+    level_refs, dz_refs = refs[:pieces], refs[pieces : 2 * pieces]
+    center_ref, source_ref, out_ref = refs[2 * pieces :]
+    level = sum(level_ref[...] for level_ref in level_refs)
+    center = jnp.transpose(jnp.broadcast_to(center_ref[...], (8, center_ref.shape[1])))[:, :1]
+    terms = -center * level
+    lo = 0
+    for dz_ref in dz_refs:
+        count = dz_ref.shape[0]
+        terms += lax.dot_general(
+            source_ref[lo : lo + count, :],
+            dz_ref[...],
+            (((0,), (0,)), ((), ())),
+            preferred_element_type=jnp.float32,
+        )
+        lo += count
+    out_ref[...] = terms.astype(jnp.bfloat16)
+
+
+def weight_terms(source, center, dz, levels):
     frames, rows = source.shape
-    cols = dz.shape[1]
+    cols = dz[0].shape[1]
     tile = 256
     return pl.pallas_call(
-        weight_kernel,
+        functools.partial(weight_kernel, len(dz)),
         grid=(rows // tile,),
-        in_specs=[
-            whole((1, cols)),
+        in_specs=[whole((1, cols))] * len(dz)
+        + [whole(d.shape) for d in dz]
+        + [
+            pl.BlockSpec((1, tile), lambda i: (0, i)),
             pl.BlockSpec((frames, tile), lambda i: (0, i)),
-            whole((frames, cols)),
-            pl.BlockSpec((tile, 1), lambda i: (i, 0)),
         ],
         out_specs=pl.BlockSpec((tile, cols), lambda i: (i, 0)),
         out_shape=jax.ShapeDtypeStruct((rows, cols), jnp.bfloat16),
         compiler_params=params_of(),
         cost_estimate=BRIEF,
         name="weight",
-    )(level, source, dz, center.reshape(rows, 1))
+    )(*levels, *dz, center, source)
 
 
 def per_device(sizes, inputs, flags, w_one, *rest):
@@ -499,32 +513,32 @@
     spread = jnp.zeros((6, each * wide * narrow), jnp.float32)
     spread = lax.dynamic_update_slice_in_dim(spread, own, (n * wide + w) * each, 1)
 
-    groups = [(0, tiles // 4), (tiles // 4, 3 * tiles // 4), (3 * tiles // 4, tiles)]
-
-    def columns(held, g):
-        lo, hi = groups[g]
-        return swap(held[:, lo * LANES : hi * LANES].reshape(narrow, frames, -1))
+    groups_in = [(0, tiles // 4), (tiles // 4, 3 * tiles // 4), (3 * tiles // 4, tiles)]
+    groups_out = groups_in
+
+    held = [
+        cotangent[:, lo * LANES : hi * LANES].reshape(narrow, frames, -1) for lo, hi in groups_in
+    ]
 
     split = frames // 4
-    held = inputs.reshape(narrow, frames, part)
-    piece = swap(held[:, :split])
+    blocks = inputs.reshape(narrow, frames, part)
+    early, late = blocks[:, :split], blocks[:, split:]
+    early = swap(early)
     share_one, share_two = gather_rows([w_one, w_two], wide)
-    share_one, share_two, held = tie((share_one, share_two, held))
-    pieces = [piece, swap(held[:, split:])]
+    share_one, share_two, early, late, held = tie((share_one, share_two, early, late, held))
+    late = swap(late)
     full_one = lax.all_gather(share_one, "wide", axis=0, tiled=True)
-    full_one, share_two = tie((full_one, share_two))
+    late, held, share_two = tie((late, held, share_two))
     full_two = lax.all_gather(share_two, "wide", axis=0, tiled=True)
-
-    pieces, held = tie((pieces, cotangent))
-    group = columns(held, 0)
-    z_one, moments, source = project(pieces, full_one)
+    group = swap(held[0])
+    z_one, moments, source = project([early, late], full_one)
     moments, group = tie((moments, group))
     grads = [group]
     moments = jnp.concatenate([moments, spread])
     merge = merge_moments(frames)
     moments = along(moments, merge)
-    moments, held = tie((moments, cotangent))
-    group = columns(held, 1)
+    moments, held = tie((moments, held))
+    group = swap(held[1])
     moments_one = across(moments, merge)
     gains_one, gains_two = moments_one[3:6], moments_one[6:9]
     moments_one = moments_one[:3]
@@ -537,63 +551,76 @@
     grads.append(group)
     merge = merge_moments(frames)
     moments = along(moments, merge)
-    moments, held = tie((moments, cotangent))
-    group = columns(held, 2)
+    moments, held = tie((moments, held))
+    group = swap(held[2])
     moments_two = across(moments, merge)
     states_two, h_two = forward(
-        z_two, moments_two, gains_two, keep, narrow, groups, total_frames
+        z_two, moments_two, gains_two, keep, narrow, groups_out, total_frames
     )
     h_two, group = tie((h_two, group))
     grads.append(group)
 
     second = [swap(h_two[0])]
-    dpre, sums = backward(grads, groups, states_two, z_two, moments_two, gains_two, keep)
+    dpre, sums = backward(grads, groups_in, states_two, z_two, moments_two, gains_two, keep)
     sums, second[0] = tie((sums, second[0]))
     sums = along(sums, add)
     sums, h_two = tie((sums, h_two))
     group = swap(h_two[1])
     sums_two = across(sums, add)
     dz_two, level_two, dh_one = dproject(
-        dpre, z_two, moments_two, gains_two, sums_two, full_two, 1, total_frames
+        dpre, z_two, moments_two, gains_two, sums_two, full_two, 1, total_frames, 0, frames
     )
+    center_one, center_two = moments_one[2:3], moments_two[2:3]
+    terms_two = weight_terms(h_one[0], center_two, [dz_two], [level_two])
+    terms_two, dh_one, group = tie((terms_two, dh_one, group))
+    second.append(group)
+    plane_two = lax.psum_scatter(terms_two, "wide", scatter_dimension=0, tiled=True)
     dpre, sums = backward([dh_one], every, states_one, z_one, moments_one, gains_one, keep)
-    own_level_two = level_two
-    sums = jnp.concatenate([sums, level_two], 0)
-    sums, group = tie((sums, group))
-    second.append(group)
-    sums = along(sums, add)
+    sums = along(jnp.concatenate([sums, level_two], 0), add)
     sums, h_two = tie((sums, h_two))
     group = swap(h_two[2])
     sums_one = across(sums, add)
-    level_two = sums_one[3:]
+    level_two = sums_one[3:, :]
     sums_one = sums_one[:3]
-    dz_one, level_one, dsource = dproject(
-        dpre, z_one, moments_one, gains_one, sums_one, full_one, narrow, total_frames
+    back = functools.partial(
+        dproject, dpre, z_one, moments_one, gains_one, sums_one, full_one, narrow, total_frames
     )
-    dsource, group, dz_one, dz_two = tie((dsource, group, dz_one, dz_two))
+    dz_early, level_early, da_early = back(0, split)
+    da_early, group = tie((da_early, group))
     second.append(group)
-    arrived = swap(dsource).reshape(inputs.shape)
+    da_early = swap(da_early)
+    dz_late, level_late, da_late = back(split, frames)
+    terms_one = weight_terms(source, center_one, [dz_early, dz_late], [level_early, level_late])
+    da_early, da_late, terms_one, plane_two = tie((da_early, da_late, terms_one, plane_two))
+    plane_one = lax.psum_scatter(terms_one, "wide", scatter_dimension=0, tiled=True)
+    da_late = swap(da_late)
+    level_one = across(level_early + level_late, add)
 
     whole_two = jnp.concatenate(second, axis=2).reshape(inputs.shape).astype(jnp.float32)
     output = (inputs.astype(jnp.float32) + whole_two).astype(jnp.bfloat16)
 
-    center_one, center_two = moments_one[2], moments_two[2]
-    terms_two = weight_terms(h_one[0], center_two, dz_two, own_level_two)
-    terms_one = weight_terms(source, center_one, dz_one, level_one)
-    level_one = along(across(level_one, add), add)
+    def summed(plane):
+        blocks = plane.reshape(plane.shape[0], narrow, part)
+        weight = lax.dynamic_index_in_dim(blocks, n, 1, keepdims=False).astype(jnp.float32)
+        for k in range(1, narrow):
+            block = lax.dynamic_index_in_dim(blocks, n ^ k, 1, keepdims=False)
+            weight += lax.ppermute(block, "narrow", [(i, i ^ k) for i in range(narrow)])
+        return weight
+
+    span = plane_one.shape[0]
+    dw_two = summed(plane_two)
+    level_one, da_late = tie((level_one, da_late))
+    arrived = jnp.concatenate([da_early, da_late], axis=1).reshape(inputs.shape)
     grad_inputs = cotangent.astype(jnp.float32) + arrived.astype(jnp.float32)
-
-    def summed(terms, center, level):
-        plane = lax.psum_scatter(terms, "wide", scatter_dimension=0, tiled=True)
-        span = plane.shape[0]
-        blocks = plane.reshape(span, narrow, part).transpose(1, 0, 2)
-        weight = jnp.sum(swap(blocks).astype(jnp.float32), 0)
-        rows_of = lax.dynamic_slice_in_dim(center, w * span, span, 0)
-        cols_of = lax.dynamic_slice_in_dim(level[0], n * part, part, 0)
-        return weight + rows_of[:, None] * cols_of[None, :]
-
-    dw_two = summed(terms_two, center_two, level_two)
-    dw_one = summed(terms_one, center_one, level_one)
+    level_one = along(level_one, add)
+    dw_one = summed(plane_one)
+
+    def restored(weight, center, level):
+        rows_of = lax.dynamic_slice_in_dim(center, w * span, span, 1).reshape(span, 1)
+        return weight + rows_of * lax.dynamic_slice_in_dim(level, n * part, part, 1)
+
+    dw_one = restored(dw_one, center_one, level_one)
+    dw_two = restored(dw_two, center_two, level_two)
 
     def small(sums, moments):
         rstd = lax.rsqrt(moments[1] / total_frames + EPSILON)

time: 655 us -> 616 us (0.940)
  waiting for transfers between devices: 363 us -> 242 us
  blocking collectives: 0 us -> 76.6 us
    all_to_all x11 -> x9, waiting for transfers between devices: 152 us -> 38.7 us  [swap(): return lax.all_to_all(blocks, 'narrow', split_axis=0, concat_axis=0)]
    ppermute x0 -> x6, waiting for transfers between devices: none -> 80.7 us  [summed(): weight += lax.ppermute(block, 'narrow', [(i, i ^ k) for i in range(narrow)])]
    all_to_all x0 -> x1, blocking collectives: none -> 76.6 us  [swap(): return lax.all_to_all(blocks, 'narrow', split_axis=0, concat_axis=0)]
    ppermute x25, waiting for transfers between devices: 122 us -> 69.3 us  [merge_all(): other = lax.ppermute(value, axis, [(i, i ^ k) for i in range(size)])]
    reduce_scatter x2, waiting for transfers between devices: 22.8 us -> 0.02 us  [the longest x1 0.02 us: per_device(): lax.psum_scatter(terms_two, 'wide', scatter_dimension=0, tiled=True)]
    all_gather x1, waiting for transfers between devices: 16.8 us -> 0.02 us  [per_device(): full_one = lax.all_gather(share_one, 'wide', axis=0, tiled=True)]
    ppermute x0 -> x6, starting transfers between devices: none -> 8.97 us  [summed(): weight += lax.ppermute(block, 'narrow', [(i, i ^ k) for i in range(narrow)])]
    all_to_all x11 -> x9, starting transfers between devices: 42.8 us -> 36.3 us  [swap(): return lax.all_to_all(blocks, 'narrow', split_axis=0, concat_axis=0)]
  transfers between devices with their start and end apart: 41 -> 45, of which waited for: 34 -> 33; matrix products, arithmetic and copies ran while one was open for 7% -> 8% of each run, Pallas kernels for 21% -> 26%
where the time goes in v1:
time: 616 us; the launch traced here: 614 us
  waiting for transfers between devices  242 us (39%)
  Pallas kernels  160 us (26%)
  blocking collectives  76.6 us (12%)
  starting transfers between devices  62 us (10%)
  local copies, waits for them, and re-layouts  32.9 us (5%)
  other arithmetic  26.7 us (4%)
  between operations  14.5 us (2%)
    ppermute x6, waiting for transfers between devices, summed(): weight += lax.ppermute(block, 'narrow', [(i, i ^ k) for i in range(narrow)])  80.7 us
    all_to_all x1, blocking collectives, swap(): return lax.all_to_all(blocks, 'narrow', split_axis=0, concat_axis=0)  76.6 us
    ppermute x25, waiting for transfers between devices, merge_all(): other = lax.ppermute(value, axis, [(i, i ^ k) for i in range(size)])  69.3 us
    all_gather x1, waiting for transfers between devices, gather_rows(): lax.all_gather(jnp.concatenate(shares, 0), 'narrow', axis=1, tiled=True)  52.8 us
    pallas_call x3, Pallas kernels, dproject(): pl.pallas_call(functools.partial(dproject_kernel, total_frames), grid=(fr...  40 us
    all_to_all x9, waiting for transfers between devices, swap(): return lax.all_to_all(blocks, 'narrow', split_axis=0, concat_axis=0)  38.7 us
    all_to_all x9, starting transfers between devices, swap(): return lax.all_to_all(blocks, 'narrow', split_axis=0, concat_axis=0)  36.3 us
    pallas_call x2, Pallas kernels, project(): pl.pallas_call(kernel, grid=(steps,), in_specs=[whole(p.shape) for p in p...  31 us
  transfers between devices with their start and end apart: 45, of which 33 were waited for; matrix products, arithmetic and copies ran while one was open for 8% of the time, Pallas kernels for 26%

profile of v1, /device:TPU:0, one launch (start us, length us, event | category | flops | bytes accessed | tf_op | source)
XLA Modules:
  0.0 613.8 jit_solution(17411855158913162578)
XLA Ops:
  12.9 6.3 %all-to-all-start = ((bf16[4,256,512]{2,1,0:T(8,128)(2,1)}), bf16[4,256,512]{2,1,0:T(8,128)(2,1)S(1)}, u32[]{:S(2)}, u32[]{:S(2)}) async-start(bf16[4,256,512]{2,1,0:T(8,128)(2,1)} %slice.183), calls=%async_computation | async-start | bytes 2097152 | tf_op jit(solution)/shard_map/all_to_all | solution.py:30
  26.3 52.8 %all-gather.4.cloned.1.call-done = bf16[512,2048]{1,0:T(8,128)(2,1)} async-done(((bf16[512,512]{1,0:T(8,128)(2,1)}), bf16[512,2048]{1,0:T(8,128)(2,1)}) %all-gather.4.cloned.1.call-update) | async-done | bytes 2097168 | tf_op jit(solution)/shard_map/all_gather | solution.py:64
  82.3 76.6 %all_to_all.50.refs_1_ = bf16[4,768,512]{2,1,0:T(8,128)(2,1)} all-to-all(bf16[4,768,512]{2,1,0:T(8,128)(2,1)} %slice.184), channel_id=1, replica_groups=mesh['wide'=8,'narrow'=4] {'narrow'}, dimensions={0} | all-to-all | bytes 6291456 | tf_op jit(solution)/shard_map/all_to_all | solution.py:30
  162.9 16.0 %project.2 = (bf16[1024,2048]{1,0:T(8,128)(2,1)}, f32[3,2048]{1,0:T(4,128)}, bf16[1024,2048]{1,0:T(8,128)(2,1)}) custom-call(bf16[4,256,512]{2,1,0:T(8,128)(2,1)} %copy-done.7, bf16[4,768,512]{2,1,0:T(8,128)(2,1)} %all_to_all.50.refs_1_, bf16[2048,2048]{1,0:T(8,128)(2,1)} %all-gather.6.cloned.1.call-done.refs_2_.w_ref), custom_call_target="tpu_custom_call" | custom-call | flops 1 | bytes 1 | tf_op jit(solution)/shard_map/project/pallas_call | solution.py:134
  178.9 8.9 %all-to-all-done.2 = bf16[4,1024,128]{2,1,0:T(8,128)(2,1)S(1)} async-done(((bf16[4,1024,128]{2,1,0:T(8,128)(2,1)}), bf16[4,1024,128]{2,1,0:T(8,128)(2,1)S(1)}, u32[]{:S(2)}, u32[]{:S(2)}) %all-to-all-start.2) | async-done | bytes 1048608 | tf_op jit(solution)/shard_map/all_to_all | solution.py:30
  195.4 7.1 %collective-permute-done.1 = f32[9,2048]{1,0:T(8,128)S(1)} collective-permute-done((f32[9,2048]{1,0:T(8,128)S(1)}, f32[9,2048]{1,0:T(8,128)S(1)}, u32[]{:S(2)}, u32[]{:S(2)}) %collective-permute-start.1) | collective-permute-done | bytes 73760 | tf_op jit(solution)/shard_map/ppermute | solution.py:36
  219.7 14.5 %forward.2 = (f32[2,8192,128]{2,1,0:T(8,128)}, bf16[1,2,512,2048]{3,2,1,0:T(8,128)(2,1)}) custom-call(f32[2,512]{1,0:T(2,128)} %convert_element_type.58.keep, f32[3,2048]{1,0:T(4,128)} %get-tuple-element.160.moments, f32[3,2048]{1,0:T(4,128)} %get-tuple-element.159.gains, bf16[2,512,2048]{2,1,0:T(8,128)(2,1)} %bitcast.84), custom_call_target="tpu_custom_call" | custom-call | flops 1 | bytes 1 | tf_op jit(solution)/shard_map/forward/pallas_call | solution.py:219
  234.2 15.1 %project.3 = (bf16[1024,2048]{1,0:T(8,128)(2,1)}, f32[3,2048]{1,0:T(4,128)}) custom-call(bf16[1,1024,2048]{2,1,0:T(8,128)(2,1)} %bitcast.90, bf16[2048,2048]{1,0:T(8,128)(2,1)} %all-gather.8.cloned.1.call-done.refs_1_.w_ref), custom_call_target="tpu_custom_call" | custom-call | flops 1 | bytes 1 | tf_op jit(solution)/shard_map/project/pallas_call | solution.py:134
  249.3 6.1 all-to-all-done.3
  277.4 14.9 %forward.3 = (f32[2,8192,128]{2,1,0:T(8,128)}, bf16[4,2,512,128]{3,2,1,0:T(8,128)(2,1)}, bf16[4,2,512,256]{3,2,1,0:T(8,128)(2,1)}, bf16[4,2,512,128]{3,2,1,0:T(8,128)(2,1)}) custom-call(f32[2,512]{1,0:T(2,128)} %convert_element_type.58.keep, f32[3,2048]{1,0:T(4,128)} %select_add_fusion.5.moments, f32[3,2048]{1,0:T(4,128)} %get-tuple-element.158.gains, ...), custom_call_target="tpu_custom_call" | custom-call | flops 1 | bytes 1 | tf_op jit(solution)/shard_map/forward/pallas_call | solution.py:219
  292.2 6.4 %all-to-all-done.4 = bf16[4,1024,128]{2,1,0:T(8,128)(2,1)S(1)} async-done(((bf16[4,1024,128]{2,1,0:T(8,128)(2,1)}), bf16[4,1024,128]{2,1,0:T(8,128)(2,1)S(1)}, u32[]{:S(2)}, u32[]{:S(2)}) %all-to-all-start.4) | async-done | bytes 1048608 | tf_op jit(solution)/shard_map/all_to_all | solution.py:30
  303.1 14.9 %backward.2 = (f32[2,512,2048]{2,1,0:T(8,128)}, f32[16,2048]{1,0:T(8,128)}) custom-call(f32[2,512]{1,0:T(2,128)} %convert_element_type.58.keep, f32[3,2048]{1,0:T(4,128)} %select_add_fusion.5.moments, f32[3,2048]{1,0:T(4,128)} %get-tuple-element.158.gains, f32[2,8192,128]{2,1,0:T(8,128)} %get-tuple-element.100.s_ref.before_ref, ...), custom_call_target="tpu_custom_call" | custom-call | flops 1 | bytes 1 | tf_op jit(solution)/shard_map/backward/pallas_call | solution.py:343
  318.8 9.5 %all-to-all-done.5 = bf16[4,1024,128]{2,1,0:T(8,128)(2,1)S(1)} async-done(((bf16[4,1024,128]{2,1,0:T(8,128)(2,1)}), bf16[4,1024,128]{2,1,0:T(8,128)(2,1)S(1)}, u32[]{:S(2)}, u32[]{:S(2)}) %all-to-all-start.5) | async-done | bytes 1048608 | tf_op jit(solution)/shard_map/all_to_all | solution.py:30
  350.9 17.5 %dproject.3 = (bf16[1024,2048]{1,0:T(8,128)(2,1)}, f32[1,2048]{1,0:T(1,128)}, bf16[1,1024,2048]{2,1,0:T(8,128)(2,1)}) custom-call(f32[3,2048]{1,0:T(4,128)} %select_add_fusion.5.moments, f32[3,2048]{1,0:T(4,128)} %get-tuple-element.158.gains, f32[3,2048]{1,0:T(4,128)} %add.230.sums, f32[1024,2048]{1,0:T(8,128)} %bitcast.94, ...), custom_call_target="tpu_custom_call" | custom-call | flops 1 | bytes 1 | tf_op jit(solution)/shard_map/dproject/pallas_call | solution.py:423
  368.4 14.4 %weight.2 = bf16[2048,2048]{1,0:T(8,128)(2,1)} custom-call(f32[1,2048]{1,0:T(1,128)} %get-tuple-element.116.refs_0_, bf16[1024,2048]{1,0:T(8,128)(2,1)} %get-tuple-element.117.refs_1_, f32[1,2048]{1,0:T(1,128)} %get-tuple-element.165.refs_2_, bf16[1024,2048]{1,0:T(8,128)(2,1)} %bitcast.91), custom_call_target="tpu_custom_call" | custom-call | flops 1 | bytes 1 | tf_op jit(solution)/shard_map/weight/pallas_call | solution.py:473
  387.5 15.6 %backward.3 = (f32[2,512,2048]{2,1,0:T(8,128)}, f32[16,2048]{1,0:T(8,128)}) custom-call(f32[2,512]{1,0:T(2,128)} %convert_element_type.58.keep, f32[3,2048]{1,0:T(4,128)} %get-tuple-element.160.moments, f32[3,2048]{1,0:T(4,128)} %get-tuple-element.159.gains, f32[2,8192,128]{2,1,0:T(8,128)} %get-tuple-element.121.s_ref.before_ref, ...), custom_call_target="tpu_custom_call" | custom-call | flops 1 | bytes 1 | tf_op jit(solution)/shard_map/backward/pallas_call | solution.py:343
  427.8 8.0 %dproject.4 = (bf16[256,2048]{1,0:T(8,128)(2,1)}, f32[1,2048]{1,0:T(1,128)}, bf16[4,256,512]{2,1,0:T(8,128)(2,1)}) custom-call(f32[3,2048]{1,0:T(4,128)} %get-tuple-element.160.moments, f32[3,2048]{1,0:T(4,128)} %get-tuple-element.159.gains, f32[3,2048]{1,0:T(4,128)} %bitcast.101, f32[1024,2048]{1,0:T(8,128)} %bitcast.88, ...), custom_call_target="tpu_custom_call" | custom-call | flops 1 | bytes 1 | tf_op jit(solution)/shard_map/dproject/pallas_call | solution.py:423
  444.3 14.6 %dproject.5 = (bf16[768,2048]{1,0:T(8,128)(2,1)}, f32[1,2048]{1,0:T(1,128)}, bf16[4,768,512]{2,1,0:T(8,128)(2,1)}) custom-call(f32[3,2048]{1,0:T(4,128)} %get-tuple-element.160.moments, f32[3,2048]{1,0:T(4,128)} %get-tuple-element.159.gains, f32[3,2048]{1,0:T(4,128)} %bitcast.102, f32[1024,2048]{1,0:T(8,128)} %bitcast.89, ...), custom_call_target="tpu_custom_call" | custom-call | flops 1 | bytes 1 | tf_op jit(solution)/shard_map/dproject/pallas_call | solution.py:423
  458.9 14.2 %weight.3 = bf16[2048,2048]{1,0:T(8,128)(2,1)} custom-call(f32[1,2048]{1,0:T(1,128)} %get-tuple-element.132.refs_0_, f32[1,2048]{1,0:T(1,128)} %get-tuple-element.133.refs_1_, bf16[256,2048]{1,0:T(8,128)(2,1)} %get-tuple-element.134.refs_2_, bf16[768,2048]{1,0:T(8,128)(2,1)} %get-tuple-element.135.refs_3_, f32[1,2048]{1,0:T(1,128)} %get-tuple-element.157.refs_4_, ...), custom_call_target="tpu_custom_call" | custom-call | flops 1 | bytes 1 | tf_op jit(solution)/shard_map/weight/pallas_call | solution.py:473
  474.1 5.2 all-to-all-start.9
  500.9 40.2 %collective-permute-done.30 = bf16[256,512]{1,0:T(8,128)(2,1)S(1)} collective-permute-done((bf16[256,512]{1,0:T(8,128)(2,1)S(1)}, bf16[256,512]{1,0:T(8,128)(2,1)S(1)}, u32[]{:S(2)}, u32[]{:S(2)}) %collective-permute-start.30) | collective-permute-done | bytes 262176 | tf_op jit(solution)/shard_map/ppermute | solution.py:607
  542.5 29.1 %collective-permute-done.29 = bf16[256,512]{1,0:T(8,128)(2,1)S(1)} collective-permute-done((bf16[256,512]{1,0:T(8,128)(2,1)S(1)}, bf16[256,512]{1,0:T(8,128)(2,1)S(1)}, u32[]{:S(2)}, u32[]{:S(2)}) %collective-permute-start.29) | collective-permute-done | bytes 262176 | tf_op jit(solution)/shard_map/ppermute | solution.py:607
  587.4 8.9 %convert_add_fusion = (f32[4096,512]{1,0:T(8,128)}, bf16[4096,512]{1,0:T(8,128)(2,1)}) fusion(bf16[4096,512]{1,0:T(8,128)(2,1)} %param.21, bf16[4,1024,512]{2,1,0:T(8,128)(2,1)} %pad_maximum_fusion.1, bf16[4,1024,512]{2,1,0:T(8,128)(2,1)} %pad_maximum_fusion, bf16[4096,512]{1,0:T(8,128)(2,1)S(1)} %copy-done.2), kind=kLoop, calls=%fused_computation | loop fusion | flops 14680064 | bytes 29360128 | tf_op jit(solution)/shard_map/add | solution.py:614
  597.8 8.6 %collective-permute-done.24 = bf16[256,512]{1,0:T(8,128)(2,1)S(1)} collective-permute-done((bf16[256,512]{1,0:T(8,128)(2,1)S(1)}, bf16[256,512]{1,0:T(8,128)(2,1)S(1)}, u32[]{:S(2)}, u32[]{:S(2)}) %collective-permute-start.24) | collective-permute-done | bytes 262176 | tf_op jit(solution)/shard_map/ppermute | solution.py:607
  (214 shorter events, 174.1 us)
Async XLA Ops:
  7.2 71.9 %all-gather.4.cloned.1.call-start = ((), (), s32[]{:S(2)}) async-start(), calls=%async_computation.12 | async-start | bytes 2621440 | tf_op jit(solution)/shard_map/all_gather | solution.py:64
  12.9 69.3 %all-to-all-start = ((bf16[4,256,512]{2,1,0:T(8,128)(2,1)}), bf16[4,256,512]{2,1,0:T(8,128)(2,1)S(1)}, u32[]{:S(2)}, u32[]{:S(2)}) async-start(bf16[4,256,512]{2,1,0:T(8,128)(2,1)} %slice.183), calls=%async_computation | async-start | bytes 2097152 | tf_op jit(solution)/shard_map/all_to_all | solution.py:30
  19.2 143.7 %all-gather.6.cloned.1.call-start = ((), (), s32[]{:S(2)}) async-start(), calls=%async_computation.13 | async-start | bytes 9437184 | tf_op jit(solution)/shard_map/all_gather | solution.py:530
  82.3 152.0 %all-gather.8.cloned.1.call-start = ((), (), s32[]{:S(2)}) async-start(), calls=%async_computation.14 | async-start | bytes 9437184 | tf_op jit(solution)/shard_map/all_gather | solution.py:532
  159.0 28.9 %all-to-all-start.2 = ((bf16[4,1024,128]{2,1,0:T(8,128)(2,1)}), bf16[4,1024,128]{2,1,0:T(8,128)(2,1)S(1)}, u32[]{:S(2)}, u32[]{:S(2)}) async-start(bf16[4,1024,128]{2,1,0:T(8,128)(2,1)} %bitcast.1), calls=%async_computation.2 | async-start | bytes 2097152 | tf_op jit(solution)/shard_map/all_to_all | solution.py:30
  195.3 7.2 %collective-permute-start.1 = (f32[9,2048]{1,0:T(8,128)S(1)}, f32[9,2048]{1,0:T(8,128)S(1)}, u32[]{:S(2)}, u32[]{:S(2)}) collective-permute-start(f32[9,2048]{1,0:T(8,128)S(1)} %select_add_fusion.4), channel_id=1, source_target_pairs={{0,2},{1,3},{2,0},{3,1},{4,6},{5,7},{6,4},{7,5},{8,10},{9,11},{10,... | collective-permute-start | bytes 221192 | tf_op jit(solution)/shard_map/ppermute | solution.py:36
  202.7 52.7 %all-to-all-start.3 = ((bf16[4,1024,256]{2,1,0:T(8,128)(2,1)}), bf16[4,1024,256]{2,1,0:T(8,128)(2,1)S(1)}, u32[]{:S(2)}, u32[]{:S(2)}) async-start(bf16[4,1024,256]{2,1,0:T(8,128)(2,1)} %bitcast.2), calls=%async_computation.3 | async-start | bytes 4194304 | tf_op jit(solution)/shard_map/all_to_all | solution.py:30
  206.4 7.0 %collective-permute-start.3 = (f32[9,2048]{1,0:T(8,128)S(1)}, f32[9,2048]{1,0:T(8,128)S(1)}, u32[]{:S(2)}, u32[]{:S(2)}) collective-permute-start(f32[9,2048]{1,0:T(8,128)S(1)} %select_add_fusion.2), channel_id=1, source_target_pairs={{0,8},{4,12},{8,0},{12,4},{16,24},{20,28},{24,16},{28,20},{1,9},{5... | collective-permute-start | bytes 221192 | tf_op jit(solution)/shard_map/ppermute | solution.py:36
  213.6 5.4 collective-permute-start.4
  269.1 29.5 %all-to-all-start.4 = ((bf16[4,1024,128]{2,1,0:T(8,128)(2,1)}), bf16[4,1024,128]{2,1,0:T(8,128)(2,1)S(1)}, u32[]{:S(2)}, u32[]{:S(2)}) async-start(bf16[4,1024,128]{2,1,0:T(8,128)(2,1)} %bitcast.3), calls=%async_computation.4 | async-start | bytes 2097152 | tf_op jit(solution)/shard_map/all_to_all | solution.py:30
  299.6 28.8 %all-to-all-start.5 = ((bf16[4,1024,128]{2,1,0:T(8,128)(2,1)}), bf16[4,1024,128]{2,1,0:T(8,128)(2,1)S(1)}, u32[]{:S(2)}, u32[]{:S(2)}) async-start(bf16[4,1024,128]{2,1,0:T(8,128)(2,1)} %bitcast.100), calls=%async_computation.5 | async-start | bytes 2097152 | tf_op jit(solution)/shard_map/all_to_all | solution.py:30
  337.2 49.0 %all-to-all-start.6 = ((bf16[4,1024,256]{2,1,0:T(8,128)(2,1)}), bf16[4,1024,256]{2,1,0:T(8,128)(2,1)S(1)}, u32[]{:S(2)}, u32[]{:S(2)}) async-start(bf16[4,1024,256]{2,1,0:T(8,128)(2,1)} %bitcast.99), calls=%async_computation.6 | async-start | bytes 4194304 | tf_op jit(solution)/shard_map/all_to_all | solution.py:30
  340.8 132.3 %reduce-scatter.3.cloned.1.call-start = ((), (), s32[]{:S(2)}) async-start(), calls=%async_computation.15 | async-start | bytes 9437184 | tf_op jit(solution)/shard_map/reduce_scatter | solution.py:577
  412.9 27.2 %all-to-all-start.7 = ((bf16[4,1024,128]{2,1,0:T(8,128)(2,1)}), bf16[4,1024,128]{2,1,0:T(8,128)(2,1)S(1)}, u32[]{:S(2)}, u32[]{:S(2)}) async-start(bf16[4,1024,128]{2,1,0:T(8,128)(2,1)} %bitcast.27), calls=%async_computation.7 | async-start | bytes 2097152 | tf_op jit(solution)/shard_map/all_to_all | solution.py:30
  440.1 33.0 %all-to-all-start.8 = ((bf16[4,256,512]{2,1,0:T(8,128)(2,1)}), bf16[4,256,512]{2,1,0:T(8,128)(2,1)S(1)}, u32[]{:S(2)}, u32[]{:S(2)}) async-start(bf16[4,256,512]{2,1,0:T(8,128)(2,1)} %get-tuple-element.130), calls=%async_computation.8 | async-start | bytes 2097152 | tf_op jit(solution)/shard_map/all_to_all | solution.py:30
  443.6 135.2 %reduce-scatter.5.cloned.1.call-start = ((), (), s32[]{:S(2)}) async-start(), calls=%async_computation.16 | async-start | bytes 9437184 | tf_op jit(solution)/shard_map/reduce_scatter | solution.py:595
  474.1 98.4 %all-to-all-start.9 = ((bf16[4,768,512]{2,1,0:T(8,128)(2,1)}), bf16[4,768,512]{2,1,0:T(8,128)(2,1)}, u32[]{:S(2)}, u32[]{:S(2)}) async-start(bf16[4,768,512]{2,1,0:T(8,128)(2,1)} %get-tuple-element.139), calls=%async_computation.10 | async-start | bytes 6291456 | tf_op jit(solution)/shard_map/all_to_all | solution.py:30
  494.1 47.0 %collective-permute-start.30 = (bf16[256,512]{1,0:T(8,128)(2,1)S(1)}, bf16[256,512]{1,0:T(8,128)(2,1)S(1)}, u32[]{:S(2)}, u32[]{:S(2)}) collective-permute-start(bf16[256,512]{1,0:T(8,128)(2,1)S(1)} %bitcast.108), channel_id=1, source_target_pairs={{0,3},{1,2},{2,1},{3,0},{4,7},{5,6},{6,5},{7,4},{8,11},{9,10},{10,... | collective-permute-start | bytes 786440 | tf_op jit(solution)/shard_map/ppermute | solution.py:607
  498.0 44.5 %collective-permute-start.28 = (bf16[256,512]{1,0:T(8,128)(2,1)S(1)}, bf16[256,512]{1,0:T(8,128)(2,1)S(1)}, u32[]{:S(2)}, u32[]{:S(2)}) collective-permute-start(bf16[256,512]{1,0:T(8,128)(2,1)S(1)} %bitcast.107), channel_id=1, source_target_pairs={{0,1},{1,0},{2,3},{3,2},{4,5},{5,4},{6,7},{7,6},{8,9},{9,8},{10,11... | collective-permute-start | bytes 786440 | tf_op jit(solution)/shard_map/ppermute | solution.py:607
  498.0 73.6 %collective-permute-start.29 = (bf16[256,512]{1,0:T(8,128)(2,1)S(1)}, bf16[256,512]{1,0:T(8,128)(2,1)S(1)}, u32[]{:S(2)}, u32[]{:S(2)}) collective-permute-start(bf16[256,512]{1,0:T(8,128)(2,1)S(1)} %bitcast.105), channel_id=1, source_target_pairs={{0,2},{1,3},{2,0},{3,1},{4,6},{5,7},{6,4},{7,5},{8,10},{9,11},{10,... | collective-permute-start | bytes 786440 | tf_op jit(solution)/shard_map/ppermute | solution.py:607
  576.7 19.6 %collective-permute-start.27 = (f32[1,2048]{1,0:T(1,128)S(1)}, f32[1,2048]{1,0:T(1,128)S(1)}, u32[]{:S(2)}, u32[]{:S(2)}) collective-permute-start(f32[1,2048]{1,0:T(1,128)S(1)} %add.249), channel_id=1, source_target_pairs={{0,2},{1,3},{2,0},{3,1},{4,6},{5,7},{6,4},{7,5},{8,10},{9,11},{10,... | collective-permute-start | bytes 24584 | tf_op jit(solution)/shard_map/ppermute | solution.py:36
  583.0 13.4 %collective-permute-start.25 = (bf16[256,512]{1,0:T(8,128)(2,1)S(1)}, bf16[256,512]{1,0:T(8,128)(2,1)S(1)}, u32[]{:S(2)}, u32[]{:S(2)}) collective-permute-start(bf16[256,512]{1,0:T(8,128)(2,1)S(1)} %bitcast.106), channel_id=1, source_target_pairs={{0,3},{1,2},{2,1},{3,0},{4,7},{5,6},{6,5},{7,4},{8,11},{9,10},{10,... | collective-permute-start | bytes 786440 | tf_op jit(solution)/shard_map/ppermute | solution.py:607
  585.4 12.4 %collective-permute-start.23 = (bf16[256,512]{1,0:T(8,128)(2,1)S(1)}, bf16[256,512]{1,0:T(8,128)(2,1)S(1)}, u32[]{:S(2)}, u32[]{:S(2)}) collective-permute-start(bf16[256,512]{1,0:T(8,128)(2,1)S(1)} %bitcast.104), channel_id=1, source_target_pairs={{0,1},{1,0},{2,3},{3,2},{4,5},{5,4},{6,7},{7,6},{8,9},{9,8},{10,11... | collective-permute-start | bytes 786440 | tf_op jit(solution)/shard_map/ppermute | solution.py:607
  585.4 20.9 %collective-permute-start.24 = (bf16[256,512]{1,0:T(8,128)(2,1)S(1)}, bf16[256,512]{1,0:T(8,128)(2,1)S(1)}, u32[]{:S(2)}, u32[]{:S(2)}) collective-permute-start(bf16[256,512]{1,0:T(8,128)(2,1)S(1)} %bitcast.103), channel_id=1, source_target_pairs={{0,2},{1,3},{2,0},{3,1},{4,6},{5,7},{6,4},{7,5},{8,10},{9,11},{10,... | collective-permute-start | bytes 786440 | tf_op jit(solution)/shard_map/ppermute | solution.py:607
  (45 other events, 887.3 us)
Sparse Core Ops, SparseCore 0:
  10.7 68.2 all-gather.3
  82.3 53.5 all-gather.5
  159.1 54.3 all-gather.7
  386.4 70.0 reduce-scatter.2
  473.3 71.9 reduce-scatter.4

commit v2 on v1

--- a/solution.py
+++ b/solution.py
@@ -1,4 +1,5 @@
 import functools
+import math
 
 import jax
 import jax.numpy as jnp
@@ -31,28 +32,38 @@
 
 
 def merge_all(value, merge, axis, size):
-    k = 1
-    while k < size:
-        other = lax.ppermute(value, axis, [(i, i ^ k) for i in range(size)])
-        value = merge(value, other)
-        k *= 2
+    k = size
+    while k > 1:
+        if k % 4 == 0:
+            k //= 4
+            turns = (k, 2 * k, 3 * k)
+        else:
+            k //= 2
+            turns = (k,)
+        others = [lax.ppermute(value, axis, [(i, i ^ t) for i in range(size)]) for t in turns]
+        value = merge([value, *others])
     return value
 
 
-def add(a, b):
-    return a + b
+def add(values):
+    while len(values) > 1:
+        values = [a + b for a, b in zip(values[::2], values[1::2], strict=True)]
+    return values[0]
 
 
 def merge_moments(frames):
     count = [frames]
 
-    def merge(a, b):
-        row = lax.broadcasted_iota(jnp.int32, a.shape, 0)
-        scale = jnp.where((row == 0) | (row == 2), 0.5, 1.0)
-        gap = a[0:1] - b[0:1]
-        squares = gap * gap * (count[0] / 2)
-        count[0] *= 2
-        return (a + b) * scale + jnp.where(row == 1, squares, 0.0)
+    def merge(values):
+        summed = add(values)
+        row = lax.broadcasted_iota(jnp.int32, summed.shape, 0)
+        part = 1 / len(values)
+        mean = summed[0:1] * part
+        gaps = [v[0:1] - mean for v in values]
+        squares = add([gap * gap for gap in gaps]) * count[0]
+        count[0] *= len(values)
+        scale = jnp.where((row == 0) | (row == 2), part, 1.0)
+        return summed * scale + jnp.where(row == 1, squares, 0.0)
 
     return merge
 
@@ -61,14 +72,14 @@
     rows = weights[0].shape[0] // wide
     first = lax.axis_index("wide") * rows
     shares = [lax.dynamic_slice_in_dim(weight, first, rows, 0) for weight in weights]
-    both = lax.all_gather(jnp.concatenate(shares, 0), "narrow", axis=1, tiled=True)
-    return [both[i * rows : (i + 1) * rows] for i in range(len(weights))]
+    return lax.all_gather(jnp.stack(shares), "narrow", axis=1)
 
 
 def project_kernel(groups, x_refs, w_ref, z_ref, moments_ref, joined_ref=None):
     frames, cols = z_ref.shape
     here = pl.program_id(0)
-    step = min(256, frames)
+    step = math.gcd(256, *[x_ref.shape[1] for x_ref in x_refs])
+    weight = w_ref[...].reshape(-1, cols)
     sums = jnp.zeros((1, cols), jnp.float32)
     for m in range(0, frames, step):
         acc = None
@@ -78,7 +89,7 @@
             x_ref = x_refs[ref]
             block, first, depth = feature
             x = x_ref[block, m - lo : m - lo + step, :]
-            term = jnp.dot(x, w_ref[first : first + depth, :], preferred_element_type=jnp.float32)
+            term = jnp.dot(x, weight[first : first + depth, :], preferred_element_type=jnp.float32)
             acc = term if acc is None else acc + term
         rounded = acc.astype(jnp.bfloat16)
         z_ref[m : m + step, :] = rounded
@@ -110,10 +121,9 @@
 def project(pieces, weight):
     blocks, _, depth = pieces[0].shape
     frames = sum(p.shape[1] for p in pieces)
-    rows, cols = weight.shape
+    row_blocks, steps, span, width = weight.shape
+    rows, cols = row_blocks * span, steps * width
     joined = blocks > 1
-    steps = blocks if joined else 4
-    width = cols // steps
     groups = []
     lo = 0
     for i, p in enumerate(pieces):
@@ -135,7 +145,7 @@
         kernel,
         grid=(steps,),
         in_specs=[whole(p.shape) for p in pieces]
-        + [pl.BlockSpec((rows, width), lambda i: (0, i))],
+        + [pl.BlockSpec((row_blocks, 1, span, width), lambda i: (0, i, 0, 0))],
         out_specs=out_specs,
         out_shape=out_shape,
         compiler_params=params_of(),
@@ -185,8 +195,8 @@
                 )
                 running[r] = fresh
                 s_ref[r, pl.ds(pl.multiple_of((c * SUB + k) * tiles, tiles), tiles), :] = fresh
-        for r in range(rows):
-            for (lo, hi), h_ref in zip(ranges, h_refs, strict=True):
+        for (lo, hi, first_row, count), h_ref in zip(ranges, h_refs, strict=True):
+            for r in range(first_row, first_row + count):
                 per_block = tiles // h_ref.shape[0]
                 for q in range(h_ref.shape[0]):
                     for j in range(lo, hi):
@@ -201,7 +211,7 @@
                         ]
                         h_ref[
                             q,
-                            r,
+                            r - first_row,
                             pl.ds(pl.multiple_of(c * SUB, SUB), SUB),
                             (j - lo) * LANES : (j - lo + 1) * LANES,
                         ] = jnp.concatenate(halves, 0).astype(jnp.bfloat16)
@@ -227,13 +237,13 @@
         ],
         out_specs=[pl.BlockSpec((rows, CHUNK * tiles, LANES), lambda i: (0, i, 0))]
         + [
-            pl.BlockSpec((blocks, rows, CHUNK, (hi - lo) * LANES), lambda i: (0, 0, i, 0))
-            for lo, hi in ranges
+            pl.BlockSpec((blocks, count, CHUNK, (hi - lo) * LANES), lambda i: (0, 0, i, 0))
+            for lo, hi, _, count in ranges
         ],
         out_shape=[jax.ShapeDtypeStruct((rows, length * tiles, LANES), jnp.float32)]
         + [
-            jax.ShapeDtypeStruct((blocks, rows, length, (hi - lo) * LANES), jnp.bfloat16)
-            for lo, hi in ranges
+            jax.ShapeDtypeStruct((blocks, count, length, (hi - lo) * LANES), jnp.bfloat16)
+            for lo, hi, _, count in ranges
         ],
         scratch_shapes=[
             pltpu.VMEM((4, tiles, LANES), jnp.float32),
@@ -244,7 +254,7 @@
         cost_estimate=BRIEF,
         name="forward",
     )(keep, moments, gains, z.reshape(rows, length, width))
-    return results[0], [h.reshape(blocks, rows * length, -1) for h in results[1:]]
+    return results[0], [h.reshape(blocks, h.shape[1] * length, -1) for h in results[1:]]
 
 
 def backward_kernel(ranges, keep, moments, gains, s_ref, before_ref, z_ref, *refs):
@@ -386,60 +396,94 @@
     return dpre.reshape(rows * length, width), sums[0:3]
 
 
-def dproject_kernel(total_frames, moments, gains, sums, dpre_ref, z_ref, w_ref, dz_ref, level_ref, da_ref):
-    rstd = lax.rsqrt(moments[1:2, :] / total_frames + EPSILON)
-    scale = gains[0:1, :] * rstd
-    level = sums[0:1, :] / total_frames
-    slope = sums[1:2, :] * (rstd * rstd) / total_frames
-    gap = z_ref[...].astype(jnp.float32) - moments[0:1, :]
-    dz = (scale * (dpre_ref[...] - level - gap * slope)).astype(jnp.bfloat16)
-    dz_ref[...] = dz
-    here = jnp.sum(dz.astype(jnp.float32), 0, keepdims=True)
-
-    @pl.when(pl.program_id(0) == 0)
+def dproject_kernel(total_frames, moments, gains, sums, dpre_ref, z_ref, w_ref, *refs):
+    dz_ref, level_ref, da_ref, dz_held, weight, arrived = refs
+    here = pl.program_id(0)
+    last = pl.num_programs(0) - 1
+    width = dpre_ref.shape[1]
+    slot = lax.rem(here, 2)
+
+    def fetch(j):
+        cols = w_ref.shape[3]
+        return pltpu.make_async_copy(
+            w_ref.at[:, j], weight.at[:, :, pl.ds(j * cols, cols)], arrived.at[j]
+        )
+
+    def differentiate():
+        rstd = lax.rsqrt(moments[1:2, :] / total_frames + EPSILON)
+        scale = gains[0:1, :] * rstd
+        level = sums[0:1, :] / total_frames
+        slope = sums[1:2, :] * (rstd * rstd) / total_frames
+        gap = z_ref[...].astype(jnp.float32) - moments[0:1, :]
+        dz = (scale * (dpre_ref[...] - level - gap * slope)).astype(jnp.bfloat16)
+        dz_ref[...] = dz
+        dz_held[slot] = dz
+        level_ref[...] += jnp.sum(dz.astype(jnp.float32), 0, keepdims=True)
+
+    def multiply(da_ref):
+        parts = da_ref.shape[0]
+        whole_weight = weight[...].reshape(-1, width)
+        depth = whole_weight.shape[0] // parts
+        for p in range(parts):
+            da_ref[p] = lax.dot_general(
+                dz_held[1 - slot],
+                whole_weight[p * depth : (p + 1) * depth, :],
+                (((1,), (1,)), ((), ())),
+                preferred_element_type=jnp.float32,
+            ).astype(jnp.bfloat16)
+
+    @pl.when(here == 0)
     def _():
-        level_ref[...] = here
-
-    @pl.when(pl.program_id(0) > 0)
+        for j in range(w_ref.shape[1]):
+            fetch(j).start()
+        level_ref[...] = jnp.zeros_like(level_ref)
+        differentiate()
+        for j in range(w_ref.shape[1]):
+            fetch(j).wait()
+
+    @pl.when((here > 0) & (here < last))
     def _():
-        level_ref[...] += here
-
-    parts = da_ref.shape[0]
-    depth = w_ref.shape[0] // parts
-    for p in range(parts):
-        da_ref[p] = lax.dot_general(
-            dz_ref[...],
-            w_ref[p * depth : (p + 1) * depth, :],
-            (((1,), (1,)), ((), ())),
-            preferred_element_type=jnp.float32,
-        ).astype(jnp.bfloat16)
+        multiply(da_ref)
+        differentiate()
+
+    @pl.when(here == last)
+    def _():
+        multiply(da_ref)
 
 
 def dproject(dpre, z, moments, gains, sums, weight, parts, total_frames, lo, hi):
-    width = z.shape[1]
-    rows = weight.shape[0]
-    step = min(256, hi - lo)
-    frames = hi - lo
+    frames, width = hi - lo, z.shape[1]
+    row_blocks, col_blocks, span, cols = weight.shape
+    rows = row_blocks * span
+    step = math.gcd(frames, 256)
+    steps = frames // step
     return pl.pallas_call(
         functools.partial(dproject_kernel, total_frames),
-        grid=(frames // step,),
+        grid=(steps + 1,),
         in_specs=[
             whole((3, width)),
             whole((3, width)),
             whole((3, width)),
-            pl.BlockSpec((step, width), lambda i: (i + lo // step, 0)),
-            pl.BlockSpec((step, width), lambda i: (i + lo // step, 0)),
-            whole((rows, width)),
+            pl.BlockSpec((step, width), lambda i: (jnp.minimum(i, steps - 1) + lo // step, 0)),
+            pl.BlockSpec((step, width), lambda i: (jnp.minimum(i, steps - 1) + lo // step, 0)),
+            pl.BlockSpec(memory_space=pl.ANY),
         ],
         out_specs=[
-            pl.BlockSpec((step, width), lambda i: (i, 0)),
+            pl.BlockSpec((step, width), lambda i: (jnp.minimum(i, steps - 1), 0)),
             whole((1, width)),
-            pl.BlockSpec((parts, step, rows // parts), lambda i: (0, i, 0)),
+            pl.BlockSpec(
+                (parts, step, rows // parts), lambda i: (0, jnp.maximum(i - 1, 0), 0)
+            ),
         ],
         out_shape=[
             jax.ShapeDtypeStruct((frames, width), jnp.bfloat16),
             jax.ShapeDtypeStruct((1, width), jnp.float32),
             jax.ShapeDtypeStruct((parts, frames, rows // parts), jnp.bfloat16),
+        ],
+        scratch_shapes=[
+            pltpu.VMEM((2, step, width), jnp.bfloat16),
+            pltpu.VMEM((row_blocks, span, width), jnp.bfloat16),
+            pltpu.SemaphoreType.DMA((col_blocks,)),
         ],
         compiler_params=params_of(),
         cost_estimate=BRIEF,
@@ -469,7 +513,7 @@
 def weight_terms(source, center, dz, levels):
     frames, rows = source.shape
     cols = dz[0].shape[1]
-    tile = 256
+    tile = 512
     return pl.pallas_call(
         functools.partial(weight_kernel, len(dz)),
         grid=(rows // tile,),
@@ -514,7 +558,8 @@
     spread = lax.dynamic_update_slice_in_dim(spread, own, (n * wide + w) * each, 1)
 
     groups_in = [(0, tiles // 4), (tiles // 4, 3 * tiles // 4), (3 * tiles // 4, tiles)]
-    groups_out = groups_in
+    groups_out = [(lo, hi, 0, rows) for lo, hi in groups_in[:2]]
+    groups_out += [(*groups_in[2], 0, rows // 2), (*groups_in[2], rows // 2, rows // 2)]
 
     held = [
         cotangent[:, lo * LANES : hi * LANES].reshape(narrow, frames, -1) for lo, hi in groups_in
@@ -524,27 +569,27 @@
     blocks = inputs.reshape(narrow, frames, part)
     early, late = blocks[:, :split], blocks[:, split:]
     early = swap(early)
-    share_one, share_two = gather_rows([w_one, w_two], wide)
-    share_one, share_two, early, late, held = tie((share_one, share_two, early, late, held))
+    shares = gather_rows([w_one, w_two], wide)
+    shares, early, late, held, spread = tie((shares, early, late, held, spread))
     late = swap(late)
-    full_one = lax.all_gather(share_one, "wide", axis=0, tiled=True)
-    late, held, share_two = tie((late, held, share_two))
-    full_two = lax.all_gather(share_two, "wide", axis=0, tiled=True)
+    gains = along(across(spread, add), add)
+    share_one, share_two = shares[0], shares[1]
+    full_one = lax.all_gather(share_one, "wide", axis=0)
+    late, held, share_two, gains = tie((late, held, share_two, gains))
+    gains_one, gains_two = gains[:3], gains[3:]
+    full_two = lax.all_gather(share_two, "wide", axis=0)
     group = swap(held[0])
     z_one, moments, source = project([early, late], full_one)
     moments, group = tie((moments, group))
     grads = [group]
-    moments = jnp.concatenate([moments, spread])
     merge = merge_moments(frames)
     moments = along(moments, merge)
     moments, held = tie((moments, held))
     group = swap(held[1])
     moments_one = across(moments, merge)
-    gains_one, gains_two = moments_one[3:6], moments_one[6:9]
-    moments_one = moments_one[:3]
     every = [(0, z_one.shape[1] // LANES)]
     states_one, (h_one,) = forward(
-        z_one, moments_one, gains_one, keep, 1, every, total_frames
+        z_one, moments_one, gains_one, keep, 1, [(*every[0], 0, rows)], total_frames
     )
     z_two, moments = project([h_one], full_two)
     moments, group = tie((moments, group))
@@ -575,45 +620,58 @@
     terms_two, dh_one, group = tie((terms_two, dh_one, group))
     second.append(group)
     plane_two = lax.psum_scatter(terms_two, "wide", scatter_dimension=0, tiled=True)
+    group = swap(h_two[2])
     dpre, sums = backward([dh_one], every, states_one, z_one, moments_one, gains_one, keep)
+    sums, group = tie((sums, group))
+    thirds = [group]
     sums = along(jnp.concatenate([sums, level_two], 0), add)
     sums, h_two = tie((sums, h_two))
-    group = swap(h_two[2])
+    group = swap(h_two[3])
     sums_one = across(sums, add)
     level_two = sums_one[3:, :]
     sums_one = sums_one[:3]
     back = functools.partial(
         dproject, dpre, z_one, moments_one, gains_one, sums_one, full_one, narrow, total_frames
     )
+    split = frames // 2
     dz_early, level_early, da_early = back(0, split)
     da_early, group = tie((da_early, group))
-    second.append(group)
+    thirds.append(group)
+    second.append(jnp.concatenate(thirds, 1))
     da_early = swap(da_early)
     dz_late, level_late, da_late = back(split, frames)
     terms_one = weight_terms(source, center_one, [dz_early, dz_late], [level_early, level_late])
     da_early, da_late, terms_one, plane_two = tie((da_early, da_late, terms_one, plane_two))
     plane_one = lax.psum_scatter(terms_one, "wide", scatter_dimension=0, tiled=True)
     da_late = swap(da_late)
-    level_one = across(level_early + level_late, add)
+    level_one = level_early + level_late
+    level_one = across(level_one, add)
 
     whole_two = jnp.concatenate(second, axis=2).reshape(inputs.shape).astype(jnp.float32)
     output = (inputs.astype(jnp.float32) + whole_two).astype(jnp.bfloat16)
 
-    def summed(plane):
-        blocks = plane.reshape(plane.shape[0], narrow, part)
-        weight = lax.dynamic_index_in_dim(blocks, n, 1, keepdims=False).astype(jnp.float32)
-        for k in range(1, narrow):
-            block = lax.dynamic_index_in_dim(blocks, n ^ k, 1, keepdims=False)
-            weight += lax.ppermute(block, "narrow", [(i, i ^ k) for i in range(narrow)])
-        return weight
-
     span = plane_one.shape[0]
-    dw_two = summed(plane_two)
+    blocks = plane_two.reshape(span, narrow, part)
+    mine = lax.dynamic_index_in_dim(blocks, n, 1, keepdims=False)
+    others = [
+        lax.ppermute(
+            lax.dynamic_index_in_dim(blocks, n ^ k, 1, keepdims=False),
+            "narrow",
+            [(i, i ^ k) for i in range(narrow)],
+        )
+        for k in range(1, narrow)
+    ]
     level_one, da_late = tie((level_one, da_late))
     arrived = jnp.concatenate([da_early, da_late], axis=1).reshape(inputs.shape)
     grad_inputs = cotangent.astype(jnp.float32) + arrived.astype(jnp.float32)
-    level_one = along(level_one, add)
-    dw_one = summed(plane_one)
+    blocks = swap(plane_one.reshape(span, narrow, part).transpose(1, 0, 2))
+    for k in (1, 2):
+        level_one = level_one + lax.ppermute(
+            level_one, "narrow", [(i, i ^ k) for i in range(narrow)]
+        )
+    mine, others, blocks = tie((mine, others, blocks))
+    dw_two = mine.astype(jnp.float32) + sum(other.astype(jnp.float32) for other in others)
+    dw_one = jnp.sum(blocks.astype(jnp.float32), 0)
 
     def restored(weight, center, level):
         rows_of = lax.dynamic_slice_in_dim(center, w * span, span, 1).reshape(span, 1)

time: 616 us -> 610 us (level); the launches traced: 614 us -> 600 us
  blocking collectives: 76.6 us -> 0 us
  starting transfers between devices: 62 us -> 104 us
  waiting for transfers between devices: 242 us -> 267 us
    all_to_all x9 -> x12, waiting for transfers between devices: 38.7 us -> 142 us  [swap(): return lax.all_to_all(blocks, 'narrow', split_axis=0, concat_axis=0)]
    all_to_all x1 -> x0, blocking collectives: 76.6 us -> none  [swap(): return lax.all_to_all(blocks, 'narrow', split_axis=0, concat_axis=0)]
    all_gather x3, waiting for transfers between devices: 52.8 us -> 8.81 us  [the longest x1 8.81 us: gather_rows(): return lax.all_gather(jnp.stack(shares), 'narrow', axis=1)]
    ppermute x31 -> x44, waiting for transfers between devices: 150 us -> 115 us  [the longest x39 99.5 us: merge_all(): lax.ppermute(value, axis, [(i, i ^ t) for i in range(size)])]
    ppermute x31 -> x44, starting transfers between devices: 25.3 us -> 51.4 us  [the longest x39 43.8 us: merge_all(): lax.ppermute(value, axis, [(i, i ^ t) for i in range(size)])]
    all_to_all x9 -> x12, starting transfers between devices: 36.3 us -> 51.8 us  [swap(): return lax.all_to_all(blocks, 'narrow', split_axis=0, concat_axis=0)]
  transfers between devices with their start and end apart: 45 -> 61, of which waited for: 33 -> 39; matrix products, arithmetic and copies ran while one was open for 8% -> 7% of each run, Pallas kernels for 26% -> 27%
where the time goes in v2:
time: 610 us; the launch traced here: 600 us
  waiting for transfers between devices  267 us (44%)
  Pallas kernels  160 us (26%)
  starting transfers between devices  104 us (17%)
  local copies, waits for them, and re-layouts  30.3 us (5%)
  other arithmetic  24.3 us (4%)
  between operations  14.7 us (2%)
    all_to_all x12, waiting for transfers between devices, swap(): return lax.all_to_all(blocks, 'narrow', split_axis=0, concat_axis=0)  142 us
    ppermute x39, waiting for transfers between devices, merge_all(): lax.ppermute(value, axis, [(i, i ^ t) for i in range(size)])  99.5 us
    all_to_all x12, starting transfers between devices, swap(): return lax.all_to_all(blocks, 'narrow', split_axis=0, concat_axis=0)  51.8 us
    ppermute x39, starting transfers between devices, merge_all(): lax.ppermute(value, axis, [(i, i ^ t) for i in range(size)])  43.8 us
    pallas_call x3, Pallas kernels, dproject(): pl.pallas_call(functools.partial(dproject_kernel, total_frames), grid=(st...  41.3 us
    pallas_call x2, Pallas kernels, project(): pl.pallas_call(kernel, grid=(steps,), in_specs=[whole(p.shape) for p in p...  31.2 us
    pallas_call x2, Pallas kernels, backward(): pl.pallas_call(functools.partial(backward_kernel, ranges), grid=(length /...  31.2 us
    pallas_call x2, Pallas kernels, forward(): pl.pallas_call(functools.partial(forward_kernel, total_frames, ranges), g...  29.4 us
  transfers between devices with their start and end apart: 61, of which 39 were waited for; matrix products, arithmetic and copies ran while one was open for 7% of the time, Pallas kernels for 27%

profile of v2, /device:TPU:0, one launch (start us, length us, event | category | flops | bytes accessed | tf_op | source)
XLA Modules:
  0.0 600.3 jit_solution(11418965733302696152)
XLA Ops:
  11.4 6.3 %all-to-all-start = ((bf16[4,256,512]{2,1,0:T(8,128)(2,1)}), bf16[4,256,512]{2,1,0:T(8,128)(2,1)S(1)}, u32[]{:S(2)}, u32[]{:S(2)}) async-start(bf16[4,256,512]{2,1,0:T(8,128)(2,1)} %slice.199), calls=%async_computation | async-start | bytes 2097152 | tf_op jit(solution)/shard_map/all_to_all | solution.py:31
  26.7 42.2 %all-to-all-done.refs_0_ = bf16[4,256,512]{2,1,0:T(8,128)(2,1)S(1)} async-done(((bf16[4,256,512]{2,1,0:T(8,128)(2,1)}), bf16[4,256,512]{2,1,0:T(8,128)(2,1)S(1)}, u32[]{:S(2)}, u32[]{:S(2)}) %all-to-all-start) | async-done | bytes 1048608 | tf_op jit(solution)/shard_map/all_to_all | solution.py:31
  68.9 8.8 %all-gather.8.cloned.1.call-done = bf16[2,1024,512]{2,1,0:T(8,128)(2,1)} async-done(((bf16[2,256,512]{2,1,0:T(8,128)(2,1)}), bf16[2,1024,512]{2,1,0:T(8,128)(2,1)}) %all-gather.8.cloned.1.call-update) | async-done | bytes 2097168 | tf_op jit(solution)/shard_map/all_gather | solution.py:75
  99.6 38.1 %collective-permute-done.4 = f32[6,2048]{1,0:T(8,128)S(1)} collective-permute-done((f32[6,2048]{1,0:T(8,128)S(1)}, f32[6,2048]{1,0:T(8,128)S(1)}, u32[]{:S(2)}, u32[]{:S(2)}) %collective-permute-start.4) | collective-permute-done | bytes 49184 | tf_op jit(solution)/shard_map/ppermute | solution.py:43
  137.7 22.8 %collective-permute-done.5 = f32[6,2048]{1,0:T(8,128)S(1)} collective-permute-done((f32[6,2048]{1,0:T(8,128)S(1)}, f32[6,2048]{1,0:T(8,128)S(1)}, u32[]{:S(2)}, u32[]{:S(2)}) %collective-permute-start.5) | collective-permute-done | bytes 49184 | tf_op jit(solution)/shard_map/ppermute | solution.py:43
  165.6 16.1 %project.2 = (bf16[1024,2048]{1,0:T(8,128)(2,1)}, f32[3,2048]{1,0:T(4,128)}, bf16[1024,2048]{1,0:T(8,128)(2,1)}) custom-call(bf16[4,256,512]{2,1,0:T(8,128)(2,1)} %copy-done.5, bf16[4,768,512]{2,1,0:T(8,128)(2,1)} %copy-done.3, bf16[8,4,256,512]{3,2,1,0:T(8,128)(2,1)} %all-gather.6.cloned.1.call-done.refs_2_.w_ref), custom_call_target="tpu_custom_call" | custom-call | flops 1 | bytes 1 | tf_op jit(solution)/shard_map/project/pallas_call | solution.py:144
  181.7 7.9 %all-to-all-done.2 = bf16[4,1024,128]{2,1,0:T(8,128)(2,1)} async-done(((bf16[4,1024,128]{2,1,0:T(8,128)(2,1)}), bf16[4,1024,128]{2,1,0:T(8,128)(2,1)}, u32[]{:S(2)}, u32[]{:S(2)}) %all-to-all-start.2) | async-done | bytes 1048608 | tf_op jit(solution)/shard_map/all_to_all | solution.py:31
  209.9 14.5 %forward.2 = (f32[2,8192,128]{2,1,0:T(8,128)}, bf16[1,2,512,2048]{3,2,1,0:T(8,128)(2,1)}) custom-call(f32[2,512]{1,0:T(2,128)} %convert_element_type.43.keep, f32[3,2048]{1,0:T(4,128)} %select_add_fusion.3.moments, f32[3,2048]{1,0:T(4,128)} %get-tuple-element.175.gains, bf16[2,512,2048]{2,1,0:T(8,128)(2,1)} %bitcast.80), custom_call_target="tpu_custom_call" | custom-call | flops 1 | bytes 1 | tf_op jit(solution)/shard_map/forward/pallas_call | solution.py:229
  224.4 15.1 %project.3 = (bf16[1024,2048]{1,0:T(8,128)(2,1)}, f32[3,2048]{1,0:T(4,128)}) custom-call(bf16[1,1024,2048]{2,1,0:T(8,128)(2,1)} %bitcast.88, bf16[8,4,256,512]{3,2,1,0:T(8,128)(2,1)} %bitcast.86), custom_call_target="tpu_custom_call" | custom-call | flops 1 | bytes 1 | tf_op jit(solution)/shard_map/project/pallas_call | solution.py:144
  239.5 12.6 %all-to-all-done.3 = bf16[4,1024,256]{2,1,0:T(8,128)(2,1)S(1)} async-done(((bf16[4,1024,256]{2,1,0:T(8,128)(2,1)}), bf16[4,1024,256]{2,1,0:T(8,128)(2,1)S(1)}, u32[]{:S(2)}, u32[]{:S(2)}) %all-to-all-start.3) | async-done | bytes 2097184 | tf_op jit(solution)/shard_map/all_to_all | solution.py:31
  271.7 14.9 %forward.3 = (f32[2,8192,128]{2,1,0:T(8,128)}, bf16[4,2,512,128]{3,2,1,0:T(8,128)(2,1)}, bf16[4,2,512,256]{3,2,1,0:T(8,128)(2,1)}, bf16[4,1,512,128]{3,2,1,0:T(8,128)(2,1)}, bf16[4,1,512,128]{3,2,1,0:T(8,128)(2,1)}) custom-call(f32[2,512]{1,0:T(2,128)} %convert_element_type.43.keep, f32[3,2048]{1,0:T(4,128)} %select_add_fusion.moments, ...), custom_call_target="tpu_custom_call" | custom-call | flops 1 | bytes 1 | tf_op jit(solution)/shard_map/forward/pallas_call | solution.py:229
  296.0 14.9 %backward.2 = (f32[2,512,2048]{2,1,0:T(8,128)}, f32[16,2048]{1,0:T(8,128)}) custom-call(f32[2,512]{1,0:T(2,128)} %convert_element_type.43.keep, f32[3,2048]{1,0:T(4,128)} %select_add_fusion.moments, f32[3,2048]{1,0:T(4,128)} %get-tuple-element.174.gains, f32[2,8192,128]{2,1,0:T(8,128)} %get-tuple-element.112.s_ref.before_ref, ...), custom_call_target="tpu_custom_call" | custom-call | flops 1 | bytes 1 | tf_op jit(solution)/shard_map/backward/pallas_call | solution.py:353
  311.7 8.7 %all-to-all-done.5 = bf16[4,1024,128]{2,1,0:T(8,128)(2,1)S(1)} async-done(((bf16[4,1024,128]{2,1,0:T(8,128)(2,1)}), bf16[4,1024,128]{2,1,0:T(8,128)(2,1)S(1)}, u32[]{:S(2)}, u32[]{:S(2)}) %all-to-all-start.5) | async-done | bytes 1048608 | tf_op jit(solution)/shard_map/all_to_all | solution.py:31
  342.2 17.2 %dproject.3 = (bf16[1024,2048]{1,0:T(8,128)(2,1)}, f32[1,2048]{1,0:T(1,128)}, bf16[1,1024,2048]{2,1,0:T(8,128)(2,1)}) custom-call(f32[3,2048]{1,0:T(4,128)} %select_add_fusion.moments, f32[3,2048]{1,0:T(4,128)} %get-tuple-element.174.gains, f32[3,2048]{1,0:T(4,128)} %add.318.sums, f32[1024,2048]{1,0:T(8,128)} %bitcast.92, ...), custom_call_target="tpu_custom_call" | custom-call | flops 1 | bytes 1 | tf_op jit(solution)/shard_map/dproject/pallas_call | solution.py:460
  359.5 13.6 %weight.2 = bf16[2048,2048]{1,0:T(8,128)(2,1)} custom-call(f32[1,2048]{1,0:T(1,128)} %get-tuple-element.130.refs_0_, bf16[1024,2048]{1,0:T(8,128)(2,1)} %get-tuple-element.131.refs_1_, f32[1,2048]{1,0:T(1,128)} %get-tuple-element.180.refs_2_, bf16[1024,2048]{1,0:T(8,128)(2,1)} %bitcast.89), custom_call_target="tpu_custom_call" | custom-call | flops 1 | bytes 1 | tf_op jit(solution)/shard_map/weight/pallas_call | solution.py:517
  382.0 16.3 %backward.3 = (f32[2,512,2048]{2,1,0:T(8,128)}, f32[16,2048]{1,0:T(8,128)}) custom-call(f32[2,512]{1,0:T(2,128)} %convert_element_type.43.keep, f32[3,2048]{1,0:T(4,128)} %select_add_fusion.3.moments, f32[3,2048]{1,0:T(4,128)} %get-tuple-element.175.gains, f32[2,8192,128]{2,1,0:T(8,128)} %get-tuple-element.135.s_ref.before_ref, ...), custom_call_target="tpu_custom_call" | custom-call | flops 1 | bytes 1 | tf_op jit(solution)/shard_map/backward/pallas_call | solution.py:353
  424.0 12.0 %dproject.4 = (bf16[512,2048]{1,0:T(8,128)(2,1)}, f32[1,2048]{1,0:T(1,128)}, bf16[4,512,512]{2,1,0:T(8,128)(2,1)}) custom-call(f32[3,2048]{1,0:T(4,128)} %select_add_fusion.3.moments, f32[3,2048]{1,0:T(4,128)} %get-tuple-element.175.gains, f32[3,2048]{1,0:T(4,128)} %bitcast.103, f32[1024,2048]{1,0:T(8,128)} %bitcast.84, ...), custom_call_target="tpu_custom_call" | custom-call | flops 1 | bytes 1 | tf_op jit(solution)/shard_map/dproject/pallas_call | solution.py:460
  436.0 5.1 all-to-all-start.9
  442.0 12.0 %dproject.5 = (bf16[512,2048]{1,0:T(8,128)(2,1)}, f32[1,2048]{1,0:T(1,128)}, bf16[4,512,512]{2,1,0:T(8,128)(2,1)}) custom-call(f32[3,2048]{1,0:T(4,128)} %select_add_fusion.3.moments, f32[3,2048]{1,0:T(4,128)} %get-tuple-element.175.gains, f32[3,2048]{1,0:T(4,128)} %bitcast.104, f32[1024,2048]{1,0:T(8,128)} %bitcast.85, ...), custom_call_target="tpu_custom_call" | custom-call | flops 1 | bytes 1 | tf_op jit(solution)/shard_map/dproject/pallas_call | solution.py:460
  454.0 13.7 %weight.3 = bf16[2048,2048]{1,0:T(8,128)(2,1)} custom-call(f32[1,2048]{1,0:T(1,128)} %get-tuple-element.149.refs_0_, f32[1,2048]{1,0:T(1,128)} %get-tuple-element.150.refs_1_, bf16[512,2048]{1,0:T(8,128)(2,1)} %get-tuple-element.151.refs_2_, bf16[512,2048]{1,0:T(8,128)(2,1)} %get-tuple-element.152.refs_3_, f32[1,2048]{1,0:T(1,128)} %get-tuple-element.186.refs_4_, ...), custom_call_target="tpu_custom_call" | custom-call | flops 1 | bytes 1 | tf_op jit(solution)/shard_map/weight/pallas_call | solution.py:517
  467.7 22.1 %all-to-all-done.9 = bf16[4,512,512]{2,1,0:T(8,128)(2,1)} async-done(((bf16[4,512,512]{2,1,0:T(8,128)(2,1)}), bf16[4,512,512]{2,1,0:T(8,128)(2,1)}, u32[]{:S(2)}, u32[]{:S(2)}) %all-to-all-start.9) | async-done | bytes 2097184 | tf_op jit(solution)/shard_map/all_to_all | solution.py:31
  518.6 38.7 %all-to-all-done.10 = bf16[4,512,512]{2,1,0:T(8,128)(2,1)} async-done(((bf16[4,512,512]{2,1,0:T(8,128)(2,1)}), bf16[4,512,512]{2,1,0:T(8,128)(2,1)}, u32[]{:S(2)}, u32[]{:S(2)}) %all-to-all-start.10) | async-done | bytes 2097184 | tf_op jit(solution)/shard_map/all_to_all | solution.py:31
  571.1 5.0 convert_add_fusion
  576.1 15.4 %collective-permute-done.43 = f32[1,2048]{1,0:T(1,128)S(1)} collective-permute-done((f32[1,2048]{1,0:T(1,128)S(1)}, f32[1,2048]{1,0:T(1,128)S(1)}, u32[]{:S(2)}, u32[]{:S(2)}) %collective-permute-start.43) | collective-permute-done | bytes 8224 | tf_op jit(solution)/shard_map/ppermute | solution.py:669
  (234 shorter events, 191.6 us)
Async XLA Ops:
  7.2 70.5 %all-gather.8.cloned.1.call-start = ((), (), s32[]{:S(2)}) async-start(), calls=%async_computation.17 | async-start | bytes 2621440 | tf_op jit(solution)/shard_map/all_gather | solution.py:75
  11.4 57.4 %all-to-all-start = ((bf16[4,256,512]{2,1,0:T(8,128)(2,1)}), bf16[4,256,512]{2,1,0:T(8,128)(2,1)S(1)}, u32[]{:S(2)}, u32[]{:S(2)}) async-start(bf16[4,256,512]{2,1,0:T(8,128)(2,1)} %slice.199), calls=%async_computation | async-start | bytes 2097152 | tf_op jit(solution)/shard_map/all_to_all | solution.py:31
  17.8 147.8 %all-gather.6.cloned.1.call-start = ((), (), s32[]{:S(2)}) async-start(), calls=%async_computation.14 | async-start | bytes 9437184 | tf_op jit(solution)/shard_map/all_gather | solution.py:577
  80.8 79.8 %all-to-all-start.1 = ((bf16[4,768,512]{2,1,0:T(8,128)(2,1)}), bf16[4,768,512]{2,1,0:T(8,128)(2,1)S(1)}, u32[]{:S(2)}, u32[]{:S(2)}) async-start(bf16[4,768,512]{2,1,0:T(8,128)(2,1)} %slice.200), calls=%async_computation.1 | async-start | bytes 6291456 | tf_op jit(solution)/shard_map/all_to_all | solution.py:31
  84.5 139.9 %all-gather.10.cloned.1.call-start = ((), (), s32[]{:S(2)}) async-start(), calls=%async_computation.18 | async-start | bytes 9437184 | tf_op jit(solution)/shard_map/all_gather | solution.py:580
  95.1 42.6 %collective-permute-start.4 = (f32[6,2048]{1,0:T(8,128)S(1)}, f32[6,2048]{1,0:T(8,128)S(1)}, u32[]{:S(2)}, u32[]{:S(2)}) collective-permute-start(f32[6,2048]{1,0:T(8,128)S(1)} %add.274), channel_id=1, source_target_pairs={{0,1},{1,0},{2,3},{3,2},{4,5},{5,4},{6,7},{7,6},{8,9},{9,8},{10,11... | collective-permute-start | bytes 147464 | tf_op jit(solution)/shard_map/ppermute | solution.py:43
  97.2 63.3 %collective-permute-start.5 = (f32[6,2048]{1,0:T(8,128)S(1)}, f32[6,2048]{1,0:T(8,128)S(1)}, u32[]{:S(2)}, u32[]{:S(2)}) collective-permute-start(f32[6,2048]{1,0:T(8,128)S(1)} %add.274), channel_id=1, source_target_pairs={{0,2},{1,3},{2,0},{3,1},{4,6},{5,7},{6,4},{7,5},{8,10},{9,11},{10,... | collective-permute-start | bytes 147464 | tf_op jit(solution)/shard_map/ppermute | solution.py:43
  99.5 61.0 %collective-permute-start.6 = (f32[6,2048]{1,0:T(8,128)S(1)}, f32[6,2048]{1,0:T(8,128)S(1)}, u32[]{:S(2)}, u32[]{:S(2)}) collective-permute-start(f32[6,2048]{1,0:T(8,128)S(1)} %add.274), channel_id=1, source_target_pairs={{0,3},{1,2},{2,1},{3,0},{4,7},{5,6},{6,5},{7,4},{8,11},{9,10},{10,... | collective-permute-start | bytes 147464 | tf_op jit(solution)/shard_map/ppermute | solution.py:43
  160.6 29.0 %all-to-all-start.2 = ((bf16[4,1024,128]{2,1,0:T(8,128)(2,1)}), bf16[4,1024,128]{2,1,0:T(8,128)(2,1)}, u32[]{:S(2)}, u32[]{:S(2)}) async-start(bf16[4,1024,128]{2,1,0:T(8,128)(2,1)} %bitcast.95), calls=%async_computation.2 | async-start | bytes 2097152 | tf_op jit(solution)/shard_map/all_to_all | solution.py:31
  203.3 48.8 %all-to-all-start.3 = ((bf16[4,1024,256]{2,1,0:T(8,128)(2,1)}), bf16[4,1024,256]{2,1,0:T(8,128)(2,1)S(1)}, u32[]{:S(2)}, u32[]{:S(2)}) async-start(bf16[4,1024,256]{2,1,0:T(8,128)(2,1)} %bitcast.93), calls=%async_computation.3 | async-start | bytes 4194304 | tf_op jit(solution)/shard_map/all_to_all | solution.py:31
  265.2 26.3 %all-to-all-start.4 = ((bf16[4,1024,128]{2,1,0:T(8,128)(2,1)}), bf16[4,1024,128]{2,1,0:T(8,128)(2,1)S(1)}, u32[]{:S(2)}, u32[]{:S(2)}) async-start(bf16[4,1024,128]{2,1,0:T(8,128)(2,1)} %bitcast.6), calls=%async_computation.4 | async-start | bytes 2097152 | tf_op jit(solution)/shard_map/all_to_all | solution.py:31
  292.5 28.0 %all-to-all-start.5 = ((bf16[4,1024,128]{2,1,0:T(8,128)(2,1)}), bf16[4,1024,128]{2,1,0:T(8,128)(2,1)S(1)}, u32[]{:S(2)}, u32[]{:S(2)}) async-start(bf16[4,1024,128]{2,1,0:T(8,128)(2,1)} %bitcast.101), calls=%async_computation.5 | async-start | bytes 2097152 | tf_op jit(solution)/shard_map/all_to_all | solution.py:31
  328.2 49.6 %all-to-all-start.6 = ((bf16[4,1024,256]{2,1,0:T(8,128)(2,1)}), bf16[4,1024,256]{2,1,0:T(8,128)(2,1)S(1)}, u32[]{:S(2)}, u32[]{:S(2)}) async-start(bf16[4,1024,256]{2,1,0:T(8,128)(2,1)} %bitcast.98), calls=%async_computation.6 | async-start | bytes 4194304 | tf_op jit(solution)/shard_map/all_to_all | solution.py:31
  331.9 157.9 %reduce-scatter.3.cloned.1.call-start = ((), (), s32[]{:S(2)}) async-start(), calls=%async_computation.15 | async-start | bytes 9437184 | tf_op jit(solution)/shard_map/reduce_scatter | solution.py:622
  377.9 21.3 %all-to-all-start.7 = ((bf16[4,512,128]{2,1,0:T(8,128)(2,1)}), bf16[4,512,128]{2,1,0:T(8,128)(2,1)}, u32[]{:S(2)}, u32[]{:S(2)}) async-start(bf16[4,512,128]{2,1,0:T(8,128)(2,1)} %bitcast.106), calls=%async_computation.7 | async-start | bytes 1048576 | tf_op jit(solution)/shard_map/all_to_all | solution.py:31
  409.2 26.9 %all-to-all-start.8 = ((bf16[4,512,128]{2,1,0:T(8,128)(2,1)}), bf16[4,512,128]{2,1,0:T(8,128)(2,1)}, u32[]{:S(2)}, u32[]{:S(2)}) async-start(bf16[4,512,128]{2,1,0:T(8,128)(2,1)} %bitcast.105), calls=%async_computation.8 | async-start | bytes 1048576 | tf_op jit(solution)/shard_map/all_to_all | solution.py:31
  436.0 53.8 %all-to-all-start.9 = ((bf16[4,512,512]{2,1,0:T(8,128)(2,1)}), bf16[4,512,512]{2,1,0:T(8,128)(2,1)}, u32[]{:S(2)}, u32[]{:S(2)}) async-start(bf16[4,512,512]{2,1,0:T(8,128)(2,1)} %get-tuple-element.147), calls=%async_computation.9 | async-start | bytes 4194304 | tf_op jit(solution)/shard_map/all_to_all | solution.py:31
  441.1 117.4 %reduce-scatter.5.cloned.1.call-start = ((), (), s32[]{:S(2)}) async-start(), calls=%async_computation.16 | async-start | bytes 9437184 | tf_op jit(solution)/shard_map/reduce_scatter | solution.py:645
  492.4 64.8 %all-to-all-start.10 = ((bf16[4,512,512]{2,1,0:T(8,128)(2,1)}), bf16[4,512,512]{2,1,0:T(8,128)(2,1)}, u32[]{:S(2)}, u32[]{:S(2)}) async-start(bf16[4,512,512]{2,1,0:T(8,128)(2,1)} %get-tuple-element.156), calls=%async_computation.11 | async-start | bytes 4194304 | tf_op jit(solution)/shard_map/all_to_all | solution.py:31
  513.9 77.6 %collective-permute-start.39 = (bf16[256,512]{1,0:T(8,128)(2,1)S(1)}, bf16[256,512]{1,0:T(8,128)(2,1)S(1)}, u32[]{:S(2)}, u32[]{:S(2)}) collective-permute-start(bf16[256,512]{1,0:T(8,128)(2,1)S(1)} %bitcast.107), channel_id=1, source_target_pairs={{0,1},{1,0},{2,3},{3,2},{4,5},{5,4},{6,7},{7,6},{8,9},{9,8},{10,11... | collective-permute-start | bytes 786440 | tf_op jit(solution)/shard_map/ppermute | solution.py:657
  516.0 75.6 %collective-permute-start.40 = (bf16[256,512]{1,0:T(8,128)(2,1)S(1)}, bf16[256,512]{1,0:T(8,128)(2,1)S(1)}, u32[]{:S(2)}, u32[]{:S(2)}) collective-permute-start(bf16[256,512]{1,0:T(8,128)(2,1)S(1)} %bitcast.108), channel_id=1, source_target_pairs={{0,2},{1,3},{2,0},{3,1},{4,6},{5,7},{6,4},{7,5},{8,10},{9,11},{10,... | collective-permute-start | bytes 786440 | tf_op jit(solution)/shard_map/ppermute | solution.py:657
  518.4 73.1 %collective-permute-start.41 = (bf16[256,512]{1,0:T(8,128)(2,1)S(1)}, bf16[256,512]{1,0:T(8,128)(2,1)S(1)}, u32[]{:S(2)}, u32[]{:S(2)}) collective-permute-start(bf16[256,512]{1,0:T(8,128)(2,1)S(1)} %bitcast.109), channel_id=1, source_target_pairs={{0,3},{1,2},{2,1},{3,0},{4,7},{5,6},{6,5},{7,4},{8,11},{9,10},{10,... | collective-permute-start | bytes 786440 | tf_op jit(solution)/shard_map/ppermute | solution.py:657
  560.8 30.7 %all-to-all-start.11 = ((bf16[4,256,512]{2,1,0:T(8,128)(2,1)}), bf16[4,256,512]{2,1,0:T(8,128)(2,1)S(1)}, u32[]{:S(2)}, u32[]{:S(2)}) async-start(bf16[4,256,512]{2,1,0:T(8,128)(2,1)} %bitcast.74), calls=%async_computation.13 | async-start | bytes 2097152 | tf_op jit(solution)/shard_map/all_to_all | solution.py:31
  568.1 23.4 %collective-permute-start.43 = (f32[1,2048]{1,0:T(1,128)S(1)}, f32[1,2048]{1,0:T(1,128)S(1)}, u32[]{:S(2)}, u32[]{:S(2)}) collective-permute-start(f32[1,2048]{1,0:T(1,128)S(1)} %add.337), channel_id=1, source_target_pairs={{0,2},{1,3},{2,0},{3,1},{4,6},{5,7},{6,4},{7,5},{8,10},{9,11},{10,... | collective-permute-start | bytes 24584 | tf_op jit(solution)/shard_map/ppermute | solution.py:669
  (58 other events, 362.6 us)
Sparse Core Ops, SparseCore 0:
  10.2 67.4 all-gather.7
  80.9 54.3 all-gather.5
  160.7 54.8 all-gather.9
  378.0 71.7 reduce-scatter.2
  489.9 68.5 reduce-scatter.4

commit v3 on v2

v3 whole, which is shorter than its diff:
```python
import functools
import math

import jax
import jax.numpy as jnp
from jax import lax
from jax.experimental import pallas as pl
from jax.experimental.pallas import tpu as pltpu
from jax.sharding import PartitionSpec as P

ROW_LEN = 512
EPSILON = 1e-05
LOG2E = 1.4426950408889634
LN2 = 0.6931471805599453
LANES = 128
SUB = 16
CHUNK = 64
VMEM_LIMIT = 56 * 2**20
BOTH = ("narrow", "wide")

params_of = functools.partial(pltpu.CompilerParams, vmem_limit_bytes=VMEM_LIMIT)
SMEM = pl.BlockSpec(memory_space=pltpu.SMEM)
BRIEF = pl.CostEstimate(flops=1, bytes_accessed=1, transcendentals=0)


def whole(shape):
    return pl.BlockSpec(shape, lambda *_: (0,) * len(shape))


def merge_all(value, merge, axis, size, open_end=False):
    k = size
    while k > 1:
        if open_end and k == 2:
            return [value, lax.ppermute(value, axis, [(i, i ^ 1) for i in range(size)])]
        if k % 4 == 0 and not (open_end and k == 4):
            k //= 4
            turns = (k, 2 * k, 3 * k)
        else:
            k //= 2
            turns = (k,)
        others = [lax.ppermute(value, axis, [(i, i ^ t) for i in range(size)]) for t in turns]
        value = merge([value, *others])
    return value


def add(values):
    while len(values) > 1:
        values = [a + b for a, b in zip(values[::2], values[1::2], strict=True)]
    return values[0]


def merge_moments(frames):
    count = [frames]

    def merge(values):
        summed = add(values)
        row = lax.broadcasted_iota(jnp.int32, summed.shape, 0)
        part = 1 / len(values)
        mean = summed[0:1] * part
        gaps = [v[0:1] - mean for v in values]
        squares = add([gap * gap for gap in gaps]) * count[0]
        count[0] *= len(values)
        scale = jnp.where((row == 0) | (row == 2), part, 1.0)
        return summed * scale + jnp.where(row == 1, squares, 0.0)

    return merge


def gather_rows(weights, wide):
    rows = weights[0].shape[0] // wide
    first = lax.axis_index("wide") * rows
    shares = [lax.dynamic_slice_in_dim(weight, first, rows, 0) for weight in weights]
    return lax.all_gather(jnp.stack(shares), "narrow", axis=1)


def project_kernel(blocks, cuts, order, *refs):
    pieces = len(cuts) - 1
    x_refs = [refs[i * blocks : (i + 1) * blocks] for i in range(pieces)]
    w_ref, z_ref, moments_ref, *joined_ref = refs[pieces * blocks :]
    frames, cols = z_ref.shape
    depth = x_refs[0][0].shape[1]
    here = pl.program_id(0)
    step = math.gcd(256, *cuts)
    per_block = w_ref.shape[0] // blocks
    weights = [
        w_ref[pl.ds(order[k] * per_block, per_block)].reshape(depth, cols) for k in range(blocks)
    ]
    sums = jnp.zeros((1, cols), jnp.float32)
    for piece in range(pieces):
        for m in range(cuts[piece], cuts[piece + 1], step):
            acc = None
            for x_ref, weight in zip(x_refs[piece], weights, strict=True):
                x = x_ref[m - cuts[piece] : m - cuts[piece] + step, :]
                term = jnp.dot(x, weight, preferred_element_type=jnp.float32)
                acc = term if acc is None else acc + term
            rounded = acc.astype(jnp.bfloat16)
            z_ref[m : m + step, :] = rounded
            sums += jnp.sum(rounded.astype(jnp.float32), 0, keepdims=True)
    mean = sums / frames
    squares = jnp.zeros((1, cols), jnp.float32)
    for m in range(0, frames, step):
        gap = z_ref[m : m + step, :].astype(jnp.float32) - mean
        squares += jnp.sum(gap * gap, 0, keepdims=True)
    at = pl.ds(pl.multiple_of(here * cols, cols), cols)
    moments_ref[0:1, at] = mean
    moments_ref[1:2, at] = squares
    if not joined_ref:
        own = x_refs[0][0][:, at].astype(jnp.float32)
        moments_ref[2:3, at] = jnp.sum(own, 0, keepdims=True) / frames
        return
    for k in range(blocks):

        @pl.when(here == k)
        def _():
            total = jnp.zeros((1, depth), jnp.float32)
            for piece in range(pieces):
                own = x_refs[piece][k][...]
                joined_ref[0][cuts[piece] : cuts[piece + 1], :] = own
                total += jnp.sum(own.astype(jnp.float32), 0, keepdims=True)
            place = pl.ds(pl.multiple_of(order[k] * depth, depth), depth)
            moments_ref[2:3, place] = total / frames


def project(pieces, order, weight):
    blocks = len(pieces[0])
    depth = pieces[0][0].shape[1]
    cuts = [0]
    for piece in pieces:
        cuts.append(cuts[-1] + piece[0].shape[0])
    frames = cuts[-1]
    row_blocks, steps, span, width = weight.shape
    rows, cols = row_blocks * span, steps * width
    out_shape = [
        jax.ShapeDtypeStruct((frames, cols), jnp.bfloat16),
        jax.ShapeDtypeStruct((3, cols), jnp.float32),
    ]
    out_specs = [pl.BlockSpec((frames, width), lambda i, o: (0, i)), whole((3, cols))]
    if blocks > 1:
        out_shape.append(jax.ShapeDtypeStruct((frames, rows), jnp.bfloat16))
        out_specs.append(pl.BlockSpec((frames, depth), lambda i, o: (0, o[i])))
    flat = [block for piece in pieces for block in piece]
    return pl.pallas_call(
        functools.partial(project_kernel, blocks, cuts),
        grid_spec=pltpu.PrefetchScalarGridSpec(
            num_scalar_prefetch=1,
            grid=(steps,),
            in_specs=[whole(block.shape) for block in flat]
            + [pl.BlockSpec((row_blocks, None, span, width), lambda i, o: (0, i, 0, 0))],
            out_specs=out_specs,
        ),
        out_shape=out_shape,
        compiler_params=params_of(),
        cost_estimate=BRIEF,
        name="project",
    )(order, *flat, weight)


def to_steps(row_ref, lanes_ref, tiles):
    for j in range(tiles):
        lanes_ref[j : j + 1, :] = row_ref[:, j * LANES : (j + 1) * LANES]


def forward_kernel(total_frames, groups, order, keep, mine, other, gains, z_ref, s_ref, moments, *refs):
    *h_refs, vec, state, seq = refs
    rows, chunk, width = z_ref.shape
    tiles = width // LANES

    @pl.when(pl.program_id(0) == 0)
    def _():
        gap = mine[0:1, :] - other[0:1, :]
        squares = mine[1:2, :] + other[1:2, :] + gap * gap * (total_frames / 4)
        scale = gains[0:1, :] * lax.rsqrt(squares / total_frames + EPSILON)
        moments[...] = (mine[...] + other[...]) * 0.5
        moments[1:2, :] = squares
        lanes = [moments[0:1, :], scale * LOG2E, gains[1:2, :] * LOG2E, gains[2:3, :] * LOG2E]
        for i, row in enumerate(lanes):
            for j in range(tiles):
                vec[i, j : j + 1, :] = row[:, j * LANES : (j + 1) * LANES]
        state[...] = jnp.zeros_like(state)

    mean, scale, shift, decay = (vec[i] for i in range(4))
    first = pl.program_id(0) * chunk

    def block(c, running):
        running = list(running)
        for r in range(rows):
            values = z_ref[r, pl.ds(pl.multiple_of(c * SUB, SUB), SUB), :].astype(jnp.float32)
            for j in range(tiles):
                for half in range(SUB // 8):
                    seq[r, pl.ds(half * 8 * tiles + j, 8, stride=tiles), :] = values[
                        half * 8 : half * 8 + 8, j * LANES : (j + 1) * LANES
                    ]
        for k in range(SUB):
            for r in range(rows):
                value = (seq[r, k * tiles : (k + 1) * tiles, :] - mean) * scale + shift
                before = value + (decay * keep[r, first + c * SUB + k]) * running[r]
                fresh = jnp.where(
                    before > 30.0, before * LN2, jnp.log(1.0 + jnp.exp2(before))
                )
                running[r] = fresh
                s_ref[r, pl.ds(pl.multiple_of((c * SUB + k) * tiles, tiles), tiles), :] = fresh
        def rounded(r, tile):
            halves = [
                s_ref[r, pl.ds((c * SUB + half * 8) * tiles + tile, 8, stride=tiles), :]
                for half in range(SUB // 8)
            ]
            return jnp.concatenate(halves, 0).astype(jnp.bfloat16)

        place = pl.ds(pl.multiple_of(c * SUB, SUB), SUB)
        left = list(h_refs)
        for kind, units in groups:
            if kind == "rows":
                h_ref = left.pop(0)
                for r in range(rows):
                    for j in range(tiles):
                        h_ref[r, place, j * LANES : (j + 1) * LANES] = rounded(r, j)
            elif kind == "blocks":
                h_ref = left.pop(0)
                per_block = tiles // h_ref.shape[0]
                for q in range(h_ref.shape[0]):
                    for u, (j, r) in enumerate(units):
                        h_ref[q, u, place, :] = rounded(r, q * per_block + j)
            else:
                count = order.shape[0]
                for k in range(count):
                    h_ref = left.pop(0)
                    for u, (j, r) in enumerate(units):
                        h_ref[u, place, :] = rounded(r, order[k] * (tiles // count) + j)
        return tuple(running)

    running = lax.fori_loop(0, chunk // SUB, block, tuple(state[r] for r in range(rows)))
    for r in range(rows):
        state[r] = running[r]


def unit_shapes(groups, blocks, rows, width, length):
    shapes = []
    for kind, units in groups:
        if kind == "rows":
            shapes.append((rows, length, width))
        elif kind == "blocks":
            shapes.append((blocks, len(units), length, LANES))
        else:
            shapes += [(len(units), length, LANES)] * blocks
    return shapes


def unit_spec(shape, at):
    if len(shape) == 3:
        return pl.BlockSpec((shape[0], CHUNK, shape[2]), lambda i: (0, at(i), 0))
    return pl.BlockSpec((*shape[:2], CHUNK, LANES), lambda i: (0, 0, at(i), 0))


def forward(z, moments, gains, keep, order, groups, total_frames):
    rows, length = keep.shape
    width = z.shape[1]
    tiles = width // LANES
    shapes = unit_shapes(groups, order.shape[0], rows, width, length)
    states, merged, *results = pl.pallas_call(
        functools.partial(forward_kernel, total_frames, groups),
        grid=(length // CHUNK,),
        in_specs=[
            SMEM,
            SMEM,
            whole((3, width)),
            whole((3, width)),
            whole((3, width)),
            pl.BlockSpec((rows, CHUNK, width), lambda i: (0, i, 0)),
        ],
        out_specs=[
            pl.BlockSpec((rows, CHUNK * tiles, LANES), lambda i: (0, i, 0)),
            whole((3, width)),
        ]
        + [unit_spec(shape, lambda i: i) for shape in shapes],
        out_shape=[
            jax.ShapeDtypeStruct((rows, length * tiles, LANES), jnp.float32),
            jax.ShapeDtypeStruct((3, width), jnp.float32),
        ]
        + [jax.ShapeDtypeStruct(shape, jnp.bfloat16) for shape in shapes],
        scratch_shapes=[
            pltpu.VMEM((4, tiles, LANES), jnp.float32),
            pltpu.VMEM((rows, tiles, LANES), jnp.float32),
            pltpu.VMEM((rows, SUB * tiles, LANES), jnp.float32),
        ],
        compiler_params=params_of(),
        cost_estimate=BRIEF,
        name="forward",
    )(order, keep, *moments, gains, z.reshape(rows, length, width))
    grouped = []
    for kind, _ in groups:
        grouped.append([results.pop(0) for _ in range(order.shape[0] if kind == "line" else 1)])
    return states, merged, grouped


def backward_kernel(groups, order, keep, moments, gains, extra, s_ref, before_ref, z_ref, *refs):
    *g_refs, dpre_ref, out_ref, sums_ref, vec, state, seq, grads = refs
    rows, chunk, width = z_ref.shape
    tiles = width // LANES
    step = pl.program_id(0)
    first = (pl.num_programs(0) - 1 - step) * chunk

    @pl.when(step == 0)
    def _():
        for j in range(tiles):
            vec[j : j + 1, :] = gains[2:3, j * LANES : (j + 1) * LANES]
        state[...] = jnp.zeros_like(state)
        sums_ref[...] = jnp.zeros_like(sums_ref)

    decay = vec[...]
    mean = moments[0:1, :]
    blocks = chunk // SUB

    def block(i, running):
        *running, dsum = running
        c = blocks - 1 - i
        base = pl.multiple_of(c * SUB, SUB)
        def spread(r, tile, values):
            for half in range(SUB // 8):
                seq[r, pl.ds(half * 8 * tiles + tile, 8, stride=tiles), :] = values[
                    half * 8 : half * 8 + 8, :
                ]

        left = list(g_refs)
        for kind, units in groups:
            if kind == "rows":
                g_ref = left.pop(0)
                for r in range(rows):
                    values = g_ref[r, pl.ds(base, SUB), :].astype(jnp.float32)
                    for j in range(tiles):
                        spread(r, j, values[:, j * LANES : (j + 1) * LANES])
            elif kind == "blocks":
                g_ref = left.pop(0)
                per_block = tiles // g_ref.shape[0]
                for q in range(g_ref.shape[0]):
                    for u, (j, r) in enumerate(units):
                        values = g_ref[q, u, pl.ds(base, SUB), :].astype(jnp.float32)
                        spread(r, q * per_block + j, values)
            else:
                count = order.shape[0]
                for k in range(count):
                    g_ref = left.pop(0)
                    for u, (j, r) in enumerate(units):
                        values = g_ref[u, pl.ds(base, SUB), :].astype(jnp.float32)
                        spread(r, order[k] * (tiles // count) + j, values)
        for k in range(SUB - 1, -1, -1):
            for r in range(rows):
                at = c * SUB + k
                s = s_ref[r, pl.ds(pl.multiple_of(at * tiles, tiles), tiles), :]
                if k > 0:
                    prior = s_ref[r, pl.ds(pl.multiple_of((at - 1) * tiles, tiles), tiles), :]
                else:
                    inner = s_ref[
                        r, pl.ds(pl.multiple_of(jnp.maximum(at - 1, 0) * tiles, tiles), tiles), :
                    ]
                    prior = jnp.where(c > 0, inner, before_ref[r])
                mark = keep[r, first + at]
                slope = 1.0 - jnp.exp2(s * -LOG2E)
                dpre = (seq[r, k * tiles : (k + 1) * tiles, :] + running[r]) * slope
                held = dpre * mark
                running[r] = held * decay
                dsum = dsum + held * prior
                grads[r, k * tiles : (k + 1) * tiles, :] = dpre
        gb = jnp.zeros((8, width), jnp.float32)
        gg = jnp.zeros((8, width), jnp.float32)
        for r in range(rows):
            gaps = z_ref[r, pl.ds(base, SUB), :].astype(jnp.float32) - mean
            for half in range(SUB // 8):
                dpre = jnp.concatenate(
                    [
                        grads[r, pl.ds(half * 8 * tiles + j, 8, stride=tiles), :]
                        for j in range(tiles)
                    ],
                    1,
                )
                dpre_ref[r, pl.ds(pl.multiple_of(base + half * 8, 8), 8), :] = dpre
                gb += dpre
                gg += dpre * gaps[half * 8 : half * 8 + 8, :]
        sums_ref[0:8, :] += gb
        sums_ref[8:16, :] += gg
        return (*running, dsum)

    start = tuple(state[r] for r in range(rows)) + (state[rows],)
    *running, dsum = lax.fori_loop(0, blocks, block, start)
    for r in range(rows):
        state[r] = running[r]
    state[rows] = dsum

    @pl.when(step == pl.num_programs(0) - 1)
    def _():
        gb = jnp.sum(sums_ref[0:8, :], 0, keepdims=True)
        gg = jnp.sum(sums_ref[8:16, :], 0, keepdims=True)
        out_ref[0:1, :] = gb
        out_ref[1:2, :] = gg
        for j in range(tiles):
            out_ref[2:3, j * LANES : (j + 1) * LANES] = state[rows, j : j + 1, :]
        out_ref[3:4, :] = extra[...]


def backward(grads, order, groups, states, z, moments, gains, keep, extra):
    rows, length = keep.shape
    width = z.shape[1]
    tiles = width // LANES
    last = length // CHUNK - 1
    grads = [g for group in grads for g in group]
    dpre, sums = pl.pallas_call(
        functools.partial(backward_kernel, groups),
        grid=(length // CHUNK,),
        in_specs=[
            SMEM,
            SMEM,
            whole((3, width)),
            whole((3, width)),
            whole((1, width)),
            pl.BlockSpec((rows, CHUNK * tiles, LANES), lambda i: (0, last - i, 0)),
            pl.BlockSpec(
                (rows, tiles, LANES), lambda i: (0, jnp.maximum((last - i) * CHUNK - 1, 0), 0)
            ),
            pl.BlockSpec((rows, CHUNK, width), lambda i: (0, last - i, 0)),
        ]
        + [unit_spec(g.shape, lambda i: last - i) for g in grads],
        out_specs=[
            pl.BlockSpec((rows, CHUNK, width), lambda i: (0, last - i, 0)),
            whole((4, width)),
        ],
        out_shape=[
            jax.ShapeDtypeStruct((rows, length, width), jnp.float32),
            jax.ShapeDtypeStruct((4, width), jnp.float32),
        ],
        scratch_shapes=[
            pltpu.VMEM((16, width), jnp.float32),
            pltpu.VMEM((tiles, LANES), jnp.float32),
            pltpu.VMEM((rows + 1, tiles, LANES), jnp.float32),
            pltpu.VMEM((rows, SUB * tiles, LANES), jnp.float32),
            pltpu.VMEM((rows, SUB * tiles, LANES), jnp.float32),
        ],
        compiler_params=params_of(),
        cost_estimate=BRIEF,
        name="backward",
    )(
        order,
        keep,
        moments,
        gains,
        extra,
        states,
        states,
        z.reshape(rows, length, width),
        *grads,
    )
    return dpre.reshape(rows * length, width), sums


def dproject_kernel(total_frames, order, moments, gains, mine, other, dpre_ref, z_ref, w_ref, *refs):
    dz_ref, level_ref, sums_ref, *da_refs, dz_held, weight, arrived = refs
    here = pl.program_id(0)
    last = pl.num_programs(0) - 1
    width = dpre_ref.shape[1]
    slot = lax.rem(here, 2)

    def fetch(j):
        cols = w_ref.shape[3]
        return pltpu.make_async_copy(
            w_ref.at[:, j], weight.at[:, :, pl.ds(j * cols, cols)], arrived.at[j]
        )

    def differentiate():
        rstd = lax.rsqrt(moments[1:2, :] / total_frames + EPSILON)
        scale = gains[0:1, :] * rstd
        level = (mine[0:1, :] + other[0:1, :]) / total_frames
        slope = (mine[1:2, :] + other[1:2, :]) * (rstd * rstd) / total_frames
        gap = z_ref[...].astype(jnp.float32) - moments[0:1, :]
        dz = (scale * (dpre_ref[...] - level - gap * slope)).astype(jnp.bfloat16)
        dz_ref[...] = dz
        dz_held[slot] = dz
        level_ref[...] += jnp.sum(dz.astype(jnp.float32), 0, keepdims=True)

    def multiply():
        per_part = weight.shape[0] // len(da_refs)
        for k, da_ref in enumerate(da_refs):
            part = weight[pl.ds(order[k] * per_part, per_part)].reshape(-1, width)
            da_ref[...] = lax.dot_general(
                dz_held[1 - slot],
                part,
                (((1,), (1,)), ((), ())),
                preferred_element_type=jnp.float32,
            ).astype(jnp.bfloat16)

    @pl.when(here == 0)
    def _():
        for j in range(w_ref.shape[1]):
            fetch(j).start()
        level_ref[...] = jnp.zeros_like(level_ref)
        sums_ref[...] = mine[...] + other[...]
        differentiate()
        for j in range(w_ref.shape[1]):
            fetch(j).wait()

    @pl.when((here > 0) & (here < last))
    def _():
        multiply()
        differentiate()

    @pl.when(here == last)
    def _():
        multiply()


def dproject(dpre, z, moments, gains, sums, weight, order, total_frames, lo, hi):
    frames, width = hi - lo, z.shape[1]
    row_blocks, col_blocks, span, cols = weight.shape
    parts = order.shape[0]
    depth = row_blocks * span // parts
    step = math.gcd(frames, 256)
    steps = frames // step
    dz, level, merged, *da = pl.pallas_call(
        functools.partial(dproject_kernel, total_frames),
        grid=(steps + 1,),
        in_specs=[
            SMEM,
            whole((3, width)),
            whole((3, width)),
            whole((4, width)),
            whole((4, width)),
            pl.BlockSpec((step, width), lambda i: (jnp.minimum(i, steps - 1) + lo // step, 0)),
            pl.BlockSpec((step, width), lambda i: (jnp.minimum(i, steps - 1) + lo // step, 0)),
            pl.BlockSpec(memory_space=pl.ANY),
        ],
        out_specs=[
            pl.BlockSpec((step, width), lambda i: (jnp.minimum(i, steps - 1), 0)),
            whole((1, width)),
            whole((4, width)),
        ]
        + [pl.BlockSpec((step, depth), lambda i: (jnp.maximum(i - 1, 0), 0))] * parts,
        out_shape=[
            jax.ShapeDtypeStruct((frames, width), jnp.bfloat16),
            jax.ShapeDtypeStruct((1, width), jnp.float32),
            jax.ShapeDtypeStruct((4, width), jnp.float32),
        ]
        + [jax.ShapeDtypeStruct((frames, depth), jnp.bfloat16)] * parts,
        scratch_shapes=[
            pltpu.VMEM((2, step, width), jnp.bfloat16),
            pltpu.VMEM((row_blocks, span, width), jnp.bfloat16),
            pltpu.SemaphoreType.DMA((col_blocks,)),
        ],
        compiler_params=params_of(),
        cost_estimate=BRIEF,
        name="dproject",
    )(order, moments, gains, *sums, dpre, z, weight)
    return dz, level, merged, da


def weight_kernel(pieces, *refs):
    level_refs, dz_refs = refs[:pieces], refs[pieces : 2 * pieces]
    center_ref, source_ref, out_ref = refs[2 * pieces :]
    level = sum(level_ref[...] for level_ref in level_refs)
    center = jnp.transpose(jnp.broadcast_to(center_ref[...], (8, center_ref.shape[1])))[:, :1]
    terms = -center * level
    lo = 0
    for dz_ref in dz_refs:
        count = dz_ref.shape[0]
        terms += lax.dot_general(
            source_ref[lo : lo + count, :],
            dz_ref[...],
            (((0,), (0,)), ((), ())),
            preferred_element_type=jnp.float32,
        )
        lo += count
    out_ref[...] = terms.astype(jnp.bfloat16)


def weight_terms(source, center, dz, levels):
    frames, rows = source.shape
    cols = dz[0].shape[1]
    tile = 512
    return pl.pallas_call(
        functools.partial(weight_kernel, len(dz)),
        grid=(rows // tile,),
        in_specs=[whole((1, cols))] * len(dz)
        + [whole(d.shape) for d in dz]
        + [
            pl.BlockSpec((1, tile), lambda i: (0, i)),
            pl.BlockSpec((frames, tile), lambda i: (0, i)),
        ],
        out_specs=pl.BlockSpec((tile, cols), lambda i: (i, 0)),
        out_shape=jax.ShapeDtypeStruct((rows, cols), jnp.bfloat16),
        compiler_params=params_of(),
        cost_estimate=BRIEF,
        name="weight",
    )(*levels, *dz, center, source)


def small_kernel(total_frames, place, *refs):
    ins, outs = refs[:4], refs[4:]
    each = outs[0].shape[1]
    first = place[0] * each
    aligned = pl.multiple_of(first // LANES * LANES, LANES)
    turn = lax.rem(LANES - (first - aligned), LANES)

    def own(ref, row):
        return pltpu.roll(ref[row : row + 1, pl.ds(aligned, LANES)], turn, 1)[:, :each]

    for i in range(2):
        sums, moments = ins[2 * i : 2 * i + 2]
        rstd = lax.rsqrt(own(moments, 1) / total_frames + EPSILON)
        outs[3 * i][...] = own(sums, 1) * rstd
        outs[3 * i + 1][...] = own(sums, 0)
        outs[3 * i + 2][...] = own(sums, 2)


def small_gradients(place, each, total_frames, *values):
    results = pl.pallas_call(
        functools.partial(small_kernel, total_frames),
        in_specs=[SMEM] + [pl.BlockSpec(memory_space=pltpu.VMEM)] * 4,
        out_specs=[pl.BlockSpec(memory_space=pltpu.VMEM)] * 6,
        out_shape=[jax.ShapeDtypeStruct((1, each), jnp.float32)] * 6,
        cost_estimate=BRIEF,
        name="small",
    )(place, *values)
    results = [r.reshape(each) for r in results]
    return results[:3], results[3:]


def per_device(sizes, inputs, flags, w_one, *rest):
    gamma_one, beta_one, decay_one, w_two, gamma_two, beta_two, decay_two, cotangent = rest
    wide, narrow = sizes["wide"], sizes["narrow"]
    n = lax.axis_index("narrow")
    w = lax.axis_index("wide")
    frames = inputs.shape[0] // narrow
    part = inputs.shape[1]
    tiles = part // LANES
    total_frames = inputs.shape[0] * wide
    rows = frames // ROW_LEN
    first = w * inputs.shape[0] + n * frames
    keep = lax.dynamic_slice_in_dim(flags, first, frames, 0).reshape(rows, ROW_LEN)
    keep = (1 - keep).astype(jnp.float32)
    tie = lax.optimization_barrier

    def along(value, merge):
        return merge_all(value, merge, "narrow", narrow)

    def across(value, merge, open_end=False):
        return merge_all(value, merge, "wide", wide, open_end)

    own = jnp.stack([gamma_one, beta_one, decay_one, gamma_two, beta_two, decay_two])
    each = own.shape[1]
    spread = jnp.zeros((6, each * wide * narrow), jnp.float32)
    spread = lax.dynamic_update_slice_in_dim(spread, own, (n * wide + w) * each, 1)

    units = [(j, r) for j in range(tiles) for r in range(rows)]
    quarter = len(units) // 4
    groups_in = [
        ("line", units[:quarter]),
        ("line", units[quarter : 3 * quarter]),
        ("line", units[3 * quarter :]),
    ]
    eighth = len(units) // 8
    groups_out = [
        ("line", units[:eighth]),
        ("line", units[eighth : 5 * eighth]),
        ("line", units[5 * eighth : 6 * eighth]),
        ("line", units[6 * eighth :]),
    ]

    sliced = cotangent.reshape(narrow, rows, ROW_LEN, tiles, LANES)
    held = [jnp.stack([sliced[:, r, :, j] for j, r in group], 1) for _, group in groups_in]

    line = [n ^ k for k in range(narrow)]
    order = jnp.stack([jnp.asarray(q, jnp.int32) for q in line])
    alone = jnp.zeros((1,), jnp.int32)

    def along_line(blocks):
        pairs = [[(i, i ^ k) for i in range(narrow)] for k in range(narrow)]
        return blocks[:1] + [lax.ppermute(blocks[k], "narrow", pairs[k]) for k in range(1, narrow)]

    split = frames // 4
    def frames_for(lo, hi):
        return [lax.dynamic_slice_in_dim(inputs, q * frames + lo, hi - lo, 0) for q in line]

    early = along_line(frames_for(0, split))
    late = frames_for(split, frames)
    shares = gather_rows([w_one, w_two], wide)
    held = [[lax.dynamic_index_in_dim(h, q, 0, keepdims=False) for q in line] for h in held]
    first = held[0]
    shares, early, late, held, spread, keep, first = tie(
        (shares, early, late, held, spread, keep, first)
    )
    late = along_line(late)
    gains = across(spread, add)
    for k in (1, 2):
        gains = gains + lax.ppermute(gains, "narrow", [(i, i ^ k) for i in range(narrow)])
    share_one, share_two = shares[0], shares[1]
    full_one = lax.all_gather(share_one, "wide", axis=0)
    full_one, first = tie((full_one, first))
    first = along_line(first)
    late, held, share_two, gains = tie((late, held, share_two, gains))
    gains_one, gains_two = gains[:3], gains[3:]
    full_two = lax.all_gather(share_two, "wide", axis=0)
    z_one, moments, source = project([early, late], order, full_one)
    moments, first = tie((moments, first))
    grads = [first]
    merge = merge_moments(frames)
    moments = along(moments, merge)
    moments, held = tie((moments, held))
    group = along_line(held[1])
    halves = across(moments, merge, True)
    plain = [("rows", None)]
    states_one, moments_one, ((h_one,),) = forward(
        z_one, halves, gains_one, keep, alone, plain, total_frames
    )
    h_one = h_one.reshape(frames, -1)
    z_two, moments = project([[h_one]], alone, full_two)
    moments, group = tie((moments, group))
    grads.append(group)
    merge = merge_moments(frames)
    moments = along(moments, merge)
    moments, held = tie((moments, held))
    group = along_line(held[2])
    halves = across(moments, merge, True)
    states_two, moments_two, h_two = forward(
        z_two, halves, gains_two, keep, order, groups_out, total_frames
    )
    grads.append(group)

    second = [along_line(h_two[0])]
    dpre, sums = backward(
        grads, order, groups_in, states_two, z_two, moments_two, gains_two, keep, gains_two[:1]
    )
    sums, second[0] = tie((sums, second[0]))
    sums = along(sums, add)
    sums, h_two = tie((sums, h_two))
    group = along_line(h_two[1])
    halves = across(sums, add, True)
    dz_two, level_two, sums_two, (dh_one,) = dproject(
        dpre, z_two, moments_two, gains_two, halves, full_two, alone, total_frames, 0, frames
    )
    center_one, center_two = moments_one[2:3], moments_two[2:3]
    terms_two = weight_terms(h_one, center_two, [dz_two], [level_two])
    terms_two, third = tie((terms_two, h_two[2]))
    third = along_line(third)
    terms_two, dh_one, group = tie((terms_two, dh_one, group))
    second.append(group)
    plane_two = lax.psum_scatter(terms_two, "wide", scatter_dimension=0, tiled=True)
    dh_one = dh_one.reshape(rows, ROW_LEN, -1)
    dpre, sums = backward(
        [[dh_one]], alone, plain, states_one, z_one, moments_one, gains_one, keep, level_two
    )
    sums, third = tie((sums, third))
    second.append(third)
    sums = along(sums, add)
    sums, h_two = tie((sums, h_two))
    group = along_line(h_two[3])
    halves = across(sums, add, True)
    back = functools.partial(
        dproject, dpre, z_one, moments_one, gains_one, halves, full_one, order, total_frames
    )
    split = frames // 4
    dz_early, level_early, sums_one, da_early = back(0, split)
    level_two = sums_one[3:]
    da_early, group = tie((da_early, group))
    second.append(group)
    da_early = along_line(da_early)
    dz_late, level_late, _, da_late = back(split, frames)
    terms_one = weight_terms(source, center_one, [dz_early, dz_late], [level_early, level_late])
    levels = (level_early, level_late)
    da_early, da_late, terms_one, plane_two, levels, second = tie(
        (da_early, da_late, terms_one, plane_two, levels, second)
    )
    plane_one = lax.psum_scatter(terms_one, "wide", scatter_dimension=0, tiled=True)
    da_late = along_line(da_late)
    da_late[1], second = tie((da_late[1], second))
    parts = {}
    for (kind, group), came in zip(groups_out, second, strict=True):
        if kind == "line":
            stacked = jnp.stack(came)
            came = [
                jnp.stack(
                    [lax.dynamic_index_in_dim(stacked, n ^ q, 0, keepdims=False) for q in range(narrow)]
                )
            ]
        for u, unit in enumerate(group):
            parts[unit] = came[0][:, u]
    whole_two = jnp.stack(
        [jnp.concatenate([parts[j, r] for j in range(tiles)], -1) for r in range(rows)], 1
    )
    whole_two = whole_two.reshape(inputs.shape).astype(jnp.float32)
    output = (inputs.astype(jnp.float32) + whole_two).astype(jnp.bfloat16)

    output, levels = tie((output, levels))

    span = plane_one.shape[0]

    blocks = plane_two.reshape(span, narrow, part).transpose(1, 0, 2)
    came_two = lax.all_to_all(blocks, "narrow", split_axis=0, concat_axis=0)
    came_two = [came_two[i] for i in range(narrow)]
    level_one = levels[0] + levels[1]
    k = wide // 2
    while k:
        level_one = level_one + lax.ppermute(level_one, "wide", [(i, i ^ k) for i in range(wide)])
        k //= 2
    columns = [lax.dynamic_slice_in_dim(plane_one, q * part, part, 1) for q in line]
    columns, level_one = tie((columns, level_one))
    came_one = along_line(columns)
    k = narrow // 2
    while k:
        level_one = level_one + lax.ppermute(
            level_one, "narrow", [(i, i ^ k) for i in range(narrow)]
        )
        k //= 2

    grad_inputs = jnp.zeros(inputs.shape, jnp.float32)
    for lo, came in ((0, da_early), (split, da_late)):
        for q, block in zip(line, came, strict=True):
            at = q * frames + lo
            own = lax.dynamic_slice_in_dim(cotangent, at, block.shape[0], 0).astype(jnp.float32)
            grad_inputs = lax.dynamic_update_slice_in_dim(
                grad_inputs, own + block.astype(jnp.float32), at, 0
            )
    came_two, came_one = tie((came_two, came_one))
    dw_two = sum(block.astype(jnp.float32) for block in came_two)
    dw_one = sum(block.astype(jnp.float32) for block in came_one)

    def restored(weight, center, level):
        rows_of = lax.dynamic_slice_in_dim(center, w * span, span, 1).reshape(span, 1)
        return weight + rows_of * lax.dynamic_slice_in_dim(level, n * part, part, 1)

    dw_one = restored(dw_one, center_one, level_one)
    dw_two = restored(dw_two, center_two, level_two)

    place = jnp.asarray(n * wide + w, jnp.int32).reshape(1)
    small_one, small_two = small_gradients(
        place, each, total_frames, sums_one, moments_one, sums_two, moments_two
    )
    return output, grad_inputs, dw_one, *small_one, dw_two, *small_two


def solution(mesh):
    neurons = P(("narrow", "wide"))
    frames = P("wide", "narrow")
    weight = P(None, "narrow")
    small = (neurons, neurons, neurons)
    return jax.shard_map(
        functools.partial(per_device, dict(mesh.shape)),
        mesh=mesh,
        in_specs=(frames, P(), weight, *small, weight, *small, frames),
        out_specs=(frames, frames, frames, *small, frames, *small),
        check_vma=False,
    )
```

time: 610 us -> 577 us (0.946)
  waiting for transfers between devices: 267 us -> 180 us
  local copies, waits for them, and re-layouts: 30.3 us -> 49.9 us
  starting transfers between devices: 104 us -> 121 us
  other arithmetic: 24.3 us -> 34.9 us
    all_to_all x12 -> x1, waiting for transfers between devices: 142 us -> 0.01 us  [per_device(): came_two = lax.all_to_all(blocks, 'narrow', split_axis=0, concat_axis=0)]
    ppermute x3 -> x45, waiting for transfers between devices: 0.01 us -> 116 us  [the longest x36 58.5 us: along_line(): lax.ppermute(blocks[k], 'narrow', pairs[k])]
    ppermute x39 -> x28, waiting for transfers between devices: 99.5 us -> 27.9 us  [merge_all(): lax.ppermute(value, axis, [(i, i ^ t) for i in range(size)])]
    ppermute x3 -> x45, starting transfers between devices: 4.58 us -> 71.3 us  [the longest x36 64.4 us: along_line(): lax.ppermute(blocks[k], 'narrow', pairs[k])]
    all_to_all x12 -> x1, starting transfers between devices: 51.8 us -> 3.84 us  [per_device(): came_two = lax.all_to_all(blocks, 'narrow', split_axis=0, concat_axis=0)]
    all_gather x1, waiting for transfers between devices: 8.81 us -> 26.6 us  [gather_rows(): return lax.all_gather(jnp.stack(shares), 'narrow', axis=1)]
    dynamic_update_slice x0 -> x8, other arithmetic: none -> 15.3 us  [per_device(): lax.dynamic_update_slice_in_dim(grad_inputs, own + block.astype(jnp.float...]
    ppermute x2, waiting for transfers between devices: 15.4 us -> 9 us  [per_device(): lax.ppermute(level_one, 'narrow', [(i, i ^ k) for i in range(narrow)])]
  transfers between devices with their start and end apart: 61 -> 81, of which waited for: 39 -> 27; matrix products, arithmetic and copies ran while one was open for 7% -> 12% of each run, Pallas kernels for 27% -> 29%
where the time goes in v3:
time: 577 us; the launch traced here: 567 us
  waiting for transfers between devices  180 us (31%)
  Pallas kernels  166 us (29%)
  starting transfers between devices  121 us (21%)
  local copies, waits for them, and re-layouts  49.9 us (9%)
  other arithmetic  34.9 us (6%)
  between operations  15.6 us (3%)
    ppermute x36, starting transfers between devices, along_line(): lax.ppermute(blocks[k], 'narrow', pairs[k])  64.4 us
    ppermute x36, waiting for transfers between devices, along_line(): lax.ppermute(blocks[k], 'narrow', pairs[k])  58.5 us
    ppermute x2, waiting for transfers between devices, per_device(): lax.ppermute(gains, 'narrow', [(i, i ^ k) for i in range(narrow)])  54.1 us
    ppermute x28, starting transfers between devices, merge_all(): lax.ppermute(value, axis, [(i, i ^ t) for i in range(size)])  44.7 us
    pallas_call x3, Pallas kernels, dproject(): pl.pallas_call(functools.partial(dproject_kernel, total_frames), grid=(st...  41.6 us
    pallas_call x2, Pallas kernels, project(): pl.pallas_call(functools.partial(project_kernel, blocks, cuts), grid_spec...  32.6 us
    pallas_call x2, Pallas kernels, backward(): pl.pallas_call(functools.partial(backward_kernel, groups), grid=(length /...  31.7 us
    pallas_call x2, Pallas kernels, forward(): pl.pallas_call(functools.partial(forward_kernel, total_frames, groups), g...  31.5 us
  transfers between devices with their start and end apart: 81, of which 27 were waited for; matrix products, arithmetic and copies ran while one was open for 12% of the time, Pallas kernels for 29%

profile of v3, /device:TPU:0, one launch (start us, length us, event | category | flops | bytes accessed | tf_op | source)
XLA Modules:
  0.0 567.4 jit_solution(15515812352987510336)
XLA Ops:
  16.9 6.9 %reshape.78 = bf16[4,2,512,4,128]{4,3,2,1,0:T(4,128)(2,1)} reshape(bf16[4096,512]{1,0:T(8,128)(2,1)} %param.21) | data formatting | bytes 8388608 | tf_op jit(solution)/shard_map/reshape | solution.py:664
  25.5 13.3 %fusion.38 = (bf16[4,1,512,1,128]{4,3,2,1,0:T(2,128)(2,1)S(1)}, bf16[4,1,512,1,128]{4,3,2,1,0:T(2,128)(2,1)S(1)}, bf16[4,1,512,1,128]{4,3,2,1,0:T(2,128)(2,1)S(1...) fusion(bf16[4,2,512,4,128]{4,3,2,1,0:T(4,128)(2,1)} %reshape.78), kind=kLoop, calls=%fused_computation.174 | loop fusion | bytes 8388608 | tf_op jit(solution)/shard_map/slice | solution.py:665
  45.3 26.6 %all-gather.8.cloned.1.call-done = bf16[2,1024,512]{2,1,0:T(8,128)(2,1)} async-done(((bf16[2,256,512]{2,1,0:T(8,128)(2,1)}), bf16[2,1024,512]{2,1,0:T(8,128)(2,1)}) %all-gather.8.cloned.1.call-update) | async-done | bytes 2097168 | tf_op jit(solution)/shard_map/all_gather | solution.py:73
  86.2 4.0 collective-permute-done.8
  91.6 36.2 %collective-permute-done.10 = f32[6,2048]{1,0:T(8,128)S(1)} collective-permute-done((f32[6,2048]{1,0:T(8,128)S(1)}, f32[6,2048]{1,0:T(8,128)S(1)}, u32[]{:S(2)}, u32[]{:S(2)}) %collective-permute-start.10) | collective-permute-done | bytes 49184 | tf_op jit(solution)/shard_map/ppermute | solution.py:690
  131.3 17.9 %collective-permute-done.11 = f32[6,2048]{1,0:T(8,128)S(1)} collective-permute-done((f32[6,2048]{1,0:T(8,128)S(1)}, f32[6,2048]{1,0:T(8,128)S(1)}, u32[]{:S(2)}, u32[]{:S(2)}) %collective-permute-start.11) | collective-permute-done | bytes 49184 | tf_op jit(solution)/shard_map/ppermute | solution.py:690
  154.7 17.4 %project.2 = (bf16[1024,2048]{1,0:T(8,128)(2,1)}, f32[3,2048]{1,0:T(4,128)}, bf16[1024,2048]{1,0:T(8,128)(2,1)}) custom-call(s32[4]{0:T(128)} %pad_add_fusion.order, bf16[256,512]{1,0:T(8,128)(2,1)} %get-tuple-element.238.refs_0_, bf16[256,512]{1,0:T(8,128)(2,1)} %copy-done.28, bf16[256,512]{1,0:T(8,128)(2,1)} %copy-done.29, bf16[256,512]{1,0:T(8,128)(2,1)} %copy-done.30, ...), custom_call_target="tpu_custom_call" | custom-call | flops 1 | bytes 1 | tf_op jit(solution)/shard_map/project/pallas_call | solution.py:142
  194.7 14.6 %forward.2 = (f32[2,8192,128]{2,1,0:T(8,128)}, f32[3,2048]{1,0:T(4,128)}, bf16[2,512,2048]{2,1,0:T(8,128)(2,1)}) custom-call(s32[1]{0:T(128)} %constant.101.clone.1.order, f32[2,512]{1,0:T(2,128)} %convert_element_type.92.keep, f32[3,2048]{1,0:T(4,128)} %copy-done.48, f32[3,2048]{1,0:T(4,128)} %copy-done.65, f32[3,2048]{1,0:T(4,128)} %get-tuple-element.525.gains, ...), custom_call_target="tpu_custom_call" | custom-call | flops 1 | bytes 1 | tf_op jit(solution)/shard_map/forward/pallas_call | solution.py:259
  209.3 15.1 %project.3 = (bf16[1024,2048]{1,0:T(8,128)(2,1)}, f32[3,2048]{1,0:T(4,128)}) custom-call(s32[1]{0:T(128)} %constant.101.clone.1.order, bf16[1024,2048]{1,0:T(8,128)(2,1)} %bitcast.144, bf16[8,4,256,512]{3,2,1,0:T(8,128)(2,1)} %bitcast.140), custom_call_target="tpu_custom_call" | custom-call | flops 1 | bytes 1 | tf_op jit(solution)/shard_map/project/pallas_call | solution.py:142
  226.0 7.9 %collective-permute-start.25 = (f32[3,2048]{1,0:T(4,128)}, f32[3,2048]{1,0:T(4,128)S(1)}, u32[]{:S(2)}, u32[]{:S(2)}) collective-permute-start(f32[3,2048]{1,0:T(4,128)} %get-tuple-element.290), channel_id=1, source_target_pairs={{0,1},{1,0},{2,3},{3,2},{4,5},{5,4},{6,7},{7,6},{8,9},{9,8},{10,11... | collective-permute-start | bytes 73736 | tf_op jit(solution)/shard_map/ppermute | solution.py:41
  251.6 16.9 %forward.3 = (f32[2,8192,128]{2,1,0:T(8,128)}, f32[3,2048]{1,0:T(4,128)}, bf16[1,512,128]{2,1,0:T(8,128)(2,1)}, bf16[1,512,128]{2,1,0:T(8,128)(2,1)}, bf16[1,512...) custom-call(s32[4]{0:T(128)} %pad_add_fusion.order, ...), custom_call_target="tpu_custom_call" | custom-call | flops 1 | bytes 1 | tf_op jit(solution)/shard_map/forward/pallas_call | solution.py:259
  274.4 15.3 %backward.2 = (f32[2,512,2048]{2,1,0:T(8,128)}, f32[4,2048]{1,0:T(4,128)}) custom-call(s32[4]{0:T(128)} %pad_add_fusion.order, f32[2,512]{1,0:T(2,128)} %convert_element_type.92.keep, f32[3,2048]{1,0:T(4,128)} %get-tuple-element.297.moments.refs_3_, f32[3,2048]{1,0:T(4,128)} %get-tuple-element.524.gains, f32[1,2048]{1,0:T(1,128)} %slice.171.extra, ...), custom_call_target="tpu_custom_call" | custom-call | flops 1 | bytes 1 | tf_op jit(solution)/shard_map/backward/pallas_call | solution.py:405
  313.7 17.5 %dproject.3 = (bf16[1024,2048]{1,0:T(8,128)(2,1)}, f32[1,2048]{1,0:T(1,128)}, f32[4,2048]{1,0:T(4,128)}, bf16[1024,2048]{1,0:T(8,128)(2,1)}) custom-call(s32[1]{0:T(128)} %constant.101.clone.1.order, f32[3,2048]{1,0:T(4,128)} %get-tuple-element.297.moments.refs_3_, f32[3,2048]{1,0:T(4,128)} %get-tuple-element.524.gains, f32[4,2048]{1,0:T(4,128)} %copy-done.46, ...), custom_call_target="tpu_custom_call" | custom-call | flops 1 | bytes 1 | tf_op jit(solution)/shard_map/dproject/pallas_call | solution.py:515
  331.3 13.6 %weight.2 = bf16[2048,2048]{1,0:T(8,128)(2,1)} custom-call(f32[1,2048]{1,0:T(1,128)} %get-tuple-element.331.refs_0_.extra, bf16[1024,2048]{1,0:T(8,128)(2,1)} %get-tuple-element.333.refs_1_, f32[1,2048]{1,0:T(1,128)} %slice.172.refs_2_, bf16[1024,2048]{1,0:T(8,128)(2,1)} %bitcast.145), custom_call_target="tpu_custom_call" | custom-call | flops 1 | bytes 1 | tf_op jit(solution)/shard_map/weight/pallas_call | solution.py:575
  351.4 16.4 %backward.3 = (f32[2,512,2048]{2,1,0:T(8,128)}, f32[4,2048]{1,0:T(4,128)}) custom-call(s32[1]{0:T(128)} %constant.101.clone.1.order, f32[2,512]{1,0:T(2,128)} %convert_element_type.92.keep, f32[3,2048]{1,0:T(4,128)} %get-tuple-element.282.moments.refs_1_, f32[3,2048]{1,0:T(4,128)} %get-tuple-element.525.gains, f32[1,2048]{1,0:T(1,128)} %get-tuple-element.331.refs_0_.extra, ...), custom_call_target="tpu_custom_call" | custom-call | flops 1 | bytes 1 | tf_op jit(solution)/shard_map/backward/pallas_call | solution.py:405
  386.9 9.2 %dproject.4 = (bf16[256,2048]{1,0:T(8,128)(2,1)}, f32[1,2048]{1,0:T(1,128)}, f32[4,2048]{1,0:T(4,128)}, bf16[256,512]{1,0:T(8,128)(2,1)}, bf16[256,512]{1,0:T(8,...) custom-call(s32[4]{0:T(128)} %pad_add_fusion.order, f32[3,2048]{1,0:T(4,128)} %get-tuple-element.282.moments.refs_1_, ...), custom_call_target="tpu_custom_call" | custom-call | flops 1 | bytes 1 | tf_op jit(solution)/shard_map/dproject/pallas_call | solution.py:515
  406.7 14.9 %dproject.5 = (bf16[768,2048]{1,0:T(8,128)(2,1)}, f32[1,2048]{1,0:T(1,128)}, f32[4,2048]{1,0:T(4,128)}, bf16[768,512]{1,0:T(8,128)(2,1)}, bf16[768,512]{1,0:T(8,...) custom-call(s32[4]{0:T(128)} %pad_add_fusion.order, f32[3,2048]{1,0:T(4,128)} %get-tuple-element.282.moments.refs_1_, ...), custom_call_target="tpu_custom_call" | custom-call | flops 1 | bytes 1 | tf_op jit(solution)/shard_map/dproject/pallas_call | solution.py:515
  421.6 13.7 %weight.3 = bf16[2048,2048]{1,0:T(8,128)(2,1)} custom-call(f32[1,2048]{1,0:T(1,128)} %get-tuple-element.441.refs_0_, f32[1,2048]{1,0:T(1,128)} %get-tuple-element.442.refs_1_, bf16[256,2048]{1,0:T(8,128)(2,1)} %get-tuple-element.375.refs_2_, bf16[768,2048]{1,0:T(8,128)(2,1)} %get-tuple-element.376.refs_3_, f32[1,2048]{1,0:T(1,128)} %slice.173.refs_4_, ...), custom_call_target="tpu_custom_call" | custom-call | flops 1 | bytes 1 | tf_op jit(solution)/shard_map/weight/pallas_call | solution.py:575
  456.1 21.1 %collective-permute-done.64 = bf16[768,512]{1,0:T(8,128)(2,1)S(1)} collective-permute-done((bf16[768,512]{1,0:T(8,128)(2,1)}, bf16[768,512]{1,0:T(8,128)(2,1)S(1)}, u32[]{:S(2)}, u32[]{:S(2)}) %collective-permute-start.64) | collective-permute-done | bytes 786464 | tf_op jit(solution)/shard_map/ppermute | solution.py:673
  483.3 4.9 fusion
  496.9 27.1 %collective-permute-done.65 = bf16[768,512]{1,0:T(8,128)(2,1)} collective-permute-done((bf16[768,512]{1,0:T(8,128)(2,1)}, bf16[768,512]{1,0:T(8,128)(2,1)}, u32[]{:S(2)}, u32[]{:S(2)}) %collective-permute-start.65) | collective-permute-done | bytes 786464 | tf_op jit(solution)/shard_map/ppermute | solution.py:673
  530.9 8.9 %collective-permute-start.70 = (bf16[256,512]{1,0:T(8,128)(2,1)S(1)}, bf16[256,512]{1,0:T(8,128)(2,1)S(1)}, u32[]{:S(2)}, u32[]{:S(2)}) collective-permute-start(bf16[256,512]{1,0:T(8,128)(2,1)S(1)} %get-tuple-element.444), channel_id=1, source_target_pairs={{0,1},{1,0},{2,3},{3,2},{4,5},{5,4},{6,7},{7,6},{8,9},{9,8},{10,11... | collective-permute-start | bytes 786440 | tf_op jit(solution)/shard_map/ppermute | solution.py:673
  543.4 9.0 %collective-permute-done.74 = f32[1,2048]{1,0:T(1,128)S(1)} collective-permute-done((f32[1,2048]{1,0:T(1,128)S(1)}, f32[1,2048]{1,0:T(1,128)S(1)}, u32[]{:S(2)}, u32[]{:S(2)}) %collective-permute-start.74) | collective-permute-done | bytes 8224 | tf_op jit(solution)/shard_map/ppermute | solution.py:805
  552.4 5.3 collective-permute-done.71
  (405 shorter events, 198.2 us)
Async XLA Ops:
  7.2 64.8 %all-gather.8.cloned.1.call-start = ((), (), s32[]{:S(2)}) async-start(), calls=%async_computation.6 | async-start | bytes 2621440 | tf_op jit(solution)/shard_map/all_gather | solution.py:73
  9.2 36.1 %collective-permute-start = (bf16[256,512]{1,0:T(8,128)(2,1)S(1)}, bf16[256,512]{1,0:T(8,128)(2,1)S(1)}, u32[]{:S(2)}, u32[]{:S(2)}) collective-permute-start(bf16[256,512]{1,0:T(8,128)(2,1)S(1)} %get-tuple-element.478), channel_id=1, source_target_pairs={{0,1},{1,0},{2,3},{3,2},{4,5},{5,4},{6,7},{7,6},{8,9},{9,8},{10,11... | collective-permute-start | bytes 786440 | tf_op jit(solution)/shard_map/ppermute | solution.py:673
  12.3 33.0 %collective-permute-start.1 = (bf16[256,512]{1,0:T(8,128)(2,1)S(1)}, bf16[256,512]{1,0:T(8,128)(2,1)S(1)}, u32[]{:S(2)}, u32[]{:S(2)}) collective-permute-start(bf16[256,512]{1,0:T(8,128)(2,1)S(1)} %get-tuple-element.477), channel_id=1, source_target_pairs={{0,2},{1,3},{2,0},{3,1},{4,6},{5,7},{6,4},{7,5},{8,10},{9,11},{10,... | collective-permute-start | bytes 786440 | tf_op jit(solution)/shard_map/ppermute | solution.py:673
  16.8 132.8 %all-gather.6.cloned.1.call-start = ((), (), s32[]{:S(2)}) async-start(), calls=%async_computation.3 | async-start | bytes 9437184 | tf_op jit(solution)/shard_map/all_gather | solution.py:692
  75.0 134.3 %all-gather.10.cloned.1.call-start = ((), (), s32[]{:S(2)}) async-start(), calls=%async_computation.7 | async-start | bytes 9437184 | tf_op jit(solution)/shard_map/all_gather | solution.py:697
  75.0 74.2 %collective-permute-start.3 = (bf16[768,512]{1,0:T(8,128)(2,1)}, bf16[768,512]{1,0:T(8,128)(2,1)S(1)}, u32[]{:S(2)}, u32[]{:S(2)}) collective-permute-start(bf16[768,512]{1,0:T(8,128)(2,1)} %get-tuple-element.243), channel_id=1, source_target_pairs={{0,1},{1,0},{2,3},{3,2},{4,5},{5,4},{6,7},{7,6},{8,9},{9,8},{10,11... | collective-permute-start | bytes 2359304 | tf_op jit(solution)/shard_map/ppermute | solution.py:673
  75.1 74.1 %collective-permute-start.4 = (bf16[768,512]{1,0:T(8,128)(2,1)}, bf16[768,512]{1,0:T(8,128)(2,1)S(1)}, u32[]{:S(2)}, u32[]{:S(2)}) collective-permute-start(bf16[768,512]{1,0:T(8,128)(2,1)} %get-tuple-element.244), channel_id=1, source_target_pairs={{0,2},{1,3},{2,0},{3,1},{4,6},{5,7},{6,4},{7,5},{8,10},{9,11},{10,... | collective-permute-start | bytes 2359304 | tf_op jit(solution)/shard_map/ppermute | solution.py:673
  78.1 71.2 %collective-permute-start.5 = (bf16[768,512]{1,0:T(8,128)(2,1)S(1)}, bf16[768,512]{1,0:T(8,128)(2,1)S(1)}, u32[]{:S(2)}, u32[]{:S(2)}) collective-permute-start(bf16[768,512]{1,0:T(8,128)(2,1)S(1)} %get-tuple-element.245), channel_id=1, source_target_pairs={{0,3},{1,2},{2,1},{3,0},{4,7},{5,6},{6,5},{7,4},{8,11},{9,10},{10,... | collective-permute-start | bytes 2359304 | tf_op jit(solution)/shard_map/ppermute | solution.py:673
  91.5 36.3 %collective-permute-start.10 = (f32[6,2048]{1,0:T(8,128)S(1)}, f32[6,2048]{1,0:T(8,128)S(1)}, u32[]{:S(2)}, u32[]{:S(2)}) collective-permute-start(f32[6,2048]{1,0:T(8,128)S(1)} %add.371), channel_id=1, source_target_pairs={{0,1},{1,0},{2,3},{3,2},{4,5},{5,4},{6,7},{7,6},{8,9},{9,8},{10,11... | collective-permute-start | bytes 147464 | tf_op jit(solution)/shard_map/ppermute | solution.py:690
  149.3 286.1 %reduce-scatter.3.cloned.1.call-start = ((), (), s32[]{:S(2)}) async-start(), calls=%async_computation.4 | async-start | bytes 9437184 | tf_op jit(solution)/shard_map/reduce_scatter | solution.py:742
  187.6 36.8 %collective-permute-start.22 = (bf16[4,512,128]{2,1,0:T(8,128)(2,1)}, bf16[4,512,128]{2,1,0:T(8,128)(2,1)S(1)}, u32[]{:S(2)}, u32[]{:S(2)}) collective-permute-start(bf16[4,512,128]{2,1,0:T(8,128)(2,1)} %get-tuple-element.287), channel_id=1, source_target_pairs={{0,1},{1,0},{2,3},{3,2},{4,5},{5,4},{6,7},{7,6},{8,9},{9,8},{10,11... | collective-permute-start | bytes 1572872 | tf_op jit(solution)/shard_map/ppermute | solution.py:673
  187.8 38.2 %collective-permute-start.23 = (bf16[4,512,128]{2,1,0:T(8,128)(2,1)S(1)}, bf16[4,512,128]{2,1,0:T(8,128)(2,1)S(1)}, u32[]{:S(2)}, u32[]{:S(2)}) collective-permute-start(bf16[4,512,128]{2,1,0:T(8,128)(2,1)S(1)} %copy-done.17), channel_id=1, source_target_pairs={{0,2},{1,3},{2,0},{3,1},{4,6},{5,7},{6,4},{7,5},{8,10},{9,11},{10,... | collective-permute-start | bytes 1572872 | tf_op jit(solution)/shard_map/ppermute | solution.py:673
  189.6 36.4 %collective-permute-start.24 = (bf16[4,512,128]{2,1,0:T(8,128)(2,1)S(1)}, bf16[4,512,128]{2,1,0:T(8,128)(2,1)S(1)}, u32[]{:S(2)}, u32[]{:S(2)}) collective-permute-start(bf16[4,512,128]{2,1,0:T(8,128)(2,1)S(1)} %copy-done.16), channel_id=1, source_target_pairs={{0,3},{1,2},{2,1},{3,0},{4,7},{5,6},{6,5},{7,4},{8,11},{9,10},{10,... | collective-permute-start | bytes 1572872 | tf_op jit(solution)/shard_map/ppermute | solution.py:673
  301.0 43.9 %collective-permute-start.45 = (bf16[4,512,128]{2,1,0:T(8,128)(2,1)}, bf16[4,512,128]{2,1,0:T(8,128)(2,1)S(1)}, u32[]{:S(2)}, u32[]{:S(2)}) collective-permute-start(bf16[4,512,128]{2,1,0:T(8,128)(2,1)} %get-tuple-element.341), channel_id=1, source_target_pairs={{0,1},{1,0},{2,3},{3,2},{4,5},{5,4},{6,7},{7,6},{8,9},{9,8},{10,11... | collective-permute-start | bytes 1572872 | tf_op jit(solution)/shard_map/ppermute | solution.py:673
  301.0 43.9 %collective-permute-start.46 = (bf16[4,512,128]{2,1,0:T(8,128)(2,1)}, bf16[4,512,128]{2,1,0:T(8,128)(2,1)S(1)}, u32[]{:S(2)}, u32[]{:S(2)}) collective-permute-start(bf16[4,512,128]{2,1,0:T(8,128)(2,1)} %get-tuple-element.342), channel_id=1, source_target_pairs={{0,2},{1,3},{2,0},{3,1},{4,6},{5,7},{6,4},{7,5},{8,10},{9,11},{10,... | collective-permute-start | bytes 1572872 | tf_op jit(solution)/shard_map/ppermute | solution.py:673
  303.0 41.9 %collective-permute-start.47 = (bf16[4,512,128]{2,1,0:T(8,128)(2,1)}, bf16[4,512,128]{2,1,0:T(8,128)(2,1)S(1)}, u32[]{:S(2)}, u32[]{:S(2)}) collective-permute-start(bf16[4,512,128]{2,1,0:T(8,128)(2,1)} %get-tuple-element.343), channel_id=1, source_target_pairs={{0,3},{1,2},{2,1},{3,0},{4,7},{5,6},{6,5},{7,4},{8,11},{9,10},{10,... | collective-permute-start | bytes 1572872 | tf_op jit(solution)/shard_map/ppermute | solution.py:673
  345.9 180.9 %reduce-scatter.5.cloned.1.call-start = ((), (), s32[]{:S(2)}) async-start(), calls=%async_computation.5 | async-start | bytes 9437184 | tf_op jit(solution)/shard_map/reduce_scatter | solution.py:768
  399.5 35.8 %collective-permute-start.61 = (bf16[256,512]{1,0:T(8,128)(2,1)}, bf16[256,512]{1,0:T(8,128)(2,1)S(1)}, u32[]{:S(2)}, u32[]{:S(2)}) collective-permute-start(bf16[256,512]{1,0:T(8,128)(2,1)} %get-tuple-element.366), channel_id=1, source_target_pairs={{0,1},{1,0},{2,3},{3,2},{4,5},{5,4},{6,7},{7,6},{8,9},{9,8},{10,11... | collective-permute-start | bytes 786440 | tf_op jit(solution)/shard_map/ppermute | solution.py:673
  402.9 32.4 %collective-permute-start.62 = (bf16[256,512]{1,0:T(8,128)(2,1)}, bf16[256,512]{1,0:T(8,128)(2,1)S(1)}, u32[]{:S(2)}, u32[]{:S(2)}) collective-permute-start(bf16[256,512]{1,0:T(8,128)(2,1)} %get-tuple-element.367), channel_id=1, source_target_pairs={{0,2},{1,3},{2,0},{3,1},{4,6},{5,7},{6,4},{7,5},{8,10},{9,11},{10,... | collective-permute-start | bytes 786440 | tf_op jit(solution)/shard_map/ppermute | solution.py:673
  403.8 31.5 %collective-permute-start.63 = (bf16[256,512]{1,0:T(8,128)(2,1)}, bf16[256,512]{1,0:T(8,128)(2,1)S(1)}, u32[]{:S(2)}, u32[]{:S(2)}) collective-permute-start(bf16[256,512]{1,0:T(8,128)(2,1)} %get-tuple-element.368), channel_id=1, source_target_pairs={{0,3},{1,2},{2,1},{3,0},{4,7},{5,6},{6,5},{7,4},{8,11},{9,10},{10,... | collective-permute-start | bytes 786440 | tf_op jit(solution)/shard_map/ppermute | solution.py:673
  439.9 37.4 %collective-permute-start.64 = (bf16[768,512]{1,0:T(8,128)(2,1)}, bf16[768,512]{1,0:T(8,128)(2,1)S(1)}, u32[]{:S(2)}, u32[]{:S(2)}) collective-permute-start(bf16[768,512]{1,0:T(8,128)(2,1)} %get-tuple-element.395), channel_id=1, source_target_pairs={{0,1},{1,0},{2,3},{3,2},{4,5},{5,4},{6,7},{7,6},{8,9},{9,8},{10,11... | collective-permute-start | bytes 2359304 | tf_op jit(solution)/shard_map/ppermute | solution.py:673
  442.2 101.1 %all-to-all-start = ((bf16[4,256,512]{2,1,0:T(8,128)(2,1)}), bf16[4,256,512]{2,1,0:T(8,128)(2,1)S(1)}, u32[]{:S(2)}, u32[]{:S(2)}) async-start(bf16[4,256,512]{2,1,0:T(8,128)(2,1)} %bitcast.135), calls=%async_computation.1 | async-start | bytes 2097152 | tf_op jit(solution)/shard_map/all_to_all | solution.py:793
  446.1 77.9 %collective-permute-start.65 = (bf16[768,512]{1,0:T(8,128)(2,1)}, bf16[768,512]{1,0:T(8,128)(2,1)}, u32[]{:S(2)}, u32[]{:S(2)}) collective-permute-start(bf16[768,512]{1,0:T(8,128)(2,1)} %get-tuple-element.437), channel_id=1, source_target_pairs={{0,2},{1,3},{2,0},{3,1},{4,6},{5,7},{6,4},{7,5},{8,10},{9,11},{10,... | collective-permute-start | bytes 2359304 | tf_op jit(solution)/shard_map/ppermute | solution.py:673
  449.1 79.1 %collective-permute-start.66 = (bf16[768,512]{1,0:T(8,128)(2,1)}, bf16[768,512]{1,0:T(8,128)(2,1)}, u32[]{:S(2)}, u32[]{:S(2)}) collective-permute-start(bf16[768,512]{1,0:T(8,128)(2,1)} %get-tuple-element.438), channel_id=1, source_target_pairs={{0,3},{1,2},{2,1},{3,0},{4,7},{5,6},{6,5},{7,4},{8,11},{9,10},{10,... | collective-permute-start | bytes 2359304 | tf_op jit(solution)/shard_map/ppermute | solution.py:673
  (137 other events, 1923.2 us)
Sparse Core Ops, SparseCore 0:
  16.9 54.9 all-gather.7
  75.1 55.6 all-gather.5
  149.4 55.9 all-gather.9
  345.1 72.2 reduce-scatter.2
  436.4 70.4 reduce-scatter.4

commit v4 on v3

--- a/solution.py
+++ b/solution.py
@@ -15,6 +15,7 @@
 LANES = 128
 SUB = 16
 CHUNK = 64
+CHUNK_BACK = 128
 VMEM_LIMIT = 56 * 2**20
 BOTH = ("narrow", "wide")
 
@@ -161,7 +162,7 @@
 
 
 def forward_kernel(total_frames, groups, order, keep, mine, other, gains, z_ref, s_ref, moments, *refs):
-    *h_refs, vec, state, seq = refs
+    *h_refs, vec, state, seq, hold = refs
     rows, chunk, width = z_ref.shape
     tiles = width // LANES
 
@@ -187,21 +188,24 @@
             values = z_ref[r, pl.ds(pl.multiple_of(c * SUB, SUB), SUB), :].astype(jnp.float32)
             for j in range(tiles):
                 for half in range(SUB // 8):
-                    seq[r, pl.ds(half * 8 * tiles + j, 8, stride=tiles), :] = values[
+                    seq[c % 2, r, pl.ds(half * 8 * tiles + j, 8, stride=tiles), :] = values[
                         half * 8 : half * 8 + 8, j * LANES : (j + 1) * LANES
                     ]
         for k in range(SUB):
             for r in range(rows):
-                value = (seq[r, k * tiles : (k + 1) * tiles, :] - mean) * scale + shift
+                value = (seq[c % 2, r, k * tiles : (k + 1) * tiles, :] - mean) * scale + shift
                 before = value + (decay * keep[r, first + c * SUB + k]) * running[r]
                 fresh = jnp.where(
                     before > 30.0, before * LN2, jnp.log(1.0 + jnp.exp2(before))
                 )
                 running[r] = fresh
-                s_ref[r, pl.ds(pl.multiple_of((c * SUB + k) * tiles, tiles), tiles), :] = fresh
+                hold[c % 2, r, k * tiles : (k + 1) * tiles, :] = fresh
+                at = pl.ds(pl.multiple_of((c * SUB + k) * tiles, tiles), tiles)
+                s_ref[r, at, :] = fresh.astype(jnp.bfloat16)
+
         def rounded(r, tile):
             halves = [
-                s_ref[r, pl.ds((c * SUB + half * 8) * tiles + tile, 8, stride=tiles), :]
+                hold[c % 2, r, pl.ds(half * 8 * tiles + tile, 8, stride=tiles), :]
                 for half in range(SUB // 8)
             ]
             return jnp.concatenate(halves, 0).astype(jnp.bfloat16)
@@ -228,7 +232,9 @@
                         h_ref[u, place, :] = rounded(r, order[k] * (tiles // count) + j)
         return tuple(running)
 
-    running = lax.fori_loop(0, chunk // SUB, block, tuple(state[r] for r in range(rows)))
+    running = tuple(state[r] for r in range(rows))
+    for c in range(chunk // SUB):
+        running = block(c, running)
     for r in range(rows):
         state[r] = running[r]
 
@@ -245,10 +251,10 @@
     return shapes
 
 
-def unit_spec(shape, at):
+def unit_spec(shape, at, chunk):
     if len(shape) == 3:
-        return pl.BlockSpec((shape[0], CHUNK, shape[2]), lambda i: (0, at(i), 0))
-    return pl.BlockSpec((*shape[:2], CHUNK, LANES), lambda i: (0, 0, at(i), 0))
+        return pl.BlockSpec((shape[0], chunk, shape[2]), lambda i: (0, at(i), 0))
+    return pl.BlockSpec((*shape[:2], chunk, LANES), lambda i: (0, 0, at(i), 0))
 
 
 def forward(z, moments, gains, keep, order, groups, total_frames):
@@ -271,16 +277,17 @@
             pl.BlockSpec((rows, CHUNK * tiles, LANES), lambda i: (0, i, 0)),
             whole((3, width)),
         ]
-        + [unit_spec(shape, lambda i: i) for shape in shapes],
+        + [unit_spec(shape, lambda i: i, CHUNK) for shape in shapes],
         out_shape=[
-            jax.ShapeDtypeStruct((rows, length * tiles, LANES), jnp.float32),
+            jax.ShapeDtypeStruct((rows, length * tiles, LANES), jnp.bfloat16),
             jax.ShapeDtypeStruct((3, width), jnp.float32),
         ]
         + [jax.ShapeDtypeStruct(shape, jnp.bfloat16) for shape in shapes],
         scratch_shapes=[
             pltpu.VMEM((4, tiles, LANES), jnp.float32),
             pltpu.VMEM((rows, tiles, LANES), jnp.float32),
-            pltpu.VMEM((rows, SUB * tiles, LANES), jnp.float32),
+            pltpu.VMEM((2, rows, SUB * tiles, LANES), jnp.float32),
+            pltpu.VMEM((2, rows, SUB * tiles, LANES), jnp.float32),
         ],
         compiler_params=params_of(),
         cost_estimate=BRIEF,
@@ -342,17 +349,21 @@
                     for u, (j, r) in enumerate(units):
                         values = g_ref[u, pl.ds(base, SUB), :].astype(jnp.float32)
                         spread(r, order[k] * (tiles // count) + j, values)
+        def held_state(r, at):
+            rows_at = pl.ds(pl.multiple_of(at * tiles, tiles), tiles)
+            return s_ref[r, rows_at, :].astype(jnp.float32)
+
+        states = [held_state(r, c * SUB + SUB - 1) for r in range(rows)]
         for k in range(SUB - 1, -1, -1):
             for r in range(rows):
                 at = c * SUB + k
-                s = s_ref[r, pl.ds(pl.multiple_of(at * tiles, tiles), tiles), :]
+                s = states[r]
                 if k > 0:
-                    prior = s_ref[r, pl.ds(pl.multiple_of((at - 1) * tiles, tiles), tiles), :]
+                    prior = held_state(r, at - 1)
                 else:
-                    inner = s_ref[
-                        r, pl.ds(pl.multiple_of(jnp.maximum(at - 1, 0) * tiles, tiles), tiles), :
-                    ]
-                    prior = jnp.where(c > 0, inner, before_ref[r])
+                    inner = held_state(r, jnp.maximum(at - 1, 0))
+                    prior = jnp.where(c > 0, inner, before_ref[r].astype(jnp.float32))
+                states[r] = prior
                 mark = keep[r, first + at]
                 slope = 1.0 - jnp.exp2(s * -LOG2E)
                 dpre = (seq[r, k * tiles : (k + 1) * tiles, :] + running[r]) * slope
@@ -393,33 +404,33 @@
         out_ref[1:2, :] = gg
         for j in range(tiles):
             out_ref[2:3, j * LANES : (j + 1) * LANES] = state[rows, j : j + 1, :]
-        out_ref[3:4, :] = extra[...]
+        out_ref[3:4, :] = extra[0:1, :]
 
 
 def backward(grads, order, groups, states, z, moments, gains, keep, extra):
     rows, length = keep.shape
     width = z.shape[1]
     tiles = width // LANES
-    last = length // CHUNK - 1
+    last = length // CHUNK_BACK - 1
     grads = [g for group in grads for g in group]
     dpre, sums = pl.pallas_call(
         functools.partial(backward_kernel, groups),
-        grid=(length // CHUNK,),
+        grid=(length // CHUNK_BACK,),
         in_specs=[
             SMEM,
             SMEM,
             whole((3, width)),
             whole((3, width)),
-            whole((1, width)),
-            pl.BlockSpec((rows, CHUNK * tiles, LANES), lambda i: (0, last - i, 0)),
+            whole(extra.shape),
+            pl.BlockSpec((rows, CHUNK_BACK * tiles, LANES), lambda i: (0, last - i, 0)),
             pl.BlockSpec(
-                (rows, tiles, LANES), lambda i: (0, jnp.maximum((last - i) * CHUNK - 1, 0), 0)
+                (rows, tiles, LANES), lambda i: (0, jnp.maximum((last - i) * CHUNK_BACK - 1, 0), 0)
             ),
-            pl.BlockSpec((rows, CHUNK, width), lambda i: (0, last - i, 0)),
+            pl.BlockSpec((rows, CHUNK_BACK, width), lambda i: (0, last - i, 0)),
         ]
-        + [unit_spec(g.shape, lambda i: last - i) for g in grads],
+        + [unit_spec(g.shape, lambda i: last - i, CHUNK_BACK) for g in grads],
         out_specs=[
-            pl.BlockSpec((rows, CHUNK, width), lambda i: (0, last - i, 0)),
+            pl.BlockSpec((rows, CHUNK_BACK, width), lambda i: (0, last - i, 0)),
             whole((4, width)),
         ],
         out_shape=[
@@ -553,7 +564,7 @@
     level_refs, dz_refs = refs[:pieces], refs[pieces : 2 * pieces]
     center_ref, source_ref, out_ref = refs[2 * pieces :]
     level = sum(level_ref[...] for level_ref in level_refs)
-    center = jnp.transpose(jnp.broadcast_to(center_ref[...], (8, center_ref.shape[1])))[:, :1]
+    center = jnp.transpose(jnp.broadcast_to(center_ref[2:3, :], (8, center_ref.shape[1])))[:, :1]
     terms = -center * level
     lo = 0
     for dz_ref in dz_refs:
@@ -568,7 +579,7 @@
     out_ref[...] = terms.astype(jnp.bfloat16)
 
 
-def weight_terms(source, center, dz, levels):
+def weight_terms(source, moments, dz, levels):
     frames, rows = source.shape
     cols = dz[0].shape[1]
     tile = 512
@@ -578,7 +589,7 @@
         in_specs=[whole((1, cols))] * len(dz)
         + [whole(d.shape) for d in dz]
         + [
-            pl.BlockSpec((1, tile), lambda i: (0, i)),
+            pl.BlockSpec((3, tile), lambda i: (0, i)),
             pl.BlockSpec((frames, tile), lambda i: (0, i)),
         ],
         out_specs=pl.BlockSpec((tile, cols), lambda i: (i, 0)),
@@ -586,7 +597,7 @@
         compiler_params=params_of(),
         cost_estimate=BRIEF,
         name="weight",
-    )(*levels, *dz, center, source)
+    )(*levels, *dz, moments, source)
 
 
 def small_kernel(total_frames, place, *refs):
@@ -681,8 +692,8 @@
     shares = gather_rows([w_one, w_two], wide)
     held = [[lax.dynamic_index_in_dim(h, q, 0, keepdims=False) for q in line] for h in held]
     first = held[0]
-    shares, early, late, held, spread, keep, first = tie(
-        (shares, early, late, held, spread, keep, first)
+    shares, early, late, held, spread, keep, first, order = tie(
+        (shares, early, late, held, spread, keep, first, order)
     )
     late = along_line(late)
     gains = across(spread, add)
@@ -723,7 +734,7 @@
 
     second = [along_line(h_two[0])]
     dpre, sums = backward(
-        grads, order, groups_in, states_two, z_two, moments_two, gains_two, keep, gains_two[:1]
+        grads, order, groups_in, states_two, z_two, moments_two, gains_two, keep, gains_two
     )
     sums, second[0] = tie((sums, second[0]))
     sums = along(sums, add)
@@ -733,8 +744,7 @@
     dz_two, level_two, sums_two, (dh_one,) = dproject(
         dpre, z_two, moments_two, gains_two, halves, full_two, alone, total_frames, 0, frames
     )
-    center_one, center_two = moments_one[2:3], moments_two[2:3]
-    terms_two = weight_terms(h_one, center_two, [dz_two], [level_two])
+    terms_two = weight_terms(h_one, moments_two, [dz_two], [level_two])
     terms_two, third = tie((terms_two, h_two[2]))
     third = along_line(third)
     terms_two, dh_one, group = tie((terms_two, dh_one, group))
@@ -755,19 +765,20 @@
     )
     split = frames // 4
     dz_early, level_early, sums_one, da_early = back(0, split)
-    level_two = sums_one[3:]
     da_early, group = tie((da_early, group))
     second.append(group)
     da_early = along_line(da_early)
     dz_late, level_late, _, da_late = back(split, frames)
-    terms_one = weight_terms(source, center_one, [dz_early, dz_late], [level_early, level_late])
+    terms_one = weight_terms(source, moments_one, [dz_early, dz_late], [level_early, level_late])
     levels = (level_early, level_late)
     da_early, da_late, terms_one, plane_two, levels, second = tie(
         (da_early, da_late, terms_one, plane_two, levels, second)
     )
     plane_one = lax.psum_scatter(terms_one, "wide", scatter_dimension=0, tiled=True)
     da_late = along_line(da_late)
-    da_late[1], second = tie((da_late[1], second))
+    da_late[1], second, moments_one, moments_two, sums_one, sums_two = tie(
+        (da_late[1], second, moments_one, moments_two, sums_one, sums_two)
+    )
     parts = {}
     for (kind, group), came in zip(groups_out, second, strict=True):
         if kind == "line":
@@ -819,12 +830,12 @@
     dw_two = sum(block.astype(jnp.float32) for block in came_two)
     dw_one = sum(block.astype(jnp.float32) for block in came_one)
 
-    def restored(weight, center, level):
-        rows_of = lax.dynamic_slice_in_dim(center, w * span, span, 1).reshape(span, 1)
-        return weight + rows_of * lax.dynamic_slice_in_dim(level, n * part, part, 1)
-
-    dw_one = restored(dw_one, center_one, level_one)
-    dw_two = restored(dw_two, center_two, level_two)
+    def restored(weight, moments, level, row):
+        rows_of = lax.dynamic_slice(moments, (2, w * span), (1, span)).reshape(span, 1)
+        return weight + rows_of * lax.dynamic_slice(level, (row, n * part), (1, part))
+
+    dw_one = restored(dw_one, moments_one, level_one, 0)
+    dw_two = restored(dw_two, moments_two, sums_one, 3)
 
     place = jnp.asarray(n * wide + w, jnp.int32).reshape(1)
     small_one, small_two = small_gradients(

time: 577 us -> 570 us (0.988)
  starting transfers between devices: 121 us -> 133 us
  waiting for transfers between devices: 180 us -> 169 us
    all_gather x1, waiting for transfers between devices: 26.6 us -> 7.42 us  [gather_rows(): return lax.all_gather(jnp.stack(shares), 'narrow', axis=1)]
    ppermute x2, starting transfers between devices: 1.26 us -> 19.3 us  [per_device(): lax.ppermute(level_one, 'narrow', [(i, i ^ k) for i in range(narrow)])]
  transfers between devices with their start and end apart: 81 -> 81, of which waited for: 27 -> 32; matrix products, arithmetic and copies ran while one was open for 12% -> 11% of each run, Pallas kernels for 29% -> 29%
where the time goes in v4:
time: 570 us; the launch traced here: 561 us
  waiting for transfers between devices  169 us (30%)
  Pallas kernels  163 us (29%)
  starting transfers between devices  133 us (23%)
  local copies, waits for them, and re-layouts  47 us (8%)
  other arithmetic  33.9 us (6%)
  between operations  15.6 us (3%)
    ppermute x36, waiting for transfers between devices, along_line(): lax.ppermute(blocks[k], 'narrow', pairs[k])  60.7 us
    ppermute x36, starting transfers between devices, along_line(): lax.ppermute(blocks[k], 'narrow', pairs[k])  59.2 us
    ppermute x2, waiting for transfers between devices, per_device(): lax.ppermute(gains, 'narrow', [(i, i ^ k) for i in range(narrow)])  53.9 us
    pallas_call x3, Pallas kernels, dproject(): pl.pallas_call(functools.partial(dproject_kernel, total_frames), grid=(st...  42.5 us
    ppermute x28, starting transfers between devices, merge_all(): lax.ppermute(value, axis, [(i, i ^ t) for i in range(size)])  42.3 us
    pallas_call x2, Pallas kernels, project(): pl.pallas_call(functools.partial(project_kernel, blocks, cuts), grid_spec...  32.9 us
    pallas_call x2, Pallas kernels, backward(): pl.pallas_call(functools.partial(backward_kernel, groups), grid=(length /...  30 us
    pallas_call x2, Pallas kernels, forward(): pl.pallas_call(functools.partial(forward_kernel, total_frames, groups), g...  29.3 us
  transfers between devices with their start and end apart: 81, of which 32 were waited for; matrix products, arithmetic and copies ran while one was open for 11% of the time, Pallas kernels for 29%

profile of v4, /device:TPU:0, one launch (start us, length us, event | category | flops | bytes accessed | tf_op | source)
XLA Modules:
  0.0 561.1 jit_solution(15892906121273448473)
XLA Ops:
  11.2 5.0 collective-permute-start.2
  18.2 7.1 %reshape.78 = bf16[4,2,512,4,128]{4,3,2,1,0:T(4,128)(2,1)} reshape(bf16[4096,512]{1,0:T(8,128)(2,1)} %param.21) | data formatting | bytes 8388608 | tf_op jit(solution)/shard_map/reshape | solution.py:675
  25.6 13.4 %fusion.38 = (bf16[4,1,512,1,128]{4,3,2,1,0:T(2,128)(2,1)S(1)}, bf16[4,1,512,1,128]{4,3,2,1,0:T(2,128)(2,1)S(1)}, bf16[4,1,512,1,128]{4,3,2,1,0:T(2,128)(2,1)S(1...) fusion(bf16[4,2,512,4,128]{4,3,2,1,0:T(4,128)(2,1)} %reshape.78), kind=kLoop, calls=%fused_computation.174 | loop fusion | bytes 8388608 | tf_op jit(solution)/shard_map/slice | solution.py:676
  46.3 19.2 %collective-permute-done.1.refs_2_ = bf16[256,512]{1,0:T(8,128)(2,1)S(1)} collective-permute-done((bf16[256,512]{1,0:T(8,128)(2,1)S(1)}, bf16[256,512]{1,0:T(8,128)(2,1)S(1)}, u32[]{:S(2)}, u32[]{:S(2)}) %collective-permute-start.1) | collective-permute-done | bytes 262176 | tf_op jit(solution)/shard_map/ppermute | solution.py:684
  65.5 7.4 %all-gather.8.cloned.1.call-done = bf16[2,1024,512]{2,1,0:T(8,128)(2,1)} async-done(((bf16[2,256,512]{2,1,0:T(8,128)(2,1)}), bf16[2,1024,512]{2,1,0:T(8,128)(2,1)}) %all-gather.8.cloned.1.call-update) | async-done | bytes 2097168 | tf_op jit(solution)/shard_map/all_gather | solution.py:74
  92.8 36.0 %collective-permute-done.10 = f32[6,2048]{1,0:T(8,128)S(1)} collective-permute-done((f32[6,2048]{1,0:T(8,128)S(1)}, f32[6,2048]{1,0:T(8,128)S(1)}, u32[]{:S(2)}, u32[]{:S(2)}) %collective-permute-start.10) | collective-permute-done | bytes 49184 | tf_op jit(solution)/shard_map/ppermute | solution.py:701
  132.2 18.0 %collective-permute-done.11 = f32[6,2048]{1,0:T(8,128)S(1)} collective-permute-done((f32[6,2048]{1,0:T(8,128)S(1)}, f32[6,2048]{1,0:T(8,128)S(1)}, u32[]{:S(2)}, u32[]{:S(2)}) %collective-permute-start.11) | collective-permute-done | bytes 49184 | tf_op jit(solution)/shard_map/ppermute | solution.py:701
  154.9 17.8 %project.2 = (bf16[1024,2048]{1,0:T(8,128)(2,1)}, f32[3,2048]{1,0:T(4,128)}, bf16[1024,2048]{1,0:T(8,128)(2,1)}) custom-call(s32[4]{0:T(128)} %pad_add_fusion.order, bf16[256,512]{1,0:T(8,128)(2,1)} %get-tuple-element.244.refs_0_, bf16[256,512]{1,0:T(8,128)(2,1)} %copy-done.31, bf16[256,512]{1,0:T(8,128)(2,1)} %copy-done.30, bf16[256,512]{1,0:T(8,128)(2,1)} %copy-done.29, ...), custom_call_target="tpu_custom_call" | custom-call | flops 1 | bytes 1 | tf_op jit(solution)/shard_map/project/pallas_call | solution.py:143
  193.8 13.5 %forward.2 = (bf16[2,8192,128]{2,1,0:T(8,128)(2,1)}, f32[3,2048]{1,0:T(4,128)}, bf16[2,512,2048]{2,1,0:T(8,128)(2,1)}) custom-call(s32[1]{0:T(128)} %constant.114.clone.1.order, f32[2,512]{1,0:T(2,128)} %convert_element_type.92.keep, f32[3,2048]{1,0:T(4,128)} %copy-done.49, f32[3,2048]{1,0:T(4,128)} %copy-done.68, f32[3,2048]{1,0:T(4,128)} %get-tuple-element.535.gains, ...), custom_call_target="tpu_custom_call" | custom-call | flops 1 | bytes 1 | tf_op jit(solution)/shard_map/forward/pallas_call | solution.py:265
  207.4 15.1 %project.3 = (bf16[1024,2048]{1,0:T(8,128)(2,1)}, f32[3,2048]{1,0:T(4,128)}) custom-call(s32[1]{0:T(128)} %constant.114.clone.1.order, bf16[1024,2048]{1,0:T(8,128)(2,1)} %bitcast.144, bf16[8,4,256,512]{3,2,1,0:T(8,128)(2,1)} %bitcast.140), custom_call_target="tpu_custom_call" | custom-call | flops 1 | bytes 1 | tf_op jit(solution)/shard_map/project/pallas_call | solution.py:143
  228.2 7.6 %collective-permute-start.26 = (f32[3,2048]{1,0:T(4,128)}, f32[3,2048]{1,0:T(4,128)S(1)}, u32[]{:S(2)}, u32[]{:S(2)}) collective-permute-start(f32[3,2048]{1,0:T(4,128)} %get-tuple-element.296), channel_id=1, source_target_pairs={{0,2},{1,3},{2,0},{3,1},{4,6},{5,7},{6,4},{7,5},{8,10},{9,11},{10,... | collective-permute-start | bytes 73736 | tf_op jit(solution)/shard_map/ppermute | solution.py:42
  254.6 15.8 %forward.3 = (bf16[2,8192,128]{2,1,0:T(8,128)(2,1)}, f32[3,2048]{1,0:T(4,128)}, bf16[1,512,128]{2,1,0:T(8,128)(2,1)}, bf16[1,512,128]{2,1,0:T(8,128)(2,1)}, bf16...) custom-call(s32[4]{0:T(128)} %pad_add_fusion.order, ...), custom_call_target="tpu_custom_call" | custom-call | flops 1 | bytes 1 | tf_op jit(solution)/shard_map/forward/pallas_call | solution.py:265
  275.7 15.3 %backward.2 = (f32[2,512,2048]{2,1,0:T(8,128)}, f32[4,2048]{1,0:T(4,128)}) custom-call(s32[4]{0:T(128)} %pad_add_fusion.order, f32[2,512]{1,0:T(2,128)} %convert_element_type.92.keep, f32[3,2048]{1,0:T(4,128)} %get-tuple-element.463.moments.refs_2_.refs_3_, f32[3,2048]{1,0:T(4,128)} %get-tuple-element.534.gains.extra, ...), custom_call_target="tpu_custom_call" | custom-call | flops 1 | bytes 1 | tf_op jit(solution)/shard_map/backward/pallas_call | solution.py:416
  312.1 17.8 %dproject.3 = (bf16[1024,2048]{1,0:T(8,128)(2,1)}, f32[1,2048]{1,0:T(1,128)}, f32[4,2048]{1,0:T(4,128)}, bf16[1024,2048]{1,0:T(8,128)(2,1)}) custom-call(s32[1]{0:T(128)} %constant.114.clone.1.order, f32[3,2048]{1,0:T(4,128)} %get-tuple-element.463.moments.refs_2_.refs_3_, f32[3,2048]{1,0:T(4,128)} %get-tuple-element.534.gains.extra, f32[4,2048]{1,0:T(4,128)} %copy-done.47, ...), custom_call_target="tpu_custom_call" | custom-call | flops 1 | bytes 1 | tf_op jit(solution)/shard_map/dproject/pallas_call | solution.py:526
  330.0 13.6 %weight.2 = bf16[2048,2048]{1,0:T(8,128)(2,1)} custom-call(f32[1,2048]{1,0:T(1,128)} %get-tuple-element.337.refs_0_.extra, bf16[1024,2048]{1,0:T(8,128)(2,1)} %get-tuple-element.339.refs_1_, f32[3,2048]{1,0:T(4,128)} %get-tuple-element.463.moments.refs_2_.refs_3_, bf16[1024,2048]{1,0:T(8,128)(2,1)} %bitcast.145), custom_call_target="tpu_custom_call" | custom-call | flops 1 | bytes 1 | tf_op jit(solution)/shard_map/weight/pallas_call | solution.py:586
  344.7 5.6 collective-permute-start.48
  352.8 14.6 %backward.3 = (f32[2,512,2048]{2,1,0:T(8,128)}, f32[4,2048]{1,0:T(4,128)}) custom-call(s32[1]{0:T(128)} %constant.114.clone.1.order, f32[2,512]{1,0:T(2,128)} %convert_element_type.92.keep, f32[3,2048]{1,0:T(4,128)} %get-tuple-element.459.moments.refs_4_.refs_1_, f32[3,2048]{1,0:T(4,128)} %get-tuple-element.535.gains, ...), custom_call_target="tpu_custom_call" | custom-call | flops 1 | bytes 1 | tf_op jit(solution)/shard_map/backward/pallas_call | solution.py:416
  385.2 9.2 %dproject.4 = (bf16[256,2048]{1,0:T(8,128)(2,1)}, f32[1,2048]{1,0:T(1,128)}, f32[4,2048]{1,0:T(4,128)}, bf16[256,512]{1,0:T(8,128)(2,1)}, bf16[256,512]{1,0:T(8,...) custom-call(s32[4]{0:T(128)} %pad_add_fusion.order, f32[3,2048]{1,0:T(4,128)} %get-tuple-element.459.moments.refs_4_.refs_1_, ...), custom_call_target="tpu_custom_call" | custom-call | flops 1 | bytes 1 | tf_op jit(solution)/shard_map/dproject/pallas_call | solution.py:526
  402.1 15.4 %dproject.5 = (bf16[768,2048]{1,0:T(8,128)(2,1)}, f32[1,2048]{1,0:T(1,128)}, f32[4,2048]{1,0:T(4,128)}, bf16[768,512]{1,0:T(8,128)(2,1)}, bf16[768,512]{1,0:T(8,...) custom-call(s32[4]{0:T(128)} %pad_add_fusion.order, f32[3,2048]{1,0:T(4,128)} %get-tuple-element.459.moments.refs_4_.refs_1_, ...), custom_call_target="tpu_custom_call" | custom-call | flops 1 | bytes 1 | tf_op jit(solution)/shard_map/dproject/pallas_call | solution.py:526
  417.6 13.8 %weight.3 = bf16[2048,2048]{1,0:T(8,128)(2,1)} custom-call(f32[1,2048]{1,0:T(1,128)} %get-tuple-element.449.refs_0_, f32[1,2048]{1,0:T(1,128)} %get-tuple-element.450.refs_1_, bf16[256,2048]{1,0:T(8,128)(2,1)} %get-tuple-element.381.refs_2_, bf16[768,2048]{1,0:T(8,128)(2,1)} %get-tuple-element.382.refs_3_, ...), custom_call_target="tpu_custom_call" | custom-call | flops 1 | bytes 1 | tf_op jit(solution)/shard_map/weight/pallas_call | solution.py:586
  449.1 18.6 %collective-permute-done.64 = bf16[768,512]{1,0:T(8,128)(2,1)S(1)} collective-permute-done((bf16[768,512]{1,0:T(8,128)(2,1)}, bf16[768,512]{1,0:T(8,128)(2,1)S(1)}, u32[]{:S(2)}, u32[]{:S(2)}) %collective-permute-start.64) | collective-permute-done | bytes 786464 | tf_op jit(solution)/shard_map/ppermute | solution.py:684
  483.8 12.9 %collective-permute-done.65 = bf16[768,512]{1,0:T(8,128)(2,1)} collective-permute-done((bf16[768,512]{1,0:T(8,128)(2,1)}, bf16[768,512]{1,0:T(8,128)(2,1)}, u32[]{:S(2)}, u32[]{:S(2)}) %collective-permute-start.65) | collective-permute-done | bytes 786464 | tf_op jit(solution)/shard_map/ppermute | solution.py:684
  508.5 19.2 %collective-permute-start.73 = (f32[1,2048]{1,0:T(1,128)S(1)}, f32[1,2048]{1,0:T(1,128)S(1)}, u32[]{:S(2)}, u32[]{:S(2)}) collective-permute-start(f32[1,2048]{1,0:T(1,128)S(1)} %add.430), channel_id=1, source_target_pairs={{0,2},{1,3},{2,0},{3,1},{4,6},{5,7},{6,4},{7,5},{8,10},{9,11},{10,... | collective-permute-start | bytes 24584 | tf_op jit(solution)/shard_map/ppermute | solution.py:816
  534.5 12.8 %collective-permute-done.74 = f32[1,2048]{1,0:T(1,128)S(1)} collective-permute-done((f32[1,2048]{1,0:T(1,128)S(1)}, f32[1,2048]{1,0:T(1,128)S(1)}, u32[]{:S(2)}, u32[]{:S(2)}) %collective-permute-start.74) | collective-permute-done | bytes 8224 | tf_op jit(solution)/shard_map/ppermute | solution.py:816
  (407 shorter events, 200.7 us)
Async XLA Ops:
  7.2 65.7 %all-gather.8.cloned.1.call-start = ((), (), s32[]{:S(2)}) async-start(), calls=%async_computation.6 | async-start | bytes 2621440 | tf_op jit(solution)/shard_map/all_gather | solution.py:74
  9.2 141.2 %all-gather.6.cloned.1.call-start = ((), (), s32[]{:S(2)}) async-start(), calls=%async_computation.3 | async-start | bytes 9437184 | tf_op jit(solution)/shard_map/all_gather | solution.py:703
  11.2 35.1 %collective-permute-start.2 = (bf16[256,512]{1,0:T(8,128)(2,1)S(1)}, bf16[256,512]{1,0:T(8,128)(2,1)S(1)}, u32[]{:S(2)}, u32[]{:S(2)}) collective-permute-start(bf16[256,512]{1,0:T(8,128)(2,1)S(1)} %get-tuple-element.486), channel_id=1, source_target_pairs={{0,3},{1,2},{2,1},{3,0},{4,7},{5,6},{6,5},{7,4},{8,11},{9,10},{10,... | collective-permute-start | bytes 786440 | tf_op jit(solution)/shard_map/ppermute | solution.py:684
  16.3 49.2 %collective-permute-start.1 = (bf16[256,512]{1,0:T(8,128)(2,1)S(1)}, bf16[256,512]{1,0:T(8,128)(2,1)S(1)}, u32[]{:S(2)}, u32[]{:S(2)}) collective-permute-start(bf16[256,512]{1,0:T(8,128)(2,1)S(1)} %get-tuple-element.487), channel_id=1, source_target_pairs={{0,2},{1,3},{2,0},{3,1},{4,6},{5,7},{6,4},{7,5},{8,10},{9,11},{10,... | collective-permute-start | bytes 786440 | tf_op jit(solution)/shard_map/ppermute | solution.py:684
  16.3 49.2 %collective-permute-start = (bf16[256,512]{1,0:T(8,128)(2,1)S(1)}, bf16[256,512]{1,0:T(8,128)(2,1)S(1)}, u32[]{:S(2)}, u32[]{:S(2)}) collective-permute-start(bf16[256,512]{1,0:T(8,128)(2,1)S(1)} %get-tuple-element.488), channel_id=1, source_target_pairs={{0,1},{1,0},{2,3},{3,2},{4,5},{5,4},{6,7},{7,6},{8,9},{9,8},{10,11... | collective-permute-start | bytes 786440 | tf_op jit(solution)/shard_map/ppermute | solution.py:684
  75.9 131.4 %all-gather.10.cloned.1.call-start = ((), (), s32[]{:S(2)}) async-start(), calls=%async_computation.7 | async-start | bytes 9437184 | tf_op jit(solution)/shard_map/all_gather | solution.py:708
  76.0 74.2 %collective-permute-start.3 = (bf16[768,512]{1,0:T(8,128)(2,1)}, bf16[768,512]{1,0:T(8,128)(2,1)S(1)}, u32[]{:S(2)}, u32[]{:S(2)}) collective-permute-start(bf16[768,512]{1,0:T(8,128)(2,1)} %get-tuple-element.249), channel_id=1, source_target_pairs={{0,1},{1,0},{2,3},{3,2},{4,5},{5,4},{6,7},{7,6},{8,9},{9,8},{10,11... | collective-permute-start | bytes 2359304 | tf_op jit(solution)/shard_map/ppermute | solution.py:684
  76.1 74.2 %collective-permute-start.4 = (bf16[768,512]{1,0:T(8,128)(2,1)}, bf16[768,512]{1,0:T(8,128)(2,1)S(1)}, u32[]{:S(2)}, u32[]{:S(2)}) collective-permute-start(bf16[768,512]{1,0:T(8,128)(2,1)} %get-tuple-element.250), channel_id=1, source_target_pairs={{0,2},{1,3},{2,0},{3,1},{4,6},{5,7},{6,4},{7,5},{8,10},{9,11},{10,... | collective-permute-start | bytes 2359304 | tf_op jit(solution)/shard_map/ppermute | solution.py:684
  79.0 71.2 %collective-permute-start.5 = (bf16[768,512]{1,0:T(8,128)(2,1)S(1)}, bf16[768,512]{1,0:T(8,128)(2,1)S(1)}, u32[]{:S(2)}, u32[]{:S(2)}) collective-permute-start(bf16[768,512]{1,0:T(8,128)(2,1)S(1)} %get-tuple-element.251), channel_id=1, source_target_pairs={{0,3},{1,2},{2,1},{3,0},{4,7},{5,6},{6,5},{7,4},{8,11},{9,10},{10,... | collective-permute-start | bytes 2359304 | tf_op jit(solution)/shard_map/ppermute | solution.py:684
  92.7 36.1 %collective-permute-start.10 = (f32[6,2048]{1,0:T(8,128)S(1)}, f32[6,2048]{1,0:T(8,128)S(1)}, u32[]{:S(2)}, u32[]{:S(2)}) collective-permute-start(f32[6,2048]{1,0:T(8,128)S(1)} %add.371), channel_id=1, source_target_pairs={{0,1},{1,0},{2,3},{3,2},{4,5},{5,4},{6,7},{7,6},{8,9},{9,8},{10,11... | collective-permute-start | bytes 147464 | tf_op jit(solution)/shard_map/ppermute | solution.py:701
  150.3 281.1 %reduce-scatter.3.cloned.1.call-start = ((), (), s32[]{:S(2)}) async-start(), calls=%async_computation.4 | async-start | bytes 9437184 | tf_op jit(solution)/shard_map/reduce_scatter | solution.py:752
  187.4 35.1 %collective-permute-start.22 = (bf16[4,512,128]{2,1,0:T(8,128)(2,1)}, bf16[4,512,128]{2,1,0:T(8,128)(2,1)S(1)}, u32[]{:S(2)}, u32[]{:S(2)}) collective-permute-start(bf16[4,512,128]{2,1,0:T(8,128)(2,1)} %get-tuple-element.293), channel_id=1, source_target_pairs={{0,1},{1,0},{2,3},{3,2},{4,5},{5,4},{6,7},{7,6},{8,9},{9,8},{10,11... | collective-permute-start | bytes 1572872 | tf_op jit(solution)/shard_map/ppermute | solution.py:684
  188.3 38.1 %collective-permute-start.23 = (bf16[4,512,128]{2,1,0:T(8,128)(2,1)S(1)}, bf16[4,512,128]{2,1,0:T(8,128)(2,1)S(1)}, u32[]{:S(2)}, u32[]{:S(2)}) collective-permute-start(bf16[4,512,128]{2,1,0:T(8,128)(2,1)S(1)} %copy-done.18), channel_id=1, source_target_pairs={{0,2},{1,3},{2,0},{3,1},{4,6},{5,7},{6,4},{7,5},{8,10},{9,11},{10,... | collective-permute-start | bytes 1572872 | tf_op jit(solution)/shard_map/ppermute | solution.py:684
  190.3 36.1 %collective-permute-start.24 = (bf16[4,512,128]{2,1,0:T(8,128)(2,1)S(1)}, bf16[4,512,128]{2,1,0:T(8,128)(2,1)S(1)}, u32[]{:S(2)}, u32[]{:S(2)}) collective-permute-start(bf16[4,512,128]{2,1,0:T(8,128)(2,1)S(1)} %copy-done.17), channel_id=1, source_target_pairs={{0,3},{1,2},{2,1},{3,0},{4,7},{5,6},{6,5},{7,4},{8,11},{9,10},{10,... | collective-permute-start | bytes 1572872 | tf_op jit(solution)/shard_map/ppermute | solution.py:684
  301.4 42.2 %collective-permute-start.45 = (bf16[4,512,128]{2,1,0:T(8,128)(2,1)}, bf16[4,512,128]{2,1,0:T(8,128)(2,1)S(1)}, u32[]{:S(2)}, u32[]{:S(2)}) collective-permute-start(bf16[4,512,128]{2,1,0:T(8,128)(2,1)} %get-tuple-element.347), channel_id=1, source_target_pairs={{0,1},{1,0},{2,3},{3,2},{4,5},{5,4},{6,7},{7,6},{8,9},{9,8},{10,11... | collective-permute-start | bytes 1572872 | tf_op jit(solution)/shard_map/ppermute | solution.py:684
  302.9 40.7 %collective-permute-start.46 = (bf16[4,512,128]{2,1,0:T(8,128)(2,1)S(1)}, bf16[4,512,128]{2,1,0:T(8,128)(2,1)S(1)}, u32[]{:S(2)}, u32[]{:S(2)}) collective-permute-start(bf16[4,512,128]{2,1,0:T(8,128)(2,1)S(1)} %copy-done.76), channel_id=1, source_target_pairs={{0,2},{1,3},{2,0},{3,1},{4,6},{5,7},{6,4},{7,5},{8,10},{9,11},{10,... | collective-permute-start | bytes 1572872 | tf_op jit(solution)/shard_map/ppermute | solution.py:684
  303.8 39.8 %collective-permute-start.47 = (bf16[4,512,128]{2,1,0:T(8,128)(2,1)S(1)}, bf16[4,512,128]{2,1,0:T(8,128)(2,1)S(1)}, u32[]{:S(2)}, u32[]{:S(2)}) collective-permute-start(bf16[4,512,128]{2,1,0:T(8,128)(2,1)S(1)} %copy-done.75), channel_id=1, source_target_pairs={{0,3},{1,2},{2,1},{3,0},{4,7},{5,6},{6,5},{7,4},{8,11},{9,10},{10,... | collective-permute-start | bytes 1572872 | tf_op jit(solution)/shard_map/ppermute | solution.py:684
  344.6 162.6 %reduce-scatter.5.cloned.1.call-start = ((), (), s32[]{:S(2)}) async-start(), calls=%async_computation.5 | async-start | bytes 9437184 | tf_op jit(solution)/shard_map/reduce_scatter | solution.py:777
  396.4 35.0 %collective-permute-start.61 = (bf16[256,512]{1,0:T(8,128)(2,1)}, bf16[256,512]{1,0:T(8,128)(2,1)S(1)}, u32[]{:S(2)}, u32[]{:S(2)}) collective-permute-start(bf16[256,512]{1,0:T(8,128)(2,1)} %get-tuple-element.372), channel_id=1, source_target_pairs={{0,1},{1,0},{2,3},{3,2},{4,5},{5,4},{6,7},{7,6},{8,9},{9,8},{10,11... | collective-permute-start | bytes 786440 | tf_op jit(solution)/shard_map/ppermute | solution.py:684
  399.7 31.6 %collective-permute-start.62 = (bf16[256,512]{1,0:T(8,128)(2,1)}, bf16[256,512]{1,0:T(8,128)(2,1)S(1)}, u32[]{:S(2)}, u32[]{:S(2)}) collective-permute-start(bf16[256,512]{1,0:T(8,128)(2,1)} %get-tuple-element.373), channel_id=1, source_target_pairs={{0,2},{1,3},{2,0},{3,1},{4,6},{5,7},{6,4},{7,5},{8,10},{9,11},{10,... | collective-permute-start | bytes 786440 | tf_op jit(solution)/shard_map/ppermute | solution.py:684
  432.3 35.4 %collective-permute-start.64 = (bf16[768,512]{1,0:T(8,128)(2,1)}, bf16[768,512]{1,0:T(8,128)(2,1)S(1)}, u32[]{:S(2)}, u32[]{:S(2)}) collective-permute-start(bf16[768,512]{1,0:T(8,128)(2,1)} %get-tuple-element.401), channel_id=1, source_target_pairs={{0,1},{1,0},{2,3},{3,2},{4,5},{5,4},{6,7},{7,6},{8,9},{9,8},{10,11... | collective-permute-start | bytes 2359304 | tf_op jit(solution)/shard_map/ppermute | solution.py:684
  433.5 63.2 %collective-permute-start.65 = (bf16[768,512]{1,0:T(8,128)(2,1)}, bf16[768,512]{1,0:T(8,128)(2,1)}, u32[]{:S(2)}, u32[]{:S(2)}) collective-permute-start(bf16[768,512]{1,0:T(8,128)(2,1)} %get-tuple-element.445), channel_id=1, source_target_pairs={{0,2},{1,3},{2,0},{3,1},{4,6},{5,7},{6,4},{7,5},{8,10},{9,11},{10,... | collective-permute-start | bytes 2359304 | tf_op jit(solution)/shard_map/ppermute | solution.py:684
  435.4 64.1 %collective-permute-start.66 = (bf16[768,512]{1,0:T(8,128)(2,1)}, bf16[768,512]{1,0:T(8,128)(2,1)}, u32[]{:S(2)}, u32[]{:S(2)}) collective-permute-start(bf16[768,512]{1,0:T(8,128)(2,1)} %get-tuple-element.446), channel_id=1, source_target_pairs={{0,3},{1,2},{2,1},{3,0},{4,7},{5,6},{6,5},{7,4},{8,11},{9,10},{10,... | collective-permute-start | bytes 2359304 | tf_op jit(solution)/shard_map/ppermute | solution.py:684
  437.8 96.5 %all-to-all-start = ((bf16[4,256,512]{2,1,0:T(8,128)(2,1)}), bf16[4,256,512]{2,1,0:T(8,128)(2,1)S(1)}, u32[]{:S(2)}, u32[]{:S(2)}) async-start(bf16[4,256,512]{2,1,0:T(8,128)(2,1)} %bitcast.135), calls=%async_computation.1 | async-start | bytes 2097152 | tf_op jit(solution)/shard_map/all_to_all | solution.py:804
  (140 other events, 1869.2 us)
Sparse Core Ops, SparseCore 0:
  10.2 62.6 all-gather.7
  76.0 55.3 all-gather.5
  150.4 55.8 all-gather.9
  343.8 74.0 reduce-scatter.2
  432.4 69.6 reduce-scatter.4

commit v5 on v4

--- a/solution.py
+++ b/solution.py
@@ -675,13 +675,28 @@
     sliced = cotangent.reshape(narrow, rows, ROW_LEN, tiles, LANES)
     held = [jnp.stack([sliced[:, r, :, j] for j, r in group], 1) for _, group in groups_in]
 
-    line = [n ^ k for k in range(narrow)]
+    apart = [list(range(1, narrow)), [*range(2, narrow), 1]]
+    in_step = [apart[0], apart[0]]
+
+    def line_of(turns):
+        return [n] + [n ^ jnp.where(w % 2 == 0, q, p) for p, q in zip(*turns, strict=True)]
+
+    def along_line(blocks, turns=apart):
+        came = blocks[:1]
+        for k in range(1, narrow):
+            pairs = [
+                (i * narrow + j, i * narrow + (j ^ turns[1 - i % 2][k - 1]))
+                for i in range(wide)
+                for j in range(narrow)
+            ]
+            came.append(lax.ppermute(blocks[k], ("wide", "narrow"), pairs))
+        return came
+
+    line = line_of(apart)
     order = jnp.stack([jnp.asarray(q, jnp.int32) for q in line])
+    last_line = line_of(in_step)
+    last_order = jnp.stack([jnp.asarray(q, jnp.int32) for q in last_line])
     alone = jnp.zeros((1,), jnp.int32)
-
-    def along_line(blocks):
-        pairs = [[(i, i ^ k) for i in range(narrow)] for k in range(narrow)]
-        return blocks[:1] + [lax.ppermute(blocks[k], "narrow", pairs[k]) for k in range(1, narrow)]
 
     split = frames // 4
     def frames_for(lo, hi):
@@ -761,13 +776,13 @@
     group = along_line(h_two[3])
     halves = across(sums, add, True)
     back = functools.partial(
-        dproject, dpre, z_one, moments_one, gains_one, halves, full_one, order, total_frames
+        dproject, dpre, z_one, moments_one, gains_one, halves, full_one, last_order, total_frames
     )
     split = frames // 4
     dz_early, level_early, sums_one, da_early = back(0, split)
     da_early, group = tie((da_early, group))
     second.append(group)
-    da_early = along_line(da_early)
+    da_early = along_line(da_early, in_step)
     dz_late, level_late, _, da_late = back(split, frames)
     terms_one = weight_terms(source, moments_one, [dz_early, dz_late], [level_early, level_late])
     levels = (level_early, level_late)
@@ -775,17 +790,22 @@
         (da_early, da_late, terms_one, plane_two, levels, second)
     )
     plane_one = lax.psum_scatter(terms_one, "wide", scatter_dimension=0, tiled=True)
-    da_late = along_line(da_late)
-    da_late[1], second, moments_one, moments_two, sums_one, sums_two = tie(
-        (da_late[1], second, moments_one, moments_two, sums_one, sums_two)
+    da_late = along_line(da_late, in_step)
+    da_late[1], second, moments_one, moments_two, sums_one, sums_two, plane_two = tie(
+        (da_late[1], second, moments_one, moments_two, sums_one, sums_two, plane_two)
     )
     parts = {}
     for (kind, group), came in zip(groups_out, second, strict=True):
         if kind == "line":
             stacked = jnp.stack(came)
+            places = []
+            for q in range(narrow):
+                turn = n ^ q
+                shifted = jnp.where(turn == 1, narrow - 1, jnp.maximum(turn - 1, 0))
+                places.append(jnp.where(w % 2 == 0, shifted, turn))
             came = [
                 jnp.stack(
-                    [lax.dynamic_index_in_dim(stacked, n ^ q, 0, keepdims=False) for q in range(narrow)]
+                    [lax.dynamic_index_in_dim(stacked, p, 0, keepdims=False) for p in places]
                 )
             ]
         for u, unit in enumerate(group):
@@ -808,9 +828,9 @@
     while k:
         level_one = level_one + lax.ppermute(level_one, "wide", [(i, i ^ k) for i in range(wide)])
         k //= 2
-    columns = [lax.dynamic_slice_in_dim(plane_one, q * part, part, 1) for q in line]
+    columns = [lax.dynamic_slice_in_dim(plane_one, q * part, part, 1) for q in last_line]
     columns, level_one = tie((columns, level_one))
-    came_one = along_line(columns)
+    came_one = along_line(columns, in_step)
     k = narrow // 2
     while k:
         level_one = level_one + lax.ppermute(
@@ -820,7 +840,7 @@
 
     grad_inputs = jnp.zeros(inputs.shape, jnp.float32)
     for lo, came in ((0, da_early), (split, da_late)):
-        for q, block in zip(line, came, strict=True):
+        for q, block in zip(last_line, came, strict=True):
             at = q * frames + lo
             own = lax.dynamic_slice_in_dim(cotangent, at, block.shape[0], 0).astype(jnp.float32)
             grad_inputs = lax.dynamic_update_slice_in_dim(

time: 570 us -> 564 us (0.989)
  waiting for transfers between devices: 169 us -> 163 us
    ppermute x36, waiting for transfers between devices: 60.7 us -> 37.1 us  [along_line(): came.append(lax.ppermute(blocks[k], ('wide', 'narrow'), pairs))]
    all_gather x1, waiting for transfers between devices: 7.42 us -> 25.3 us  [gather_rows(): return lax.all_gather(jnp.stack(shares), 'narrow', axis=1)]
    ppermute x36, starting transfers between devices: 59.2 us -> 51.9 us  [along_line(): came.append(lax.ppermute(blocks[k], ('wide', 'narrow'), pairs))]
  transfers between devices with their start and end apart: 81 -> 81, of which waited for: 32 -> 32; matrix products, arithmetic and copies ran while one was open for 11% -> 12% of each run, Pallas kernels for 29% -> 29%
where the time goes in v5:
time: 564 us; the launch traced here: 555 us
  waiting for transfers between devices  163 us (29%)
  Pallas kernels  163 us (29%)
  starting transfers between devices  132 us (23%)
  local copies, waits for them, and re-layouts  48.7 us (9%)
  other arithmetic  33 us (6%)
  between operations  15.5 us (3%)
    ppermute x2, waiting for transfers between devices, per_device(): lax.ppermute(gains, 'narrow', [(i, i ^ k) for i in range(narrow)])  53.5 us
    ppermute x36, starting transfers between devices, along_line(): came.append(lax.ppermute(blocks[k], ('wide', 'narrow'), pairs))  51.9 us
    ppermute x28, starting transfers between devices, merge_all(): lax.ppermute(value, axis, [(i, i ^ t) for i in range(size)])  48 us
    pallas_call x3, Pallas kernels, dproject(): pl.pallas_call(functools.partial(dproject_kernel, total_frames), grid=(st...  42.1 us
    ppermute x36, waiting for transfers between devices, along_line(): came.append(lax.ppermute(blocks[k], ('wide', 'narrow'), pairs))  37.1 us
    pallas_call x2, Pallas kernels, project(): pl.pallas_call(functools.partial(project_kernel, blocks, cuts), grid_spec...  32.7 us
    pallas_call x2, Pallas kernels, backward(): pl.pallas_call(functools.partial(backward_kernel, groups), grid=(length /...  29.8 us
    pallas_call x2, Pallas kernels, forward(): pl.pallas_call(functools.partial(forward_kernel, total_frames, groups), g...  29.3 us
  transfers between devices with their start and end apart: 81, of which 32 were waited for; matrix products, arithmetic and copies ran while one was open for 12% of the time, Pallas kernels for 29%

profile of v5, /device:TPU:0, one launch (start us, length us, event | category | flops | bytes accessed | tf_op | source)
XLA Modules:
  0.0 554.9 jit_solution(11467278731164141505)
XLA Ops:
  16.9 6.9 %reshape.78 = bf16[4,2,512,4,128]{4,3,2,1,0:T(4,128)(2,1)} reshape(bf16[4096,512]{1,0:T(8,128)(2,1)} %param.21) | data formatting | bytes 8388608 | tf_op jit(solution)/shard_map/reshape | solution.py:675
  25.4 13.4 %fusion.38 = (bf16[4,1,512,1,128]{4,3,2,1,0:T(2,128)(2,1)S(1)}, bf16[4,1,512,1,128]{4,3,2,1,0:T(2,128)(2,1)S(1)}, bf16[4,1,512,1,128]{4,3,2,1,0:T(2,128)(2,1)S(1...) fusion(bf16[4,2,512,4,128]{4,3,2,1,0:T(4,128)(2,1)} %reshape.78), kind=kLoop, calls=%fused_computation.175 | loop fusion | bytes 8388608 | tf_op jit(solution)/shard_map/slice | solution.py:676
  46.2 25.3 %all-gather.8.cloned.1.call-done = bf16[2,1024,512]{2,1,0:T(8,128)(2,1)} async-done(((bf16[2,256,512]{2,1,0:T(8,128)(2,1)}), bf16[2,1024,512]{2,1,0:T(8,128)(2,1)}) %all-gather.8.cloned.1.call-update) | async-done | bytes 2097168 | tf_op jit(solution)/shard_map/all_gather | solution.py:74
  91.7 35.6 %collective-permute-done.10 = f32[6,2048]{1,0:T(8,128)S(1)} collective-permute-done((f32[6,2048]{1,0:T(8,128)S(1)}, f32[6,2048]{1,0:T(8,128)S(1)}, u32[]{:S(2)}, u32[]{:S(2)}) %collective-permute-start.10) | collective-permute-done | bytes 49184 | tf_op jit(solution)/shard_map/ppermute | solution.py:716
  131.3 17.9 %collective-permute-done.11 = f32[6,2048]{1,0:T(8,128)S(1)} collective-permute-done((f32[6,2048]{1,0:T(8,128)S(1)}, f32[6,2048]{1,0:T(8,128)S(1)}, u32[]{:S(2)}, u32[]{:S(2)}) %collective-permute-start.11) | collective-permute-done | bytes 49184 | tf_op jit(solution)/shard_map/ppermute | solution.py:716
  152.9 17.6 %project.2 = (bf16[1024,2048]{1,0:T(8,128)(2,1)}, f32[3,2048]{1,0:T(4,128)}, bf16[1024,2048]{1,0:T(8,128)(2,1)}) custom-call(s32[4]{0:T(128)} %pad_add_fusion.1.order, bf16[256,512]{1,0:T(8,128)(2,1)} %get-tuple-element.245.refs_0_, bf16[256,512]{1,0:T(8,128)(2,1)} %copy-done.26, bf16[256,512]{1,0:T(8,128)(2,1)} %copy-done.27, bf16[256,512]{1,0:T(8,128)(2,1)} %copy-done.28, ...), custom_call_target="tpu_custom_call" | custom-call | flops 1 | bytes 1 | tf_op jit(solution)/shard_map/project/pallas_call | solution.py:143
  170.6 5.5 collective-permute-start.15
  194.8 13.5 %forward.2 = (bf16[2,8192,128]{2,1,0:T(8,128)(2,1)}, f32[3,2048]{1,0:T(4,128)}, bf16[2,512,2048]{2,1,0:T(8,128)(2,1)}) custom-call(s32[1]{0:T(128)} %constant.159.clone.1.order, f32[2,512]{1,0:T(2,128)} %convert_element_type.92.keep, f32[3,2048]{1,0:T(4,128)} %copy-done.46, f32[3,2048]{1,0:T(4,128)} %copy-done.63, f32[3,2048]{1,0:T(4,128)} %get-tuple-element.537.gains, ...), custom_call_target="tpu_custom_call" | custom-call | flops 1 | bytes 1 | tf_op jit(solution)/shard_map/forward/pallas_call | solution.py:265
  208.3 15.1 %project.3 = (bf16[1024,2048]{1,0:T(8,128)(2,1)}, f32[3,2048]{1,0:T(4,128)}) custom-call(s32[1]{0:T(128)} %constant.159.clone.1.order, bf16[1024,2048]{1,0:T(8,128)(2,1)} %bitcast.147, bf16[8,4,256,512]{3,2,1,0:T(8,128)(2,1)} %bitcast.143), custom_call_target="tpu_custom_call" | custom-call | flops 1 | bytes 1 | tf_op jit(solution)/shard_map/project/pallas_call | solution.py:143
  225.9 8.1 %collective-permute-start.25 = (f32[3,2048]{1,0:T(4,128)}, f32[3,2048]{1,0:T(4,128)S(1)}, u32[]{:S(2)}, u32[]{:S(2)}) collective-permute-start(f32[3,2048]{1,0:T(4,128)} %get-tuple-element.297), channel_id=1, source_target_pairs={{0,1},{1,0},{2,3},{3,2},{4,5},{5,4},{6,7},{7,6},{8,9},{9,8},{10,11... | collective-permute-start | bytes 73736 | tf_op jit(solution)/shard_map/ppermute | solution.py:42
  251.7 15.8 %forward.3 = (bf16[2,8192,128]{2,1,0:T(8,128)(2,1)}, f32[3,2048]{1,0:T(4,128)}, bf16[1,512,128]{2,1,0:T(8,128)(2,1)}, bf16[1,512,128]{2,1,0:T(8,128)(2,1)}, bf16...) custom-call(s32[4]{0:T(128)} %pad_add_fusion.1.order, ...), custom_call_target="tpu_custom_call" | custom-call | flops 1 | bytes 1 | tf_op jit(solution)/shard_map/forward/pallas_call | solution.py:265
  271.9 15.0 %backward.2 = (f32[2,512,2048]{2,1,0:T(8,128)}, f32[4,2048]{1,0:T(4,128)}) custom-call(s32[4]{0:T(128)} %pad_add_fusion.1.order, f32[2,512]{1,0:T(2,128)} %convert_element_type.92.keep, f32[3,2048]{1,0:T(4,128)} %get-tuple-element.465.moments.refs_2_.refs_3_, f32[3,2048]{1,0:T(4,128)} %get-tuple-element.536.gains.extra, ...), custom_call_target="tpu_custom_call" | custom-call | flops 1 | bytes 1 | tf_op jit(solution)/shard_map/backward/pallas_call | solution.py:416
  309.1 17.6 %dproject.3 = (bf16[1024,2048]{1,0:T(8,128)(2,1)}, f32[1,2048]{1,0:T(1,128)}, f32[4,2048]{1,0:T(4,128)}, bf16[1024,2048]{1,0:T(8,128)(2,1)}) custom-call(s32[1]{0:T(128)} %constant.159.clone.1.order, f32[3,2048]{1,0:T(4,128)} %get-tuple-element.465.moments.refs_2_.refs_3_, f32[3,2048]{1,0:T(4,128)} %get-tuple-element.536.gains.extra, f32[4,2048]{1,0:T(4,128)} %copy-done.44, ...), custom_call_target="tpu_custom_call" | custom-call | flops 1 | bytes 1 | tf_op jit(solution)/shard_map/dproject/pallas_call | solution.py:526
  326.7 13.6 %weight.2 = bf16[2048,2048]{1,0:T(8,128)(2,1)} custom-call(f32[1,2048]{1,0:T(1,128)} %get-tuple-element.338.refs_0_.extra, bf16[1024,2048]{1,0:T(8,128)(2,1)} %get-tuple-element.340.refs_1_, f32[3,2048]{1,0:T(4,128)} %get-tuple-element.465.moments.refs_2_.refs_3_, bf16[1024,2048]{1,0:T(8,128)(2,1)} %bitcast.148), custom_call_target="tpu_custom_call" | custom-call | flops 1 | bytes 1 | tf_op jit(solution)/shard_map/weight/pallas_call | solution.py:586
  341.4 4.5 collective-permute-start.48
  348.1 14.8 %backward.3 = (f32[2,512,2048]{2,1,0:T(8,128)}, f32[4,2048]{1,0:T(4,128)}) custom-call(s32[1]{0:T(128)} %constant.159.clone.1.order, f32[2,512]{1,0:T(2,128)} %convert_element_type.92.keep, f32[3,2048]{1,0:T(4,128)} %get-tuple-element.461.moments.refs_4_.refs_1_, f32[3,2048]{1,0:T(4,128)} %get-tuple-element.537.gains, ...), custom_call_target="tpu_custom_call" | custom-call | flops 1 | bytes 1 | tf_op jit(solution)/shard_map/backward/pallas_call | solution.py:416
  381.4 9.3 %dproject.4 = (bf16[256,2048]{1,0:T(8,128)(2,1)}, f32[1,2048]{1,0:T(1,128)}, f32[4,2048]{1,0:T(4,128)}, bf16[256,512]{1,0:T(8,128)(2,1)}, bf16[256,512]{1,0:T(8,...) custom-call(s32[4]{0:T(128)} %pad_add_fusion.order, f32[3,2048]{1,0:T(4,128)} %get-tuple-element.461.moments.refs_4_.refs_1_, ...), custom_call_target="tpu_custom_call" | custom-call | flops 1 | bytes 1 | tf_op jit(solution)/shard_map/dproject/pallas_call | solution.py:526
  398.8 15.2 %dproject.5 = (bf16[768,2048]{1,0:T(8,128)(2,1)}, f32[1,2048]{1,0:T(1,128)}, f32[4,2048]{1,0:T(4,128)}, bf16[768,512]{1,0:T(8,128)(2,1)}, bf16[768,512]{1,0:T(8,...) custom-call(s32[4]{0:T(128)} %pad_add_fusion.order, f32[3,2048]{1,0:T(4,128)} %get-tuple-element.461.moments.refs_4_.refs_1_, ...), custom_call_target="tpu_custom_call" | custom-call | flops 1 | bytes 1 | tf_op jit(solution)/shard_map/dproject/pallas_call | solution.py:526
  414.0 14.0 %weight.3 = bf16[2048,2048]{1,0:T(8,128)(2,1)} custom-call(f32[1,2048]{1,0:T(1,128)} %get-tuple-element.451.refs_0_, f32[1,2048]{1,0:T(1,128)} %get-tuple-element.452.refs_1_, bf16[256,2048]{1,0:T(8,128)(2,1)} %get-tuple-element.382.refs_2_, bf16[768,2048]{1,0:T(8,128)(2,1)} %get-tuple-element.383.refs_3_, ...), custom_call_target="tpu_custom_call" | custom-call | flops 1 | bytes 1 | tf_op jit(solution)/shard_map/weight/pallas_call | solution.py:586
  440.8 20.5 %collective-permute-done.64 = bf16[768,512]{1,0:T(8,128)(2,1)S(1)} collective-permute-done((bf16[768,512]{1,0:T(8,128)(2,1)}, bf16[768,512]{1,0:T(8,128)(2,1)S(1)}, u32[]{:S(2)}, u32[]{:S(2)}) %collective-permute-start.64) | collective-permute-done | bytes 786464 | tf_op jit(solution)/shard_map/ppermute | solution.py:692
  474.6 8.4 %fusion = bf16[4096,512]{1,0:T(8,128)(2,1)} fusion(f32[4,2,512,512]{3,2,1,0:T(8,128)} %copy.51, bf16[4096,512]{1,0:T(8,128)(2,1)} %param.11), kind=kLoop, calls=%fused_computation.1 | loop fusion | flops 6291456 | bytes 16777216 | tf_op jit(solution)/shard_map/convert_element_type | solution.py:817
  485.3 8.2 %collective-permute-done.65 = bf16[768,512]{1,0:T(8,128)(2,1)S(1)} collective-permute-done((bf16[768,512]{1,0:T(8,128)(2,1)}, bf16[768,512]{1,0:T(8,128)(2,1)S(1)}, u32[]{:S(2)}, u32[]{:S(2)}) %collective-permute-start.65) | collective-permute-done | bytes 786464 | tf_op jit(solution)/shard_map/ppermute | solution.py:692
  502.5 20.1 %collective-permute-start.73 = (f32[1,2048]{1,0:T(1,128)S(1)}, f32[1,2048]{1,0:T(1,128)S(1)}, u32[]{:S(2)}, u32[]{:S(2)}) collective-permute-start(f32[1,2048]{1,0:T(1,128)S(1)} %add.505), channel_id=1, source_target_pairs={{0,2},{1,3},{2,0},{3,1},{4,6},{5,7},{6,4},{7,5},{8,10},{9,11},{10,... | collective-permute-start | bytes 24584 | tf_op jit(solution)/shard_map/ppermute | solution.py:836
  529.4 12.8 %collective-permute-done.74 = f32[1,2048]{1,0:T(1,128)S(1)} collective-permute-done((f32[1,2048]{1,0:T(1,128)S(1)}, f32[1,2048]{1,0:T(1,128)S(1)}, u32[]{:S(2)}, u32[]{:S(2)}) %collective-permute-start.74) | collective-permute-done | bytes 8224 | tf_op jit(solution)/shard_map/ppermute | solution.py:836
  (398 shorter events, 190.8 us)
Async XLA Ops:
  7.2 64.3 %all-gather.8.cloned.1.call-start = ((), (), s32[]{:S(2)}) async-start(), calls=%async_computation.6 | async-start | bytes 2621440 | tf_op jit(solution)/shard_map/all_gather | solution.py:74
  9.2 36.9 %collective-permute-start = (bf16[256,512]{1,0:T(8,128)(2,1)S(1)}, bf16[256,512]{1,0:T(8,128)(2,1)S(1)}, u32[]{:S(2)}, u32[]{:S(2)}) collective-permute-start(bf16[256,512]{1,0:T(8,128)(2,1)S(1)} %get-tuple-element.490), channel_id=1, source_target_pairs={{0,2},{1,3},{2,0},{3,1},{4,5},{5,4},{6,7},{7,6},{8,10},{9,11},{10,... | collective-permute-start | bytes 786440 | tf_op jit(solution)/shard_map/ppermute | solution.py:692
  13.3 32.9 %collective-permute-start.1 = (bf16[256,512]{1,0:T(8,128)(2,1)S(1)}, bf16[256,512]{1,0:T(8,128)(2,1)S(1)}, u32[]{:S(2)}, u32[]{:S(2)}) collective-permute-start(bf16[256,512]{1,0:T(8,128)(2,1)S(1)} %get-tuple-element.489), channel_id=1, source_target_pairs={{0,3},{1,2},{2,1},{3,0},{4,6},{5,7},{6,4},{7,5},{8,11},{9,10},{10,... | collective-permute-start | bytes 786440 | tf_op jit(solution)/shard_map/ppermute | solution.py:692
  14.6 31.5 %collective-permute-start.2 = (bf16[256,512]{1,0:T(8,128)(2,1)S(1)}, bf16[256,512]{1,0:T(8,128)(2,1)S(1)}, u32[]{:S(2)}, u32[]{:S(2)}) collective-permute-start(bf16[256,512]{1,0:T(8,128)(2,1)S(1)} %get-tuple-element.488), channel_id=1, source_target_pairs={{0,1},{1,0},{2,3},{3,2},{4,7},{5,6},{6,5},{7,4},{8,9},{9,8},{10,11... | collective-permute-start | bytes 786440 | tf_op jit(solution)/shard_map/ppermute | solution.py:692
  16.8 132.6 %all-gather.6.cloned.1.call-start = ((), (), s32[]{:S(2)}) async-start(), calls=%async_computation.3 | async-start | bytes 9437184 | tf_op jit(solution)/shard_map/all_gather | solution.py:718
  74.5 133.8 %all-gather.10.cloned.1.call-start = ((), (), s32[]{:S(2)}) async-start(), calls=%async_computation.7 | async-start | bytes 9437184 | tf_op jit(solution)/shard_map/all_gather | solution.py:723
  74.5 74.6 %collective-permute-start.3 = (bf16[768,512]{1,0:T(8,128)(2,1)}, bf16[768,512]{1,0:T(8,128)(2,1)S(1)}, u32[]{:S(2)}, u32[]{:S(2)}) collective-permute-start(bf16[768,512]{1,0:T(8,128)(2,1)} %get-tuple-element.250), channel_id=1, source_target_pairs={{0,2},{1,3},{2,0},{3,1},{4,5},{5,4},{6,7},{7,6},{8,10},{9,11},{10,... | collective-permute-start | bytes 2359304 | tf_op jit(solution)/shard_map/ppermute | solution.py:692
  74.6 74.6 %collective-permute-start.4 = (bf16[768,512]{1,0:T(8,128)(2,1)}, bf16[768,512]{1,0:T(8,128)(2,1)S(1)}, u32[]{:S(2)}, u32[]{:S(2)}) collective-permute-start(bf16[768,512]{1,0:T(8,128)(2,1)} %get-tuple-element.251), channel_id=1, source_target_pairs={{0,3},{1,2},{2,1},{3,0},{4,6},{5,7},{6,4},{7,5},{8,11},{9,10},{10,... | collective-permute-start | bytes 2359304 | tf_op jit(solution)/shard_map/ppermute | solution.py:692
  77.6 71.6 %collective-permute-start.5 = (bf16[768,512]{1,0:T(8,128)(2,1)S(1)}, bf16[768,512]{1,0:T(8,128)(2,1)S(1)}, u32[]{:S(2)}, u32[]{:S(2)}) collective-permute-start(bf16[768,512]{1,0:T(8,128)(2,1)S(1)} %get-tuple-element.252), channel_id=1, source_target_pairs={{0,1},{1,0},{2,3},{3,2},{4,7},{5,6},{6,5},{7,4},{8,9},{9,8},{10,11... | collective-permute-start | bytes 2359304 | tf_op jit(solution)/shard_map/ppermute | solution.py:692
  90.1 37.2 %collective-permute-start.10 = (f32[6,2048]{1,0:T(8,128)S(1)}, f32[6,2048]{1,0:T(8,128)S(1)}, u32[]{:S(2)}, u32[]{:S(2)}) collective-permute-start(f32[6,2048]{1,0:T(8,128)S(1)} %add.433), channel_id=1, source_target_pairs={{0,1},{1,0},{2,3},{3,2},{4,5},{5,4},{6,7},{7,6},{8,9},{9,8},{10,11... | collective-permute-start | bytes 147464 | tf_op jit(solution)/shard_map/ppermute | solution.py:716
  149.3 278.8 %reduce-scatter.3.cloned.1.call-start = ((), (), s32[]{:S(2)}) async-start(), calls=%async_computation.4 | async-start | bytes 9437184 | tf_op jit(solution)/shard_map/reduce_scatter | solution.py:767
  187.6 38.3 %collective-permute-start.22 = (bf16[4,512,128]{2,1,0:T(8,128)(2,1)}, bf16[4,512,128]{2,1,0:T(8,128)(2,1)S(1)}, u32[]{:S(2)}, u32[]{:S(2)}) collective-permute-start(bf16[4,512,128]{2,1,0:T(8,128)(2,1)} %get-tuple-element.294), channel_id=1, source_target_pairs={{0,2},{1,3},{2,0},{3,1},{4,5},{5,4},{6,7},{7,6},{8,10},{9,11},{10,... | collective-permute-start | bytes 1572872 | tf_op jit(solution)/shard_map/ppermute | solution.py:692
  188.3 37.6 %collective-permute-start.23 = (bf16[4,512,128]{2,1,0:T(8,128)(2,1)S(1)}, bf16[4,512,128]{2,1,0:T(8,128)(2,1)S(1)}, u32[]{:S(2)}, u32[]{:S(2)}) collective-permute-start(bf16[4,512,128]{2,1,0:T(8,128)(2,1)S(1)} %copy-done.15), channel_id=1, source_target_pairs={{0,3},{1,2},{2,1},{3,0},{4,6},{5,7},{6,4},{7,5},{8,11},{9,10},{10,... | collective-permute-start | bytes 1572872 | tf_op jit(solution)/shard_map/ppermute | solution.py:692
  190.1 35.8 %collective-permute-start.24 = (bf16[4,512,128]{2,1,0:T(8,128)(2,1)S(1)}, bf16[4,512,128]{2,1,0:T(8,128)(2,1)S(1)}, u32[]{:S(2)}, u32[]{:S(2)}) collective-permute-start(bf16[4,512,128]{2,1,0:T(8,128)(2,1)S(1)} %copy-done.14), channel_id=1, source_target_pairs={{0,1},{1,0},{2,3},{3,2},{4,7},{5,6},{6,5},{7,4},{8,9},{9,8},{10,11... | collective-permute-start | bytes 1572872 | tf_op jit(solution)/shard_map/ppermute | solution.py:692
  297.4 43.0 %collective-permute-start.45 = (bf16[4,512,128]{2,1,0:T(8,128)(2,1)}, bf16[4,512,128]{2,1,0:T(8,128)(2,1)S(1)}, u32[]{:S(2)}, u32[]{:S(2)}) collective-permute-start(bf16[4,512,128]{2,1,0:T(8,128)(2,1)} %get-tuple-element.348), channel_id=1, source_target_pairs={{0,2},{1,3},{2,0},{3,1},{4,5},{5,4},{6,7},{7,6},{8,10},{9,11},{10,... | collective-permute-start | bytes 1572872 | tf_op jit(solution)/shard_map/ppermute | solution.py:692
  297.5 42.8 %collective-permute-start.46 = (bf16[4,512,128]{2,1,0:T(8,128)(2,1)S(1)}, bf16[4,512,128]{2,1,0:T(8,128)(2,1)S(1)}, u32[]{:S(2)}, u32[]{:S(2)}) collective-permute-start(bf16[4,512,128]{2,1,0:T(8,128)(2,1)S(1)} %copy-done.71), channel_id=1, source_target_pairs={{0,3},{1,2},{2,1},{3,0},{4,6},{5,7},{6,4},{7,5},{8,11},{9,10},{10,... | collective-permute-start | bytes 1572872 | tf_op jit(solution)/shard_map/ppermute | solution.py:692
  299.9 40.5 %collective-permute-start.47 = (bf16[4,512,128]{2,1,0:T(8,128)(2,1)S(1)}, bf16[4,512,128]{2,1,0:T(8,128)(2,1)S(1)}, u32[]{:S(2)}, u32[]{:S(2)}) collective-permute-start(bf16[4,512,128]{2,1,0:T(8,128)(2,1)S(1)} %copy-done.70), channel_id=1, source_target_pairs={{0,1},{1,0},{2,3},{3,2},{4,7},{5,6},{6,5},{7,4},{8,9},{9,8},{10,11... | collective-permute-start | bytes 1572872 | tf_op jit(solution)/shard_map/ppermute | solution.py:692
  341.2 160.1 %reduce-scatter.5.cloned.1.call-start = ((), (), s32[]{:S(2)}) async-start(), calls=%async_computation.5 | async-start | bytes 9437184 | tf_op jit(solution)/shard_map/reduce_scatter | solution.py:792
  392.5 35.5 %collective-permute-start.61 = (bf16[256,512]{1,0:T(8,128)(2,1)}, bf16[256,512]{1,0:T(8,128)(2,1)S(1)}, u32[]{:S(2)}, u32[]{:S(2)}) collective-permute-start(bf16[256,512]{1,0:T(8,128)(2,1)} %get-tuple-element.373), channel_id=1, source_target_pairs={{0,1},{1,0},{2,3},{3,2},{4,5},{5,4},{6,7},{7,6},{8,9},{9,8},{10,11... | collective-permute-start | bytes 786440 | tf_op jit(solution)/shard_map/ppermute | solution.py:692
  396.3 31.7 %collective-permute-start.62 = (bf16[256,512]{1,0:T(8,128)(2,1)}, bf16[256,512]{1,0:T(8,128)(2,1)S(1)}, u32[]{:S(2)}, u32[]{:S(2)}) collective-permute-start(bf16[256,512]{1,0:T(8,128)(2,1)} %get-tuple-element.374), channel_id=1, source_target_pairs={{0,2},{1,3},{2,0},{3,1},{4,6},{5,7},{6,4},{7,5},{8,10},{9,11},{10,... | collective-permute-start | bytes 786440 | tf_op jit(solution)/shard_map/ppermute | solution.py:692
  428.9 32.4 %collective-permute-start.64 = (bf16[768,512]{1,0:T(8,128)(2,1)}, bf16[768,512]{1,0:T(8,128)(2,1)S(1)}, u32[]{:S(2)}, u32[]{:S(2)}) collective-permute-start(bf16[768,512]{1,0:T(8,128)(2,1)} %get-tuple-element.402), channel_id=1, source_target_pairs={{0,1},{1,0},{2,3},{3,2},{4,5},{5,4},{6,7},{7,6},{8,9},{9,8},{10,11... | collective-permute-start | bytes 2359304 | tf_op jit(solution)/shard_map/ppermute | solution.py:692
  430.2 63.2 %collective-permute-start.65 = (bf16[768,512]{1,0:T(8,128)(2,1)}, bf16[768,512]{1,0:T(8,128)(2,1)S(1)}, u32[]{:S(2)}, u32[]{:S(2)}) collective-permute-start(bf16[768,512]{1,0:T(8,128)(2,1)} %get-tuple-element.447), channel_id=1, source_target_pairs={{0,2},{1,3},{2,0},{3,1},{4,6},{5,7},{6,4},{7,5},{8,10},{9,11},{10,... | collective-permute-start | bytes 2359304 | tf_op jit(solution)/shard_map/ppermute | solution.py:692
  431.9 62.9 %collective-permute-start.66 = (bf16[768,512]{1,0:T(8,128)(2,1)}, bf16[768,512]{1,0:T(8,128)(2,1)S(1)}, u32[]{:S(2)}, u32[]{:S(2)}) collective-permute-start(bf16[768,512]{1,0:T(8,128)(2,1)} %get-tuple-element.448), channel_id=1, source_target_pairs={{0,3},{1,2},{2,1},{3,0},{4,7},{5,6},{6,5},{7,4},{8,11},{9,10},{10,... | collective-permute-start | bytes 2359304 | tf_op jit(solution)/shard_map/ppermute | solution.py:692
  470.4 58.9 %all-to-all-start = ((bf16[4,256,512]{2,1,0:T(8,128)(2,1)}), bf16[4,256,512]{2,1,0:T(8,128)(2,1)S(1)}, u32[]{:S(2)}, u32[]{:S(2)}) async-start(bf16[4,256,512]{2,1,0:T(8,128)(2,1)} %bitcast.138), calls=%async_computation.1 | async-start | bytes 2097152 | tf_op jit(solution)/shard_map/all_to_all | solution.py:824
  (135 other events, 1892.9 us)
Sparse Core Ops, SparseCore 0:
  16.9 54.5 all-gather.7
  74.6 56.0 all-gather.5
  149.4 55.4 all-gather.9
  340.6 73.7 reduce-scatter.2
  428.2 70.4 reduce-scatter.4
